TPU v7x, 32 devices: a whole 2x2x4 slice. The times are simulated.
32 devices in a mesh: seq: 8 (over z, core), img: 4 (over y, x).
Axes of the slice: x: 2, y: 2, z: 4, core: 2. Of those that a mesh axis runs over, the one named last changes fastest.
Arguments:
- images: bfloat16 [4, 2048, 1024], P('img', 'seq'), may hold values from -6 to 6
- cotangent: bfloat16 [4, 2048, 1024], P('img', 'seq'), may hold values from -6 to 6
- qkv_weight: float32 [1024, 3072], P(('seq', 'img')), may hold values from -0.1875 to 0.1875
- out_weight: float32 [1024, 1024], P(('seq', 'img')), may hold values from -1 to 1
- up_weight: float32 [1024, 4096], P(('seq', 'img')), may hold values from -0.1875 to 0.1875
- down_weight: float32 [4096, 1024], P(('seq', 'img')), may hold values from -0.09375 to 0.09375
- norm_params: float32 [4, 1024], P(None, ('seq', 'img')), may hold values from -1 to 5, as said below
- qkv_first: float32 [1024, 3072], P(('seq', 'img')), may hold values from -5.6372688e-05 to 5.6372688e-05
- out_first: float32 [1024, 1024], P(('seq', 'img')), may hold values from -5.6372688e-05 to 5.6372688e-05
- up_first: float32 [1024, 4096], P(('seq', 'img')), may hold values from -5.6372688e-05 to 5.6372688e-05
- down_first: float32 [4096, 1024], P(('seq', 'img')), may hold values from -5.6372688e-05 to 5.6372688e-05
- norm_first: float32 [4, 1024], P(None, ('seq', 'img')), may hold values from -0.00022549075 to 0.00022549075
- qkv_second: float32 [1024, 3072], P(('seq', 'img')), may hold values from 7.9447e-11 to 3.17788e-10, as said below
- out_second: float32 [1024, 1024], P(('seq', 'img')), may hold values from 7.9447e-11 to 3.17788e-10, as said below
- up_second: float32 [1024, 4096], P(('seq', 'img')), may hold values from 7.9447e-11 to 3.17788e-10, as said below
- down_second: float32 [4096, 1024], P(('seq', 'img')), may hold values from 7.9447e-11 to 3.17788e-10, as said below
- norm_second: float32 [4, 1024], P(None, ('seq', 'img')), may hold values from 1.271152e-09 to 5.084608e-09, as said below
Outputs:
- activations: bfloat16 [4, 2048, 1024], P('img', 'seq')
- input_grad: bfloat16 [4, 2048, 1024], P('img', 'seq')
- grad_norm: float32 [], replicated
- qkv_new: float32 [1024, 3072], P(('seq', 'img'))
- out_new: float32 [1024, 1024], P(('seq', 'img'))
- up_new: float32 [1024, 4096], P(('seq', 'img'))
- down_new: float32 [4096, 1024], P(('seq', 'img'))
- norm_new: float32 [4, 1024], P(None, ('seq', 'img'))
- qkv_first_new: float32 [1024, 3072], P(('seq', 'img'))
- out_first_new: float32 [1024, 1024], P(('seq', 'img'))
- up_first_new: float32 [1024, 4096], P(('seq', 'img'))
- down_first_new: float32 [4096, 1024], P(('seq', 'img'))
- norm_first_new: float32 [4, 1024], P(None, ('seq', 'img'))
- qkv_second_new: float32 [1024, 3072], P(('seq', 'img'))
- out_second_new: float32 [1024, 1024], P(('seq', 'img'))
- up_second_new: float32 [1024, 4096], P(('seq', 'img'))
- down_second_new: float32 [4096, 1024], P(('seq', 'img'))
- norm_second_new: float32 [4, 1024], P(None, ('seq', 'img'))
Inputs may be any that keep to these rules, and one draw needn't show every extreme that they name: `norm_params`: rows 0 and 2 hold positive gains, rows 1 and 3 biases. `qkv_second`: positive. `out_second`: positive. `up_second`: positive. `down_second`: positive. `norm_second`: positive.
All inputs are finite; a program needn't handle non-finite values.
Results may differ from a plain program's by a relative error of at most 0.009.
Values may be sent and summed in bfloat16 or wider, within the bound.
No kernel may reach another device: no remote copies, remote signals or barrier semaphores. Data moves between devices by JAX's collectives and lax.ppermute only.
A program may use at most 256 MiB of HBM per device.

v0:
```python
import jax
import jax.numpy as jnp
from jax import lax
from jax.sharding import PartitionSpec as P

D = 1024
HEADS = 16
HEAD_DIM = 64
FF = 4096
STEP = 10


HIGH = lax.Precision.HIGHEST
NORM_EPS = 1e-05
BETA_ONE = 0.9
BETA_TWO = 0.999
ADAM_EPS = 1e-08
WEIGHT_DECAY = 0.1
CLIP_LIMIT = 1.0


def carried_in(value, axis, combine, identity):
    devices, index = (lax.axis_size(axis), lax.axis_index(axis))
    everything = jax.tree.map(
        lambda part, kind: lax.all_gather(part.astype(kind), axis),
        value,
        (jnp.bfloat16, jnp.bfloat16),
    )
    start = jax.tree.map(
        lambda part, zero: jnp.broadcast_to(jnp.asarray(zero, part.dtype), part.shape),
        value,
        identity,
    )

    def hop(k, before):
        reached = k < index
        new = combine(
            before, jax.tree.map(lambda part, own: part[k].astype(own.dtype), everything, value)
        )
        return jax.tree.map(lambda a, b: jnp.where(reached, a, b), new, before)

    return lax.fori_loop(0, devices, hop, start)


def entering(value, axis, join, neutral):
    count = lax.axis_size(axis)
    place = lax.axis_index(axis)
    ahead = count - 1 - place
    gathered = jax.tree.map(
        lambda a, kind: lax.all_gather(a.astype(kind), axis),
        value,
        jax.tree.map(lambda a: jnp.bfloat16 if a.dtype == jnp.float32 else a.dtype, value),
    )
    state = jax.tree.map(lambda a, e: jnp.zeros_like(a) + jnp.asarray(e, a.dtype), value, neutral)

    def one(hop, state):
        source = count - 1 - hop
        return join(
            state,
            jax.tree.map(
                lambda a, own: lax.dynamic_index_in_dim(a, source, 0, False).astype(own.dtype),
                gathered,
                value,
            ),
        )

    return lax.fori_loop(0, ahead, one, state)


def layer_norm(values, gain, bias):
    center = values - jnp.mean(values, axis=-1, keepdims=True)
    spread = jnp.mean(center * center, axis=-1, keepdims=True)
    return center * lax.rsqrt(spread + NORM_EPS) * gain + bias


def feature_map(values):
    return jax.nn.elu(values) + 1.0


def gelu_tanh(values):
    return jax.nn.gelu(values, approximate=True)


def round_low(values):
    return lax.optimization_barrier(values.astype(jnp.bfloat16)).astype(jnp.float32)


def attend(query_feat, key_feat, value_rows, state_in, keysum_in):
    scores = jnp.einsum("ithe,ishe->ihts", query_feat, key_feat, precision=HIGH)
    length = query_feat.shape[1]
    causal = jnp.tril(jnp.ones((length, length), jnp.float32))
    scores = scores * causal
    numer = jnp.einsum("ihts,ishf->ithf", scores, value_rows, precision=HIGH)
    numer = numer + jnp.einsum("ithe,ihef->ithf", query_feat, state_in, precision=HIGH)
    denom = jnp.transpose(jnp.sum(scores, axis=-1), (0, 2, 1))
    denom = denom + jnp.einsum("ithe,ihe->ith", query_feat, keysum_in, precision=HIGH)
    return numer / denom[..., None]


def group_state(key_feat, value_rows):
    state = jnp.einsum("ishe,ishf->ihef", key_feat, value_rows, precision=HIGH)
    return (state, jnp.sum(key_feat, axis=1))


def contract_rows(left, right):
    return lax.dot_general(
        left, right, (((0,), (0,)), ((), ())), preferred_element_type=jnp.float32
    )


def times_transpose(left, right):
    return lax.dot_general(
        left, right, (((1,), (1,)), ((), ())), preferred_element_type=jnp.float32
    )


def add_pair(earlier, later):
    return (earlier[0] + later[0], earlier[1] + later[1])


def adam_update(weight, first, second, grad, rate, decay):
    first_new = BETA_ONE * first + (1.0 - BETA_ONE) * grad
    second_new = BETA_TWO * second + (1.0 - BETA_TWO) * grad * grad
    first_hat = first_new / (1.0 - BETA_ONE**STEP)
    second_hat = second_new / (1.0 - BETA_TWO**STEP)
    weight_new = weight - rate * (first_hat / (jnp.sqrt(second_hat) + ADAM_EPS) + decay * weight)
    return (weight_new, first_new, second_new)


def body(
    images,
    cotangent,
    qkv_weight,
    out_weight,
    up_weight,
    down_weight,
    norm_params,
    qkv_first,
    out_first,
    up_first,
    down_first,
    norm_first,
    qkv_second,
    out_second,
    up_second,
    down_second,
    norm_second,
):
    qkv_low, out_low, up_low, down_low, norm_low = (
        lax.all_gather(qkv_weight.astype(jnp.bfloat16), ("seq", "img"), axis=0, tiled=True),
        lax.all_gather(out_weight.astype(jnp.bfloat16), ("seq", "img"), axis=0, tiled=True),
        lax.all_gather(up_weight.astype(jnp.bfloat16), ("seq", "img"), axis=0, tiled=True),
        lax.all_gather(down_weight.astype(jnp.bfloat16), ("seq", "img"), axis=0, tiled=True),
        lax.all_gather(norm_params.astype(jnp.bfloat16), ("seq", "img"), axis=1, tiled=True),
    )
    norm_vals = norm_low.astype(jnp.float32)
    count, group, width = images.shape
    rows = count * group
    inputs = images.reshape(rows, width).astype(jnp.float32)
    normed_one, norm_one_back = jax.vjp(layer_norm, inputs, norm_vals[0], norm_vals[1])
    normed_one_low = normed_one.astype(jnp.bfloat16)
    projected = jnp.dot(normed_one_low, qkv_low, preferred_element_type=jnp.float32)

    def split_features(values):
        shaped = values.reshape(count, group, 3, HEADS, HEAD_DIM)
        return (feature_map(shaped[:, :, 0]), feature_map(shaped[:, :, 1]), shaped[:, :, 2])

    feats, feat_back = jax.vjp(split_features, projected)
    query_feat = round_low(feats[0])
    key_feat = round_low(feats[1])
    value_rows = round_low(feats[2])
    state_loc, keysum_loc = group_state(key_feat, value_rows)
    state_flat = state_loc.reshape(count, HEADS, HEAD_DIM * HEAD_DIM)
    keysum_flat = keysum_loc.reshape(count, HEADS * HEAD_DIM)
    empty_pair = (jnp.zeros_like(state_flat), jnp.zeros_like(keysum_flat))
    prior_state, prior_sum = carried_in((state_flat, keysum_flat), "seq", add_pair, empty_pair)
    mixed, attend_back = jax.vjp(
        attend,
        query_feat,
        key_feat,
        value_rows,
        prior_state.reshape(count, HEADS, HEAD_DIM, HEAD_DIM),
        prior_sum.reshape(count, HEADS, HEAD_DIM),
    )
    mixed_low = mixed.reshape(rows, width).astype(jnp.bfloat16)
    resid = inputs + jnp.dot(mixed_low, out_low, preferred_element_type=jnp.float32)
    normed_two, norm_two_back = jax.vjp(layer_norm, resid, norm_vals[2], norm_vals[3])
    normed_two_low = normed_two.astype(jnp.bfloat16)
    hidden = jnp.dot(normed_two_low, up_low, preferred_element_type=jnp.float32)
    activated, gelu_back = jax.vjp(gelu_tanh, hidden)
    activated_low = activated.astype(jnp.bfloat16)
    output = resid + jnp.dot(activated_low, down_low, preferred_element_type=jnp.float32)
    activations = output.astype(jnp.bfloat16).reshape(count, group, width)
    grad_out = cotangent.reshape(rows, width)
    down_grad = contract_rows(activated_low, grad_out)
    grad_activated = times_transpose(grad_out, down_low)
    grad_hidden = gelu_back(grad_activated)[0].astype(jnp.bfloat16)
    up_grad = contract_rows(normed_two_low, grad_hidden)
    grad_normed_two = times_transpose(grad_hidden, up_low)
    grad_resid_norm, gain_two_grad, bias_two_grad = norm_two_back(grad_normed_two)
    grad_resid = grad_out.astype(jnp.float32) + grad_resid_norm
    grad_resid_low = grad_resid.astype(jnp.bfloat16)
    out_grad = contract_rows(mixed_low, grad_resid_low)
    grad_mixed = times_transpose(grad_resid_low, out_low).reshape(count, group, HEADS, HEAD_DIM)
    grad_query, grad_key_attend, grad_value_attend, grad_prior_state, grad_prior_sum = attend_back(
        grad_mixed
    )
    back_state = grad_prior_state.reshape(count, HEADS, HEAD_DIM * HEAD_DIM)
    back_sum = grad_prior_sum.reshape(count, HEADS * HEAD_DIM)
    later_state, later_sum = entering((back_state, back_sum), "seq", add_pair, empty_pair)
    _, state_back = jax.vjp(group_state, key_feat, value_rows)
    grad_key_state, grad_value_state = state_back(
        (
            later_state.reshape(count, HEADS, HEAD_DIM, HEAD_DIM),
            later_sum.reshape(count, HEADS, HEAD_DIM),
        )
    )
    grad_projected = feat_back(
        (grad_query, grad_key_attend + grad_key_state, grad_value_attend + grad_value_state)
    )[0]
    grad_projected_low = grad_projected.astype(jnp.bfloat16)
    qkv_grad = contract_rows(normed_one_low, grad_projected_low)
    grad_normed_one = times_transpose(grad_projected_low, qkv_low)
    grad_in_norm, gain_one_grad, bias_one_grad = norm_one_back(grad_normed_one)
    input_grad = (grad_resid + grad_in_norm).astype(jnp.bfloat16).reshape(count, group, width)
    norm_grad = jnp.stack([gain_one_grad, bias_one_grad, gain_two_grad, bias_two_grad])
    qkv_red, out_red, up_red, down_red, norm_red = (
        lax.psum_scatter(qkv_grad, ("seq", "img"), scatter_dimension=0, tiled=True),
        lax.psum_scatter(out_grad, ("seq", "img"), scatter_dimension=0, tiled=True),
        lax.psum_scatter(up_grad, ("seq", "img"), scatter_dimension=0, tiled=True),
        lax.psum_scatter(down_grad, ("seq", "img"), scatter_dimension=0, tiled=True),
        lax.psum_scatter(norm_grad, ("seq", "img"), scatter_dimension=1, tiled=True),
    )
    reduced = (qkv_red, out_red, up_red, down_red, norm_red)
    local_squares = jnp.float32(0.0)
    for grad in reduced:
        local_squares = local_squares + jnp.sum(grad * grad)
    total_squares = lax.psum(local_squares, ("seq", "img"))
    grad_norm = jnp.sqrt(total_squares)
    clip = jnp.minimum(1.0, CLIP_LIMIT / (grad_norm + 1e-06))
    out_fan = max(1, D * 64 // (group * lax.axis_size("seq")))
    rates = (3.0 * D ** (-0.5), 3.0 * out_fan ** (-0.5), 3.0 * D ** (-0.5), 3.0 * FF ** (-0.5), 1.5)
    decays = (WEIGHT_DECAY, WEIGHT_DECAY, WEIGHT_DECAY, WEIGHT_DECAY, 0.0)
    masters = (qkv_weight, out_weight, up_weight, down_weight, norm_params)
    firsts = (qkv_first, out_first, up_first, down_first, norm_first)
    seconds = (qkv_second, out_second, up_second, down_second, norm_second)
    news = [
        adam_update(masters[k], firsts[k], seconds[k], clip * reduced[k], rates[k], decays[k])
        for k in range(5)
    ]
    return (
        activations,
        input_grad,
        grad_norm,
        news[0][0],
        news[1][0],
        news[2][0],
        news[3][0],
        news[4][0],
        news[0][1],
        news[1][1],
        news[2][1],
        news[3][1],
        news[4][1],
        news[0][2],
        news[1][2],
        news[2][2],
        news[3][2],
        news[4][2],
    )


def solution(mesh):
    return jax.shard_map(
        body,
        mesh=mesh,
        in_specs=(
            P("img", "seq", None),
            P("img", "seq", None),
            P(("seq", "img"), None),
            P(("seq", "img"), None),
            P(("seq", "img"), None),
            P(("seq", "img"), None),
            P(None, ("seq", "img")),
            P(("seq", "img"), None),
            P(("seq", "img"), None),
            P(("seq", "img"), None),
            P(("seq", "img"), None),
            P(None, ("seq", "img")),
            P(("seq", "img"), None),
            P(("seq", "img"), None),
            P(("seq", "img"), None),
            P(("seq", "img"), None),
            P(None, ("seq", "img")),
        ),
        out_specs=(
            P("img", "seq", None),
            P("img", "seq", None),
            P(),
            P(("seq", "img"), None),
            P(("seq", "img"), None),
            P(("seq", "img"), None),
            P(("seq", "img"), None),
            P(None, ("seq", "img")),
            P(("seq", "img"), None),
            P(("seq", "img"), None),
            P(("seq", "img"), None),
            P(("seq", "img"), None),
            P(None, ("seq", "img")),
            P(("seq", "img"), None),
            P(("seq", "img"), None),
            P(("seq", "img"), None),
            P(("seq", "img"), None),
            P(None, ("seq", "img")),
        ),
        check_vma=False,
    )
```

profile of v0, /device:TPU:0, one launch (start us, length us, event | category | flops | bytes accessed | tf_op | source)
XLA Modules:
  0.0 1633.6 jit_solution(6049076471616553684)
XLA Ops:
  9.7 69.9 %all-gather = bf16[32,32,4]{1,2,0:T(4,128)(2,1)S(1)} all-gather(bf16[1,32,4]{1,2,0:T(4,128)(2,1)S(1)} %convert_bitcast_fusion.1), channel_id=1, replica_groups=mesh['seq'=8,'img'=4] {'seq','img'}, dimensions={0}, use_global_device_ids=true | all-gather | bytes 8448 | tf_op jit(solution)/shard_map/all_gather | solution.py:154
  83.9 8.7 copy.67
  92.6 4.9 convolution_bitcast_fusion
  103.3 14.3 all_gather.34
  121.5 8.7 while.31
  132.7 5.1 divide_convert_fusion
  137.8 43.2 %all-gather.12.cloned.1.call-done = bf16[1024,1024]{1,0:T(8,128)(2,1)} async-done(((bf16[32,1024]{1,0:T(8,128)(2,1)}), bf16[1024,1024]{1,0:T(8,128)(2,1)}) %all-gather.12.cloned.1.call-update) | async-done | bytes 2097168 | tf_op jit(solution)/shard_map/all_gather | solution.py:151
  183.7 77.1 %all-gather.14.cloned.1.call-done = bf16[1024,4096]{1,0:T(8,128)(2,1)} async-done(((bf16[32,4096]{1,0:T(8,128)(2,1)}), bf16[1024,4096]{1,0:T(8,128)(2,1)}) %all-gather.14.cloned.1.call-update) | async-done | bytes 8388624 | tf_op jit(solution)/shard_map/all_gather | solution.py:152
  260.8 7.8 fusion.109
  268.6 71.7 %all-gather.16.cloned.1.call-done = bf16[4096,1024]{1,0:T(8,128)(2,1)} async-done(((bf16[128,1024]{1,0:T(8,128)(2,1)}), bf16[4096,1024]{1,0:T(8,128)(2,1)}) %all-gather.16.cloned.1.call-update) | async-done | bytes 8388624 | tf_op jit(solution)/shard_map/all_gather | solution.py:153
  340.3 11.8 fusion.6
  365.8 14.3 all_gather.39
  392.3 7.2 while.30
  403.0 6.4 fusion.28
  420.1 7.9 fusion.95
  428.3 9.9 fusion.108
  439.2 10.7 fusion.70
  450.0 8.3 fusion.43
  458.9 89.4 %reduce-scatter.16.cloned.1.call-done = f32[32,4]{1,0:T(8,128)} async-done(((f32[1024,4]{1,0:T(8,128)}), f32[32,4]{1,0:T(8,128)}) %reduce-scatter.16.cloned.1.call-update) | async-done | bytes 528
  549.7 138.4 %reduce-scatter.10.cloned.1.call-done = f32[32,1024]{1,0:T(8,128)} async-done(((f32[1024,1024]{1,0:T(8,128)}), f32[32,1024]{1,0:T(8,128)}) %reduce-scatter.10.cloned.1.call-update) | async-done | bytes 131088 | tf_op jit(solution)/shard_map/reduce_scatter | solution.py:229
  689.7 158.9 %reduce-scatter.8.cloned.1.call-done = f32[32,3072]{1,0:T(8,128)} async-done(((f32[1024,3072]{1,0:T(8,128)}), f32[32,3072]{1,0:T(8,128)}) %reduce-scatter.8.cloned.1.call-update) | async-done | bytes 393232 | tf_op jit(solution)/shard_map/reduce_scatter | solution.py:228
  851.6 355.9 %reduce-scatter.12.cloned.1.call-done = f32[32,4096]{1,0:T(8,128)} async-done(((f32[1024,4096]{1,0:T(8,128)}), f32[32,4096]{1,0:T(8,128)}) %reduce-scatter.12.cloned.1.call-update) | async-done | bytes 524304 | tf_op jit(solution)/shard_map/reduce_scatter | solution.py:230
  1210.0 358.9 %reduce-scatter.14.cloned.1.call-done = f32[128,1024]{1,0:T(8,128)} async-done(((f32[4096,1024]{1,0:T(8,128)}), f32[128,1024]{1,0:T(8,128)}) %reduce-scatter.14.cloned.1.call-update) | async-done | bytes 524304 | tf_op jit(solution)/shard_map/reduce_scatter | solution.py:231
  1574.6 40.6 %psum.7 = f32[]{:T(128)} all-reduce(f32[]{:T(128)S(6)} %add.313), channel_id=1, replica_groups=mesh['seq'=8,'img'=4] {'seq','img'}, use_global_device_ids=true, to_apply=%region_29.30 | all-reduce | flops 1 | bytes 8 | tf_op jit(solution)/shard_map/psum | solution.py:238
  (233 shorter events, 98.7 us)
Async XLA Ops:
  7.2 76.7 %all-gather.8.cloned.1.call-start = ((), (), s32[]{:S(2)}) async-start(), calls=%async_computation.5 | async-start | bytes 6488064 | tf_op jit(solution)/shard_map/all_gather | solution.py:150
  9.0 112.6 %all-gather.10.cloned.1.call-start = ((), (), s32[]{:S(2)}) async-start(), calls=%async_computation.6 | async-start | bytes 1179648 | tf_op jit(solution)/shard_map/all_gather | solution.py:25
  100.5 80.5 %all-gather.12.cloned.1.call-start = ((), (), s32[]{:S(2)}) async-start(), calls=%async_computation.7 | async-start | bytes 2162688 | tf_op jit(solution)/shard_map/all_gather | solution.py:151
  101.3 159.5 %all-gather.14.cloned.1.call-start = ((), (), s32[]{:S(2)}) async-start(), calls=%async_computation.8 | async-start | bytes 8650752 | tf_op jit(solution)/shard_map/all_gather | solution.py:152
  102.1 238.2 %all-gather.16.cloned.1.call-start = ((), (), s32[]{:S(2)}) async-start(), calls=%async_computation.9 | async-start | bytes 8650752 | tf_op jit(solution)/shard_map/all_gather | solution.py:153
  102.9 289.4 %all-gather.18.cloned.1.call-start = ((), (), s32[]{:S(2)}) async-start(), calls=%async_computation.10 | async-start | bytes 1179648 | tf_op jit(solution)/shard_map/all_gather | solution.py:50
  103.0 284.9 %copy-start.9 = (f32[256,256]{0,1:T(8,128)}, f32[256,256]{0,1:T(8,128)S(1)}, u32[]{:S(2)}) copy-start(f32[256,256]{0,1:T(8,128)S(1)} %fusion.98) | copy-start | bytes 786436
  137.8 130.8 %copy-start.11 = (bf16[1,256,16,64]{1,3,2,0:T(8,128)(2,1)}, bf16[1,256,16,64]{1,3,2,0:T(8,128)(2,1)S(1)}, u32[]{:S(2)}) copy-start(bf16[1,256,16,64]{1,3,2,0:T(8,128)(2,1)S(1)} %get-tuple-element.293) | copy-start | bytes 1572868
  260.8 79.5 %copy-start.17 = (bf16[1,256,1024]{2,1,0:T(8,128)(2,1)S(1)}, bf16[1,256,1024]{2,1,0:T(8,128)(2,1)}, u32[]{:S(2)}) copy-start(bf16[1,256,1024]{2,1,0:T(8,128)(2,1)} %param.22) | copy-start | bytes 1572868
  362.7 185.7 %reduce-scatter.16.cloned.1.call-start = ((), (), s32[]{:S(2)}) async-start(), calls=%async_computation.15 | async-start | bytes 540672
  417.3 270.9 %reduce-scatter.10.cloned.1.call-start = ((), (), s32[]{:S(2)}) async-start(), calls=%async_computation.12 | async-start | bytes 4325376 | tf_op jit(solution)/shard_map/reduce_scatter | solution.py:229
  420.0 428.6 %reduce-scatter.8.cloned.1.call-start = ((), (), s32[]{:S(2)}) async-start(), calls=%async_computation.11 | async-start | bytes 12976128 | tf_op jit(solution)/shard_map/reduce_scatter | solution.py:228
  428.0 779.5 %reduce-scatter.12.cloned.1.call-start = ((), (), s32[]{:S(2)}) async-start(), calls=%async_computation.13 | async-start | bytes 17301504 | tf_op jit(solution)/shard_map/reduce_scatter | solution.py:230
  438.2 1130.7 %reduce-scatter.14.cloned.1.call-start = ((), (), s32[]{:S(2)}) async-start(), calls=%async_computation.14 | async-start | bytes 17301504 | tf_op jit(solution)/shard_map/reduce_scatter | solution.py:231
  450.0 1122.0 %copy-start.8 = (f32[256,1024]{1,0:T(8,128)S(1)}, f32[256,1024]{1,0:T(8,128)}, u32[]{:S(2)}) copy-start(f32[256,1024]{1,0:T(8,128)} %copy-done.7) | copy-start | bytes 3145732
  450.0 1122.0 %copy-start.37 = (f32[256]{0:T(256)S(1)}, f32[256]{0:T(256)}, u32[]{:S(2)}) copy-start(f32[256]{0:T(256)} %copy-done.35) | copy-start | bytes 3076
  450.0 1122.0 %copy-start.40 = (f32[256]{0:T(256)S(1)}, f32[256]{0:T(256)}, u32[]{:S(2)}) copy-start(f32[256]{0:T(256)} %copy-done.38) | copy-start | bytes 3076
  458.4 1158.9 %copy-start.31 = (f32[32,3072]{1,0:T(8,128)S(1)}, f32[32,3072]{1,0:T(8,128)}, u32[]{:S(2)}) copy-start(f32[32,3072]{1,0:T(8,128)} %param.23) | copy-start | bytes 1179652
  851.6 770.0 %copy-start.24 = (f32[32,4096]{1,0:T(8,128)S(1)}, f32[32,4096]{1,0:T(8,128)}, u32[]{:S(2)}) copy-start(f32[32,4096]{1,0:T(8,128)} %param.25) | copy-start | bytes 1572868
  1207.5 414.1 %copy-start.27 = (f32[32,4096]{1,0:T(8,128)S(1)}, f32[32,4096]{1,0:T(8,128)}, u32[]{:S(2)}) copy-start(f32[32,4096]{1,0:T(8,128)} %reduce-scatter.12.cloned.1.call-done) | copy-start | bytes 1572868
  1574.6 49.6 %copy-start.26 = (f32[128,1024]{1,0:T(8,128)S(1)}, f32[128,1024]{1,0:T(8,128)}, u32[]{:S(2)}) copy-start(f32[128,1024]{1,0:T(8,128)} %param.26) | copy-start | bytes 1572868
  1574.6 49.6 %copy-start.28 = (f32[128,1024]{1,0:T(8,128)S(1)}, f32[128,1024]{1,0:T(8,128)}, u32[]{:S(2)}) copy-start(f32[128,1024]{1,0:T(8,128)} %reduce-scatter.14.cloned.1.call-done) | copy-start | bytes 1572868
  1574.6 49.6 %copy-start.33 = (f32[128,1024]{1,0:T(8,128)S(1)}, f32[128,1024]{1,0:T(8,128)}, u32[]{:S(2)}) copy-start(f32[128,1024]{1,0:T(8,128)} %param.31) | copy-start | bytes 1572868
  1574.6 49.6 %copy-start.34 = (f32[128,1024]{1,0:T(8,128)S(1)}, f32[128,1024]{1,0:T(8,128)}, u32[]{:S(2)}) copy-start(f32[128,1024]{1,0:T(8,128)} %param.36) | copy-start | bytes 1572868
  (36 other events, 231.1 us)
Sparse Core Ops, SparseCore 0:
  11.5 72.3 all-gather.7
  100.6 20.8 all-gather.9
  125.0 56.0 all-gather.11
  184.3 76.3 all-gather.13
  264.1 76.1 all-gather.15
  362.8 20.7 all-gather.17
  417.4 130.8 reduce-scatter.15
  550.7 137.4 reduce-scatter.9
  695.2 153.3 reduce-scatter.7
  850.7 356.7 reduce-scatter.11
  1209.8 359.0 reduce-scatter.13
where the time goes:
time: 1640 us; the launch traced here: 1630 us
  waiting for transfers between devices  1300 us (79%)
  blocking collectives  139 us (8%)
  matrix products  106 us (6%)
  other arithmetic  48.7 us (3%)
  local copies, waits for them, and re-layouts  21.7 us (1%)
  between operations  20.1 us (1%)
    reduce_scatter x1, waiting for transfers between devices, body(): lax.psum_scatter(down_grad, ('seq', 'img'), scatter_dimension=0, tiled=True)  359 us
    reduce_scatter x1, waiting for transfers between devices, body(): lax.psum_scatter(up_grad, ('seq', 'img'), scatter_dimension=0, tiled=True)  356 us
    reduce_scatter x1, waiting for transfers between devices, body(): lax.psum_scatter(qkv_grad, ('seq', 'img'), scatter_dimension=0, tiled=True)  159 us
    reduce_scatter x1, waiting for transfers between devices, body(): lax.psum_scatter(out_grad, ('seq', 'img'), scatter_dimension=0, tiled=True)  138 us
    unnamed x12, waiting for transfers between devices  89.6 us
    all_gather x1, waiting for transfers between devices, body(): lax.all_gather(up_weight.astype(jnp.bfloat16), ('seq', 'img'), axis=0, ti...  77.1 us
    all_gather x1, waiting for transfers between devices, body(): lax.all_gather(down_weight.astype(jnp.bfloat16), ('seq', 'img'), axis=0,...  71.7 us
    all_gather x1, blocking collectives, body(): lax.all_gather(norm_params.astype(jnp.bfloat16), ('seq', 'img'), axis=1,...  69.9 us
  transfers between devices with their start and end apart: 11, of which 10 were waited for; matrix products, arithmetic and copies ran while one was open for 6% of the time, Pallas kernels for 0%

commit v1 on v0

v1 whole, which is shorter than its diff:
```python
import functools

import jax
import jax.numpy as jnp
from jax import lax
from jax.experimental import pallas as pl
from jax.experimental.pallas import tpu as pltpu
from jax.sharding import PartitionSpec as P

HEAD_DIM = 64
STEP = 10
NORM_EPS = 1e-05
BETA_ONE = 0.9
BETA_TWO = 0.999
ADAM_EPS = 1e-08
WEIGHT_DECAY = 0.1
CLIP_LIMIT = 1.0
LANES = 128

LOW = jnp.bfloat16
WIDE = jnp.float32
ALL = ("z", "c", "y", "x")
SWAP = [(0, 1), (1, 0)]


def swap(value, axis):
    return lax.ppermute(value, axis, SWAP)


def shift(value, step, wrap=True):
    size = lax.axis_size("z")
    pairs = [(i, (i + step) % size) for i in range(size) if wrap or 0 <= i + step < size]
    return lax.ppermute(value, "z", pairs)


def mine(pair_axis_first):
    return jnp.where(lax.axis_index("c") == 0, pair_axis_first[0], pair_axis_first[1])


def other(pair_axis_first):
    return jnp.where(lax.axis_index("c") == 0, pair_axis_first[1], pair_axis_first[0])


def in_order(own, mate, axis=0):
    first = lax.axis_index("c") == 0
    return jnp.concatenate([jnp.where(first, own, mate), jnp.where(first, mate, own)], axis)


def gather_chips(shard):
    column = jnp.stack([shard] + [shift(shard, k) for k in range(1, lax.axis_size("z"))])
    half = column.shape[0] // 2
    along_x, along_y = swap(column, "x"), swap(column, "y")
    far = (swap(along_y[:half], "x"), swap(along_x[half:], "y"))
    return (column, along_x, along_y) + far


def gathered_places(depth):
    half = depth // 2
    places = [(0, k, (k, 0, 0)) for k in range(depth)]
    places += [(1, k, (k, 0, 1)) for k in range(depth)]
    places += [(2, k, (k, 1, 0)) for k in range(depth)]
    places += [(3, k, (k, 1, 1)) for k in range(half)]
    places += [(4, k - half, (k, 1, 1)) for k in range(half, depth)]
    return places


def reduce_chips(send_x, keep_x, send_y, keep_y):
    depth = send_x.shape[1]
    got_x, got_y = swap(send_x, "x"), swap(send_y, "y")
    wide = lambda a: a.astype(WIDE)
    on_y = swap((wide(keep_x[1]) + wide(got_x[1])).astype(LOW), "y")
    on_x = swap((wide(keep_y[1]) + wide(got_y[1])).astype(LOW), "x")
    parts = []
    for k in range(depth):
        one = wide(keep_x[0, k]) + wide(got_x[0, k]) + wide(on_y[k])
        two = wide(keep_y[0, k]) + wide(got_y[0, k]) + wide(on_x[k])
        parts.append(jnp.concatenate([one, two]))
    total = parts[0]
    for k in range(1, depth):
        total = total + wide(shift(parts[k].astype(LOW), k))
    return total


def coordinates():
    return jnp.stack([lax.axis_index("z"), lax.axis_index("y"), lax.axis_index("x")]).astype(jnp.int32)


def chip_of(coords, rel, depth, back):
    dz, dy, dx = rel
    z, y, x = coords[0], coords[1], coords[2]
    zz = lax.rem(z + (depth - dz if back else dz), depth)
    yy = 1 - y if dy else y
    xx = 1 - x if dx else x
    return zz, yy * 2 + xx


def run_copies(copies, sems):
    started = [pltpu.make_async_copy(src, dst, sems.at[i]) for i, (src, dst) in enumerate(copies)]
    for copy in started:
        copy.start()
    for copy in started:
        copy.wait()


def window(ref, lead, row, rows, col, cols):
    rows_at = pl.ds(row if isinstance(row, int) else pl.multiple_of(row, 16), rows)
    return ref.at[(*lead, rows_at, pl.ds(col, cols))]


def place(parts, depth, outs, moves):
    spots = gathered_places(depth)
    count = len(spots) * len(moves(0, 0))

    def kernel(coords, *refs):
        ins, out_refs, sems = refs[: len(parts)], refs[len(parts) : len(parts) + len(outs)], refs[-1]
        copies = []
        for array, slot, rel in spots:
            zz, plane = chip_of(coords, rel, depth, True)
            for o, sr, sc, rows, cols, tr, tc in moves(zz, plane):
                copies.append(
                    (window(ins[array], (slot,), sr, rows, sc, cols), window(out_refs[o], (), tr, rows, tc, cols))
                )
        run_copies(copies, sems)

    return pl.pallas_call(
        kernel,
        out_shape=[jax.ShapeDtypeStruct(s, LOW) for s in outs],
        in_specs=[pl.BlockSpec(memory_space=pltpu.SMEM)] + [pl.BlockSpec(memory_space=pl.ANY)] * len(parts),
        out_specs=[pl.BlockSpec(memory_space=pl.ANY)] * len(outs),
        scratch_shapes=[pltpu.SemaphoreType.DMA((count,))],
    )(coordinates(), *parts)


def unplace(grads, depth, rows_cols, moves):
    spots = []
    for dz in range(depth):
        for d in range(2):
            spots += [(0, d, dz, (dz, d, 1), 0), (1, d, dz, (dz, d, 0), 0)]
            spots += [(2, d, dz, (dz, 1, d), 1), (3, d, dz, (dz, 0, d), 1)]
    count = len(spots) * len(moves(0, 0, 0))

    def kernel(coords, *refs):
        ins, out_refs, sems = refs[: len(grads)], refs[len(grads) : len(grads) + 4], refs[-1]
        copies = []
        for array, d, dz, rel, half in spots:
            zz, plane = chip_of(coords, rel, depth, False)
            for i, sr, sc, rows, cols, tr, tc in moves(zz, plane, half):
                copies.append(
                    (window(ins[i], (), sr, rows, sc, cols), window(out_refs[array], (d, dz), tr, rows, tc, cols))
                )
        run_copies(copies, sems)

    return pl.pallas_call(
        kernel,
        out_shape=[jax.ShapeDtypeStruct((2, depth) + rows_cols, LOW)] * 4,
        in_specs=[pl.BlockSpec(memory_space=pltpu.SMEM)] + [pl.BlockSpec(memory_space=pl.ANY)] * len(grads),
        out_specs=[pl.BlockSpec(memory_space=pl.ANY)] * 4,
        scratch_shapes=[pltpu.SemaphoreType.DMA((count,))],
    )(coordinates(), *grads)


def layer_norm(values, gain, bias):
    center = values - jnp.mean(values, axis=-1, keepdims=True)
    spread = jnp.mean(center * center, axis=-1, keepdims=True)
    return center * lax.rsqrt(spread + NORM_EPS) * gain + bias


def feature_map(values):
    return jax.nn.elu(values) + 1.0


def gelu_tanh(values):
    return jax.nn.gelu(values, approximate=True)


def dot(left, right):
    return jnp.dot(left, right, preferred_element_type=WIDE)


def dot_rows(left, right):
    return lax.dot_general(left, right, (((0,), (0,)), ((), ())), preferred_element_type=WIDE)


def dot_cols(left, right):
    return lax.dot_general(left, right, (((1,), (1,)), ((), ())), preferred_element_type=WIDE)


def mul(spec, left, right):
    return jnp.einsum(spec, left, right, preferred_element_type=WIDE)


def adam_update(weight, first, second, grad, rate, decay):
    first_new = BETA_ONE * first + (1.0 - BETA_ONE) * grad
    second_new = BETA_TWO * second + (1.0 - BETA_TWO) * grad * grad
    first_hat = first_new / (1.0 - BETA_ONE**STEP)
    second_hat = second_new / (1.0 - BETA_TWO**STEP)
    weight_new = weight - rate * (first_hat / (jnp.sqrt(second_hat) + ADAM_EPS) + decay * weight)
    return (weight_new, first_new, second_new)


def from_others(value, step):
    low = value.astype(LOW)
    total = jnp.zeros(value.shape, WIDE)
    for k in range(1, lax.axis_size("z")):
        total = total + shift(low, step * k, wrap=False).astype(WIDE)
    return total


def sum_everywhere(value, direct):
    if not direct:
        return lax.psum(value, ALL)
    value = jnp.broadcast_to(value, (8, LANES))
    value = value + swap(value, "c")
    across = lax.ppermute(value, ("y", "x"), [(i, 3 - i) for i in range(4)])
    value = value + swap(value, "y") + (swap(value, "x") + across)
    near = [shift(value, k) for k in range(1, lax.axis_size("z"))]
    for part in near:
        value = value + part
    return value[0, 0]


def body(
    images,
    cotangent,
    qkv_weight,
    out_weight,
    up_weight,
    down_weight,
    norm_params,
    qkv_first,
    out_first,
    up_first,
    down_first,
    norm_first,
    qkv_second,
    out_second,
    up_second,
    down_second,
    norm_second,
):
    depth, core = lax.axis_size("z"), lax.axis_index("c")
    count, group, width = images.shape
    hidden_units = up_weight.shape[1]
    own_rows = qkv_weight.shape[0]
    own_units = down_weight.shape[0]
    chips = lax.axis_size("y") * lax.axis_size("x")
    block, ff_block = width // (2 * depth), hidden_units // (2 * depth)
    half_qkv, half_ff, half_d = 3 * width // 2, hidden_units // 2, width // 2
    ring = lax.axis_size("y") == 2 and lax.axis_size("x") == 2 and depth % 2 == 0 and own_rows % 32 == 0
    heads = half_d // HEAD_DIM
    tokens = 2 * group

    own_x, own_g = images.reshape(group, width), cotangent.reshape(group, width)
    split_qkv = lambda w: jnp.moveaxis(w.reshape(-1, 3 * depth, 2, block), 2, 0).reshape(2, -1, half_qkv)
    split_up = lambda w: jnp.moveaxis(w.reshape(-1, depth, 2, ff_block), 2, 0).reshape(2, -1, half_ff)

    qkv_low, out_low = qkv_weight.astype(LOW), out_weight.astype(LOW)
    up_low, down_low = up_weight.astype(LOW), down_weight.astype(LOW)
    norm_low = norm_params.astype(LOW)
    if ring:
        pad = jnp.zeros((own_rows, LANES - 4), LOW)
        norm_cols = jnp.concatenate([norm_low.T, pad], axis=1)
        pair = split_qkv(qkv_low)
        qkv_mine = jnp.concatenate([mine(pair), norm_cols], axis=1)
        qkv_mate = swap(jnp.concatenate([other(pair), norm_cols], axis=1), "c")
        pair = split_up(up_low)
        up_mine, up_mate = mine(pair), swap(other(pair), "c")
        out_part = jnp.concatenate([out_low[:, :half_d], out_low[:, half_d:]])
        up_part = jnp.concatenate([in_order(up_mine, up_mate), out_part], axis=1)
        x_mate, g_mate = swap(own_x, "c"), swap(own_g, "c")
        qkv_parts = gather_chips(in_order(qkv_mine, qkv_mate))
        up_parts = gather_chips(up_part)
        down_parts = gather_chips(down_low)

        def qkv_moves(zz, plane):
            row = lambda h: ((zz * 2 + h) * chips + plane) * own_rows
            moves = [(0, h * own_rows, 0, own_rows, half_qkv, row(h), 0) for h in (0, 1)]
            return moves + [(1, h * own_rows, half_qkv, own_rows, LANES, row(h), 0) for h in (0, 1)]

        def up_moves(zz, plane):
            row = lambda h: ((zz * 2 + h) * chips + plane) * own_rows
            moves = [(0, h * own_rows, 0, own_rows, half_ff, row(h), 0) for h in (0, 1)]
            to = zz * block + plane * own_rows
            return moves + [(1, h * own_rows, half_ff, own_rows, half_d, to, h * half_d) for h in (0, 1)]

        def down_moves(zz, plane):
            return [(0, 0, 0, own_units, width, zz * ff_block + plane * own_units, 0)]

        qkv_w, norm_w = place(qkv_parts, depth, [(width, half_qkv), (width, LANES)], qkv_moves)
        up_w, out_w = place(up_parts, depth, [(width, half_ff), (half_d, width)], up_moves)
        (down_w,) = place(down_parts, depth, [(half_ff, width)], down_moves)
        norm_vals = norm_w[:, :4].T.astype(WIDE)
    else:
        x_mate, g_mate = swap(own_x, "c"), swap(own_g, "c")
        whole = lambda w, axis=0: lax.all_gather(w, ALL, axis=axis, tiled=True)
        qkv_w, up_w = mine(split_qkv(whole(qkv_low))), mine(split_up(whole(up_low)))
        rows_half = lambda w, b: mine(jnp.moveaxis(w.reshape(depth, 2, b, width), 1, 0)).reshape(-1, width)
        out_w, down_w = rows_half(whole(out_low), block), rows_half(whole(down_low), ff_block)
        norm_vals = whole(norm_low, 1).astype(WIDE)

    inputs = in_order(own_x, x_mate).astype(WIDE)
    grad_out = in_order(own_g, g_mate)
    normed_one, norm_one_back = jax.vjp(layer_norm, inputs, norm_vals[0], norm_vals[1])
    normed_one_low = normed_one.astype(LOW)
    projected = dot(normed_one_low, qkv_w)
    by_head = lambda a: a.reshape(tokens, heads, HEAD_DIM)
    feats, feat_back = jax.vjp(feature_map, projected[:, : 2 * half_d])
    feats = feats.astype(LOW)
    query_feat, key_feat = by_head(feats[:, :half_d]), by_head(feats[:, half_d:])
    values = by_head(projected[:, 2 * half_d :].astype(LOW))

    state = mul("the,thf->hef", key_feat, values)
    keysum = jnp.sum(key_feat.astype(WIDE), axis=0)
    pack = lambda s, k: jnp.concatenate([s.reshape(-1, LANES), k.reshape(-1, LANES)])
    unpack = lambda a: (
        a[: heads * HEAD_DIM // 2].reshape(heads, HEAD_DIM, HEAD_DIM),
        a[heads * HEAD_DIM // 2 :].reshape(heads, HEAD_DIM),
    )
    state_in, keysum_in = unpack(from_others(pack(state, keysum), 1))
    state_in_low, keysum_in_low = state_in.astype(LOW), keysum_in.astype(LOW)
    causal = jnp.tril(jnp.ones((tokens, tokens), WIDE))
    scores = mul("the,she->hts", query_feat, key_feat) * causal
    scores_low = scores.astype(LOW)
    numer = mul("hts,shf->thf", scores_low, values) + mul("the,hef->thf", query_feat, state_in_low)
    denom = jnp.sum(scores, axis=-1).T + mul("the,he->th", query_feat, keysum_in_low)
    mixed = (numer / denom[..., None]).reshape(tokens, half_d)
    mixed_low = mixed.astype(LOW)

    out_part = dot(mixed_low, out_w)
    resid = inputs + out_part + swap(out_part.astype(LOW), "c").astype(WIDE)
    normed_two, norm_two_back = jax.vjp(layer_norm, resid, norm_vals[2], norm_vals[3])
    normed_two_low = normed_two.astype(LOW)
    hidden = dot(normed_two_low, up_w)
    activated, gelu_back = jax.vjp(gelu_tanh, hidden)
    activated_low = activated.astype(LOW)
    down_grad = dot_rows(activated_low, grad_out).astype(LOW)

    halves = lambda a: a.reshape(2, group, -1)
    down_part = dot(activated_low, down_w)
    got = swap(other(halves(down_part)).astype(LOW), "c").astype(WIDE)
    activations = (mine(halves(resid + down_part)) + got).astype(LOW)

    grad_hidden = gelu_back(dot_cols(grad_out, down_w))[0].astype(LOW)
    up_grad = dot_rows(normed_two_low, grad_hidden).astype(LOW)
    grad_two = dot_cols(grad_hidden, up_w)
    grad_two = grad_two + swap(grad_two.astype(LOW), "c").astype(WIDE)
    grad_resid_norm, gain_two_grad, bias_two_grad = norm_two_back(grad_two)
    grad_resid = grad_out.astype(WIDE) + grad_resid_norm
    grad_resid_low = grad_resid.astype(LOW)
    out_grad = dot_rows(mixed_low, grad_resid_low).astype(LOW)

    grad_mixed = by_head(dot_cols(grad_resid_low, out_w))
    a_rows = grad_mixed / denom[..., None]
    b_rows = -jnp.sum(a_rows * by_head(mixed), axis=-1)
    a_low = a_rows.astype(LOW)
    state_grad = mul("the,thf->hef", query_feat, a_low)
    keysum_grad = jnp.sum(query_feat.astype(WIDE) * b_rows[..., None], axis=0)
    later_state, later_sum = unpack(from_others(pack(state_grad, keysum_grad), -1))
    later_state_low = later_state.astype(LOW)
    pulls = (mul("thf,shf->hts", a_low, values) + b_rows.T[:, :, None]) * causal
    pulls_low = pulls.astype(LOW)
    grad_query = mul("hts,she->the", pulls_low, key_feat)
    grad_query = grad_query + mul("thf,hef->the", a_low, state_in_low)
    grad_query = grad_query + b_rows[..., None] * keysum_in
    grad_key = mul("hts,the->she", pulls_low, query_feat)
    grad_key = grad_key + mul("shf,hef->she", values, later_state_low) + later_sum
    grad_value = mul("hts,thf->shf", scores_low, a_low) + mul("she,hef->shf", key_feat, later_state_low)
    flat = lambda a: a.reshape(tokens, half_d)
    grad_feats = feat_back(jnp.concatenate([flat(grad_query), flat(grad_key)], axis=1))[0]
    grad_projected = jnp.concatenate([grad_feats, flat(grad_value)], axis=1).astype(LOW)
    qkv_grad = dot_rows(normed_one_low, grad_projected).astype(LOW)
    grad_one = dot_cols(grad_projected, qkv_w)
    grad_one = grad_one + swap(grad_one.astype(LOW), "c").astype(WIDE)
    grad_in_norm, gain_one_grad, bias_one_grad = norm_one_back(grad_one)
    input_grad = mine(halves(grad_resid + grad_in_norm)).astype(LOW)
    norm_grad = jnp.stack([gain_one_grad, bias_one_grad, gain_two_grad, bias_two_grad])

    if ring:
        norm_cols = jnp.concatenate([norm_grad.T.astype(LOW), jnp.zeros((width, LANES - 4), LOW)], axis=1)
        thin, small = own_units // 2, own_rows // 2

        def down_cuts(zz, plane, half):
            return [(0, zz * ff_block + plane * own_units + half * thin, 0, thin, width, 0, 0)]

        def up_cuts(zz, plane, half):
            cuts = [(0, ((zz * 2 + half) * chips + plane) * own_rows, 0, own_rows, half_ff, 0, 0)]
            row = zz * block + plane * own_rows + half * small
            return cuts + [(1, row, p * half_d, small, half_d, p * small, half_ff) for p in (0, 1)]

        def qkv_cuts(zz, plane, half):
            row = ((zz * 2 + half) * chips + plane) * own_rows
            return [(0, row, 0, own_rows, half_qkv, 0, 0), (1, row, 0, own_rows, LANES, 0, half_qkv)]

        down_red = reduce_chips(*unplace([down_grad], depth, (thin, width), down_cuts))
        up_red = reduce_chips(*unplace([up_grad, out_grad], depth, (own_rows, half_ff + half_d), up_cuts))
        qkv_red = reduce_chips(*unplace([qkv_grad, norm_cols], depth, (own_rows, half_qkv + LANES), qkv_cuts))
        out_halves = up_red[:, half_ff:].reshape(2, 2, small, half_d)
        out_red = jnp.concatenate([out_halves[:, 0], out_halves[:, 1]], axis=2).reshape(own_rows, width)
        by_rows = lambda a: a.reshape(2, own_rows, -1)
        norm_red = mine(by_rows(qkv_red[:, half_qkv : half_qkv + 4])).T

        def joined(part, blocks):
            part = by_rows(part)
            got = swap(other(part), "c")
            pair = in_order(mine(part)[None], got[None])
            pair = pair.reshape(2, own_rows, blocks, -1)
            return jnp.moveaxis(pair, 0, 2).reshape(own_rows, -1)

        qkv_red = joined(qkv_red[:, :half_qkv], 3 * depth)
        up_red = joined(up_red[:, :half_ff], depth)
    else:
        scatter = lambda g: lax.psum_scatter(g, ALL, scatter_dimension=0, tiled=True)
        both = lambda a, axis: jnp.stack([jnp.where(core == k, a, 0.0) for k in (0, 1)], axis)
        to_all = lambda a: a.astype(WIDE)
        qkv_red = scatter(both(to_all(qkv_grad).reshape(width, 3 * depth, block), 2).reshape(width, -1))
        up_red = scatter(both(to_all(up_grad).reshape(width, depth, ff_block), 2).reshape(width, -1))
        out_red = scatter(both(to_all(out_grad).reshape(depth, block, width), 1).reshape(width, width))
        down_red = scatter(both(to_all(down_grad).reshape(depth, ff_block, width), 1).reshape(hidden_units, width))
        norm_red = scatter(jnp.where(core == 0, norm_grad, 0.0).T).T

    reduced = (qkv_red, out_red, up_red, down_red, norm_red)
    local_squares = sum(jnp.sum(grad * grad) for grad in reduced)
    grad_norm = jnp.sqrt(sum_everywhere(local_squares, ring))
    clip = jnp.minimum(1.0, CLIP_LIMIT / (grad_norm + 1e-06))
    out_fan = max(1, width * 64 // (tokens * depth))
    rates = (3.0 * width**-0.5, 3.0 * out_fan**-0.5, 3.0 * width**-0.5, 3.0 * hidden_units**-0.5, 1.5)
    decays = (WEIGHT_DECAY, WEIGHT_DECAY, WEIGHT_DECAY, WEIGHT_DECAY, 0.0)
    masters = (qkv_weight, out_weight, up_weight, down_weight, norm_params)
    firsts = (qkv_first, out_first, up_first, down_first, norm_first)
    seconds = (qkv_second, out_second, up_second, down_second, norm_second)
    news = [
        adam_update(masters[k], firsts[k], seconds[k], clip * reduced[k], rates[k], decays[k]) for k in range(5)
    ]
    return (
        activations.reshape(count, group, width),
        input_grad.reshape(count, group, width),
        grad_norm,
        *[new[0] for new in news],
        *[new[1] for new in news],
        *[new[2] for new in news],
    )


def solution(mesh):
    depth, planes = mesh.shape["seq"] // 2, mesh.shape["img"]
    across = max(k for k in range(1, planes + 1) if planes % k == 0 and k * k <= planes)
    grid = jax.sharding.Mesh(mesh.devices.reshape(depth, 2, planes // across, across), ALL)
    tokens = P(("y", "x"), ("z", "c"), None)
    matrix, norm = P(ALL, None), P(None, ALL)
    state = (matrix, matrix, matrix, matrix, norm)
    return jax.shard_map(
        body,
        mesh=grid,
        in_specs=(tokens, tokens) + state * 3,
        out_specs=(tokens, tokens, P()) + state * 3,
        check_vma=False,
    )
```

time: 1640 us -> 1300 us (0.79)
  waiting for transfers between devices: 1300 us -> 210 us
  Pallas kernels: 0 us -> 792 us
  blocking collectives: 139 us -> 0 us
  starting transfers between devices: 0.71 us -> 93 us
  matrix products: 106 us -> 73.7 us
  local copies, waits for them, and re-layouts: 21.7 us -> 45.4 us
  other arithmetic: 48.7 us -> 70.2 us
    reduce_scatter x4 -> x0, waiting for transfers between devices: 1010 us -> none  [the longest x1 359 us: body(): lax.psum_scatter(down_grad, ('seq', 'img'), scatter_dimension=0, tiled=True)]
    pallas_call x0 -> x6, Pallas kernels: none -> 792 us  [the longest x3 396 us: unplace(): pl.pallas_call(kernel, out_shape=[jax.ShapeDtypeStruct((2, depth) + rows_...]
    ppermute x0 -> x65, waiting for transfers between devices: none -> 210 us  [the longest x37 113 us: swap(): return lax.ppermute(value, axis, SWAP)]
    all_gather x6 -> x0, waiting for transfers between devices: 195 us -> none  [the longest x1 77.1 us: body(): lax.all_gather(up_weight.astype(jnp.bfloat16), ('seq', 'img'), axis=0, ti...]
    all_gather x3 -> x0, blocking collectives: 98.5 us -> none  [the longest x1 69.9 us: body(): lax.all_gather(norm_params.astype(jnp.bfloat16), ('seq', 'img'), axis=1,...]
    ppermute x0 -> x65, starting transfers between devices: none -> 93 us  [the longest x27 61.7 us: shift(): return lax.ppermute(value, 'z', pairs)]
    unnamed x12 -> x0, waiting for transfers between devices: 89.6 us -> none
    psum x1 -> x0, blocking collectives: 40.6 us -> none  [body(): total_squares = lax.psum(local_squares, ('seq', 'img'))]
  transfers between devices with their start and end apart: 11 -> 65, of which waited for: 10 -> 20; matrix products, arithmetic and copies ran while one was open for 6% -> 11% of each run, Pallas kernels for 0% -> 61%
where the time goes in v1:
time: 1300 us; the launch traced here: 1290 us
  Pallas kernels  792 us (61%)
  waiting for transfers between devices  210 us (16%)
  starting transfers between devices  93 us (7%)
  matrix products  73.7 us (6%)
  other arithmetic  70.2 us (5%)
  local copies, waits for them, and re-layouts  45.4 us (3%)
    pallas_call x3, Pallas kernels, unplace(): pl.pallas_call(kernel, out_shape=[jax.ShapeDtypeStruct((2, depth) + rows_...  396 us
    pallas_call x3, Pallas kernels, place(): pl.pallas_call(kernel, out_shape=[jax.ShapeDtypeStruct(s, LOW) for s in o...  396 us
    ppermute x37, waiting for transfers between devices, swap(): return lax.ppermute(value, axis, SWAP)  113 us
    ppermute x27, waiting for transfers between devices, shift(): return lax.ppermute(value, 'z', pairs)  97.9 us
    ppermute x27, starting transfers between devices, shift(): return lax.ppermute(value, 'z', pairs)  61.7 us
    ppermute x37, starting transfers between devices, swap(): return lax.ppermute(value, axis, SWAP)  29.1 us
    dot_general x13, matrix products, mul(): return jnp.einsum(spec, left, right, preferred_element_type=WIDE)  27.5 us
  transfers between devices with their start and end apart: 65, of which 20 were waited for; matrix products, arithmetic and copies ran while one was open for 11% of the time, Pallas kernels for 61%

profile of v1, /device:TPU:0, one launch (start us, length us, event | category | flops | bytes accessed | tf_op | source)
XLA Modules:
  0.0 1292.0 jit_solution(4724046848861673034)
XLA Ops:
  29.2 21.5 %collective-permute-done.3 = bf16[64,1664]{1,0:T(8,128)(2,1)S(1)} collective-permute-done((bf16[64,1664]{1,0:T(8,128)(2,1)S(1)}, bf16[64,1664]{1,0:T(8,128)(2,1)S(1)}, u32[]{:S(2)}, u32[]{:S(2)}) %collective-permute-start.3) | collective-permute-done | bytes 213024 | tf_op jit(solution)/shard_map/ppermute | solution.py:33
  50.7 5.3 collective-permute-start.13
  63.4 13.1 %collective-permute-done.14 = bf16[64,2560]{1,0:T(8,128)(2,1)S(1)} collective-permute-done((bf16[64,2560]{1,0:T(8,128)(2,1)}, bf16[64,2560]{1,0:T(8,128)(2,1)S(1)}, u32[]{:S(2)}, u32[]{:S(2)}) %collective-permute-start.14) | collective-permute-done | bytes 327712 | tf_op jit(solution)/shard_map/ppermute | solution.py:33
  84.6 33.1 %collective-permute-done.7.refs_3_ = bf16[2,64,1664]{2,1,0:T(8,128)(2,1)S(1)} collective-permute-done((bf16[2,64,1664]{2,1,0:T(8,128)(2,1)S(1)}, bf16[2,64,1664]{2,1,0:T(8,128)(2,1)S(1)}, u32[]{:S(2)}, u32[]{:S(2)}) %collective-permute-start.7) | collective-permute-done | bytes 426016 | tf_op jit(solution)/shard_map/ppermute | solution.py:27
  119.6 105.6 %shard_map.304 = (bf16[1024,1536]{1,0:T(8,128)(2,1)}, bf16[1024,128]{1,0:T(8,128)(2,1)}) custom-call(s32[3]{0:T(128)} %pad_add_fusion.coords, bf16[4,64,1664]{2,1,0:T(8,128)(2,1)} %copy-done.25, bf16[4,64,1664]{2,1,0:T(8,128)(2,1)} %copy-done.33, bf16[4,64,1664]{2,1,0:T(8,128)(2,1)} %copy-done.34, bf16[2,64,1664]{2,1,0:T(8,128)(2,1)} %copy-done.54, ...), custom_call_target="tpu_custom_call" | custom-call | tf_op jit(solution)/shard_map/pallas_call | solution.py:125
  237.1 8.5 collective-permute-start.10
  265.9 24.9 %collective-permute-done.18.refs_3_ = bf16[2,64,2560]{2,1,0:T(8,128)(2,1)} collective-permute-done((bf16[2,64,2560]{2,1,0:T(8,128)(2,1)}, bf16[2,64,2560]{2,1,0:T(8,128)(2,1)}, u32[]{:S(2)}, u32[]{:S(2)}) %collective-permute-start.18) | collective-permute-done | bytes 655392 | tf_op jit(solution)/shard_map/ppermute | solution.py:27
  292.0 161.2 %shard_map.305 = (bf16[1024,2048]{1,0:T(8,128)(2,1)}, bf16[512,1024]{1,0:T(8,128)(2,1)}) custom-call(s32[3]{0:T(128)} %pad_add_fusion.coords, bf16[4,64,2560]{2,1,0:T(8,128)(2,1)} %pad_maximum_fusion.2.refs_0_, bf16[4,64,2560]{2,1,0:T(8,128)(2,1)} %collective-permute-done.16.refs_1_, bf16[4,64,2560]{2,1,0:T(8,128)(2,1)} %collective-permute-done.17.refs_2_, ...), custom_call_target="tpu_custom_call" | custom-call | tf_op jit(solution)/shard_map/pallas_call | solution.py:125
  468.4 5.3 collective-permute-done.26.refs_3_
  475.7 129.0 %shard_map.306 = bf16[2048,1024]{1,0:T(8,128)(2,1)} custom-call(s32[3]{0:T(128)} %pad_add_fusion.coords, bf16[4,128,1024]{2,1,0:T(8,128)(2,1)} %pad_maximum_fusion.4.refs_0_, bf16[4,128,1024]{2,1,0:T(8,128)(2,1)} %collective-permute-done.24.refs_1_, bf16[4,128,1024]{2,1,0:T(8,128)(2,1)} %collective-permute-done.25.refs_2_, ...), custom_call_target="tpu_custom_call" | custom-call | tf_op jit(solution)/shard_map/pallas_call | solution.py:125
  610.4 5.5 fusion.6
  624.4 129.1 %shard_map.309 = (bf16[2,4,64,1024]{3,2,1,0:T(8,128)(2,1)}, bf16[2,4,64,1024]{3,2,1,0:T(8,128)(2,1)}, bf16[2,4,64,1024]{3,2,1,0:T(8,128)(2,1)}, bf16[2,4,64,1024]{3,2,1,0:T(8,128)(2,1)}) custom-call(s32[3]{0:T(128)} %pad_add_fusion.coords, bf16[2048,1024]{1,0:T(8,128)(2,1)} %convolution_convert_fusion.refs_0_), custom_call_target="tpu_custom_call" | custom-call | tf_op jit(solution)/shard_map/pallas_call | solution.py:153
  756.6 7.0 convolution_convert_fusion.1.refs_0_
  766.1 5.8 fusion.100
  798.6 161.4 %shard_map.308 = (bf16[2,4,32,2560]{3,2,1,0:T(8,128)(2,1)}, bf16[2,4,32,2560]{3,2,1,0:T(8,128)(2,1)}, bf16[2,4,32,2560]{3,2,1,0:T(8,128)(2,1)}, bf16[2,4,32,2560]{3,2,1,0:T(8,128)(2,1)}) custom-call(s32[3]{0:T(128)} %pad_add_fusion.coords, bf16[1024,2048]{1,0:T(8,128)(2,1)} %convolution_convert_fusion.1.refs_0_, ...), custom_call_target="tpu_custom_call" | custom-call | tf_op jit(solution)/shard_map/pallas_call | solution.py:153
  968.9 5.9 fusion.28
  998.7 18.9 %collective-permute-done.52 = bf16[4,64,1024]{2,1,0:T(8,128)(2,1)} collective-permute-done((bf16[4,64,1024]{2,1,0:T(8,128)(2,1)}, bf16[4,64,1024]{2,1,0:T(8,128)(2,1)}, u32[]{:S(2)}, u32[]{:S(2)}) %collective-permute-start.52) | collective-permute-done | bytes 524320 | tf_op jit(solution)/shard_map/ppermute | solution.py:27
  1019.2 7.3 collective-permute-start.57
  1033.9 13.6 %collective-permute-done.56 = bf16[128,1024]{1,0:T(8,128)(2,1)S(1)} collective-permute-done((bf16[128,1024]{1,0:T(8,128)(2,1)S(1)}, bf16[128,1024]{1,0:T(8,128)(2,1)S(1)}, u32[]{:S(2)}, u32[]{:S(2)}) %collective-permute-start.56) | collective-permute-done | bytes 262176 | tf_op jit(solution)/shard_map/ppermute | solution.py:33
  1051.0 105.6 %shard_map.307 = (bf16[2,4,32,1664]{3,2,1,0:T(8,128)(2,1)}, bf16[2,4,32,1664]{3,2,1,0:T(8,128)(2,1)}, bf16[2,4,32,1664]{3,2,1,0:T(8,128)(2,1)}, bf16[2,4,32,1664]{3,2,1,0:T(8,128)(2,1)}) custom-call(s32[3]{0:T(128)} %pad_add_fusion.coords, bf16[1024,1536]{1,0:T(8,128)(2,1)} %convolution_convert_fusion.2.refs_0_, bf16[1024,128]{1,0:T(8,128)(2,1)} %concatenate.126.refs_1_), custom_call_target="tpu_custom_call" | custom-call | tf_op jit(solution)/shard_map/pallas_call | solution.py:153
  1167.5 23.7 %collective-permute-done.46 = bf16[4,32,2560]{2,1,0:T(8,128)(2,1)S(1)} collective-permute-done((bf16[4,32,2560]{2,1,0:T(8,128)(2,1)S(1)}, bf16[4,32,2560]{2,1,0:T(8,128)(2,1)S(1)}, u32[]{:S(2)}, u32[]{:S(2)}) %collective-permute-start.46) | collective-permute-done | bytes 655392 | tf_op jit(solution)/shard_map/ppermute | solution.py:27
  1202.9 22.3 %collective-permute-done.48 = bf16[64,2560]{1,0:T(8,128)(2,1)S(1)} collective-permute-done((bf16[64,2560]{1,0:T(8,128)(2,1)S(1)}, bf16[64,2560]{1,0:T(8,128)(2,1)S(1)}, u32[]{:S(2)}, u32[]{:S(2)}) %collective-permute-start.48) | collective-permute-done | bytes 327712 | tf_op jit(solution)/shard_map/ppermute | solution.py:33
  1230.1 5.4 collective-permute-done.41
  1235.5 10.2 collective-permute-done.40
  (442 shorter events, 255.4 us)
Async XLA Ops:
  7.6 49.8 %collective-permute-start.22 = (bf16[128,1024]{1,0:T(8,128)(2,1)}, bf16[128,1024]{1,0:T(8,128)(2,1)}, u32[]{:S(2)}, u32[]{:S(2)}) collective-permute-start(bf16[128,1024]{1,0:T(8,128)(2,1)} %convert_element_type.629), channel_id=1, source_target_pairs={{0,16},{8,24},{16,0},{24,8},{1,17},{9,25},{17,1},{25,9},{2,18},{10... | collective-permute-start | bytes 786440 | tf_op jit(solution)/shard_map/ppermute | solution.py:33
  11.0 39.7 %collective-permute-start.3 = (bf16[64,1664]{1,0:T(8,128)(2,1)S(1)}, bf16[64,1664]{1,0:T(8,128)(2,1)S(1)}, u32[]{:S(2)}, u32[]{:S(2)}) collective-permute-start(bf16[64,1664]{1,0:T(8,128)(2,1)S(1)} %get-tuple-element.220), channel_id=1, source_target_pairs={{0,16},{8,24},{16,0},{24,8},{1,17},{9,25},{17,1},{25,9},{2,18},{10... | collective-permute-start | bytes 638984 | tf_op jit(solution)/shard_map/ppermute | solution.py:33
  13.6 37.2 %collective-permute-start.2 = (bf16[64,1664]{1,0:T(8,128)(2,1)S(1)}, bf16[64,1664]{1,0:T(8,128)(2,1)S(1)}, u32[]{:S(2)}, u32[]{:S(2)}) collective-permute-start(bf16[64,1664]{1,0:T(8,128)(2,1)S(1)} %get-tuple-element.220), channel_id=1, source_target_pairs={{0,8},{8,16},{16,24},{24,0},{1,9},{9,17},{17,25},{25,1},{2,10},{10... | collective-permute-start | bytes 638984 | tf_op jit(solution)/shard_map/ppermute | solution.py:33
  16.3 41.2 %collective-permute-start.21 = (bf16[128,1024]{1,0:T(8,128)(2,1)}, bf16[128,1024]{1,0:T(8,128)(2,1)}, u32[]{:S(2)}, u32[]{:S(2)}) collective-permute-start(bf16[128,1024]{1,0:T(8,128)(2,1)} %convert_element_type.629), channel_id=1, source_target_pairs={{0,8},{8,16},{16,24},{24,0},{1,9},{9,17},{17,25},{25,1},{2,10},{10... | collective-permute-start | bytes 786440 | tf_op jit(solution)/shard_map/ppermute | solution.py:33
  78.7 181.7 %collective-permute-start.16 = (bf16[4,64,2560]{2,1,0:T(8,128)(2,1)}, bf16[4,64,2560]{2,1,0:T(8,128)(2,1)}, u32[]{:S(2)}, u32[]{:S(2)}) collective-permute-start(bf16[4,64,2560]{2,1,0:T(8,128)(2,1)} %pad_maximum_fusion.2.refs_0_), channel_id=1, source_target_pairs={{0,1},{1,0},{2,3},{3,2},{4,5},{5,4},{6,7},{7,6},{8,9},{9,8},{10,11... | collective-permute-start | bytes 3932168 | tf_op jit(solution)/shard_map/ppermute | solution.py:27
  80.2 177.7 %collective-permute-start.17 = (bf16[4,64,2560]{2,1,0:T(8,128)(2,1)}, bf16[4,64,2560]{2,1,0:T(8,128)(2,1)}, u32[]{:S(2)}, u32[]{:S(2)}) collective-permute-start(bf16[4,64,2560]{2,1,0:T(8,128)(2,1)} %pad_maximum_fusion.2.refs_0_), channel_id=1, source_target_pairs={{0,2},{2,0},{1,3},{3,1},{4,6},{6,4},{5,7},{7,5},{8,10},{10,8},{9,1... | collective-permute-start | bytes 3932168 | tf_op jit(solution)/shard_map/ppermute | solution.py:27
  82.0 35.6 %collective-permute-start.7 = (bf16[2,64,1664]{2,1,0:T(8,128)(2,1)S(1)}, bf16[2,64,1664]{2,1,0:T(8,128)(2,1)S(1)}, u32[]{:S(2)}, u32[]{:S(2)}) collective-permute-start(bf16[2,64,1664]{2,1,0:T(8,128)(2,1)S(1)} %slice.538), channel_id=1, source_target_pairs={{0,1},{1,0},{2,3},{3,2},{4,5},{5,4},{6,7},{7,6},{8,9},{9,8},{10,11... | collective-permute-start | bytes 1277960 | tf_op jit(solution)/shard_map/ppermute | solution.py:27
  83.6 35.3 %collective-permute-start.8 = (bf16[2,64,1664]{2,1,0:T(8,128)(2,1)S(1)}, bf16[2,64,1664]{2,1,0:T(8,128)(2,1)S(1)}, u32[]{:S(2)}, u32[]{:S(2)}) collective-permute-start(bf16[2,64,1664]{2,1,0:T(8,128)(2,1)S(1)} %slice.539), channel_id=1, source_target_pairs={{0,2},{2,0},{1,3},{3,1},{4,6},{6,4},{5,7},{7,5},{8,10},{10,8},{9,1... | collective-permute-start | bytes 1277960 | tf_op jit(solution)/shard_map/ppermute | solution.py:27
  254.8 205.2 %collective-permute-start.24 = (bf16[4,128,1024]{2,1,0:T(8,128)(2,1)}, bf16[4,128,1024]{2,1,0:T(8,128)(2,1)}, u32[]{:S(2)}, u32[]{:S(2)}) collective-permute-start(bf16[4,128,1024]{2,1,0:T(8,128)(2,1)} %pad_maximum_fusion.4.refs_0_), channel_id=1, source_target_pairs={{0,1},{1,0},{2,3},{3,2},{4,5},{5,4},{6,7},{7,6},{8,9},{9,8},{10,11... | collective-permute-start | bytes 3145736 | tf_op jit(solution)/shard_map/ppermute | solution.py:27
  256.3 201.3 %collective-permute-start.25 = (bf16[4,128,1024]{2,1,0:T(8,128)(2,1)}, bf16[4,128,1024]{2,1,0:T(8,128)(2,1)}, u32[]{:S(2)}, u32[]{:S(2)}) collective-permute-start(bf16[4,128,1024]{2,1,0:T(8,128)(2,1)} %pad_maximum_fusion.4.refs_0_), channel_id=1, source_target_pairs={{0,2},{2,0},{1,3},{3,1},{4,6},{6,4},{5,7},{7,5},{8,10},{10,8},{9,1... | collective-permute-start | bytes 3145736 | tf_op jit(solution)/shard_map/ppermute | solution.py:27
  457.0 147.7 %collective-permute-start.20 = (bf16[512,1024]{1,0:T(8,128)(2,1)}, bf16[512,1024]{1,0:T(8,128)(2,1)}, u32[]{:S(2)}, u32[]{:S(2)}) collective-permute-start(bf16[512,1024]{1,0:T(8,128)(2,1)} %get-tuple-element.237), channel_id=1, source_target_pairs={{0,4},{4,0},{1,5},{5,1},{2,6},{6,2},{3,7},{7,3},{8,12},{12,8},{9,1... | collective-permute-start | bytes 3145736 | tf_op jit(solution)/shard_map/ppermute | solution.py:27
  620.0 143.6 %collective-permute-start.30 = (bf16[512,1024]{1,0:T(8,128)(2,1)}, bf16[512,1024]{1,0:T(8,128)(2,1)}, u32[]{:S(2)}, u32[]{:S(2)}) collective-permute-start(bf16[512,1024]{1,0:T(8,128)(2,1)} %get-tuple-element.239), channel_id=1, source_target_pairs={{0,4},{4,0},{1,5},{5,1},{2,6},{6,2},{3,7},{7,3},{8,12},{12,8},{9,1... | collective-permute-start | bytes 3145736 | tf_op jit(solution)/shard_map/ppermute | solution.py:27
  753.5 208.6 %collective-permute-start.53 = (bf16[2,4,64,1024]{3,2,1,0:T(8,128)(2,1)}, bf16[2,4,64,1024]{3,2,1,0:T(8,128)(2,1)}, u32[]{:S(2)}, u32[]{:S(2)}) collective-permute-start(bf16[2,4,64,1024]{3,2,1,0:T(8,128)(2,1)} %get-tuple-element.49), channel_id=1, source_target_pairs={{0,2},{2,0},{1,3},{3,1},{4,6},{6,4},{5,7},{7,5},{8,10},{10,8},{9,1... | collective-permute-start | bytes 3145736 | tf_op jit(solution)/shard_map/ppermute | solution.py:27
  755.1 219.8 %collective-permute-start.51 = (bf16[2,4,64,1024]{3,2,1,0:T(8,128)(2,1)}, bf16[2,4,64,1024]{3,2,1,0:T(8,128)(2,1)}, u32[]{:S(2)}, u32[]{:S(2)}) collective-permute-start(bf16[2,4,64,1024]{3,2,1,0:T(8,128)(2,1)} %get-tuple-element.47), channel_id=1, source_target_pairs={{0,1},{1,0},{2,3},{3,2},{4,5},{5,4},{6,7},{7,6},{8,9},{9,8},{10,11... | collective-permute-start | bytes 3145736 | tf_op jit(solution)/shard_map/ppermute | solution.py:27
  783.2 194.2 %collective-permute-start.33 = (bf16[260,128]{1,0:T(8,128)(2,1)S(1)}, bf16[260,128]{1,0:T(8,128)(2,1)}, u32[]{:S(2)}, u32[]{:S(2)}) collective-permute-start(bf16[260,128]{1,0:T(8,128)(2,1)S(1)} %pad_maximum_fusion.21), channel_id=1, source_target_pairs={{24,0},{25,1},{26,2},{27,3},{28,4},{29,5},{30,6},{31,7}} | collective-permute-start | bytes 199688 | tf_op jit(solution)/shard_map/ppermute | solution.py:33
  784.5 193.6 %collective-permute-start.32 = (bf16[260,128]{1,0:T(8,128)(2,1)S(1)}, bf16[260,128]{1,0:T(8,128)(2,1)}, u32[]{:S(2)}, u32[]{:S(2)}) collective-permute-start(bf16[260,128]{1,0:T(8,128)(2,1)S(1)} %pad_maximum_fusion.21), channel_id=1, source_target_pairs={{16,0},{24,8},{17,1},{25,9},{18,2},{26,10},{19,3},{27,11},{20,4},{... | collective-permute-start | bytes 199688 | tf_op jit(solution)/shard_map/ppermute | solution.py:33
  785.8 193.8 %collective-permute-start.31 = (bf16[260,128]{1,0:T(8,128)(2,1)S(1)}, bf16[260,128]{1,0:T(8,128)(2,1)}, u32[]{:S(2)}, u32[]{:S(2)}) collective-permute-start(bf16[260,128]{1,0:T(8,128)(2,1)S(1)} %pad_maximum_fusion.21), channel_id=1, source_target_pairs={{8,0},{16,8},{24,16},{9,1},{17,9},{25,17},{10,2},{18,10},{26,18},{... | collective-permute-start | bytes 199688 | tf_op jit(solution)/shard_map/ppermute | solution.py:33
  962.1 64.4 %collective-permute-start.28 = (bf16[256,1024]{1,0:T(8,128)(2,1)}, bf16[256,1024]{1,0:T(8,128)(2,1)}, u32[]{:S(2)}, u32[]{:S(2)}) collective-permute-start(bf16[256,1024]{1,0:T(8,128)(2,1)} %fusion.31), channel_id=1, source_target_pairs={{0,4},{4,0},{1,5},{5,1},{2,6},{6,2},{3,7},{7,3},{8,12},{12,8},{9,1... | collective-permute-start | bytes 1572872 | tf_op jit(solution)/shard_map/ppermute | solution.py:27
  974.8 187.0 %collective-permute-start.45 = (bf16[2,4,32,2560]{3,2,1,0:T(8,128)(2,1)}, bf16[2,4,32,2560]{3,2,1,0:T(8,128)(2,1)}, u32[]{:S(2)}, u32[]{:S(2)}) collective-permute-start(bf16[2,4,32,2560]{3,2,1,0:T(8,128)(2,1)} %get-tuple-element.45), channel_id=1, source_target_pairs={{0,2},{2,0},{1,3},{3,1},{4,6},{6,4},{5,7},{7,5},{8,10},{10,8},{9,1... | collective-permute-start | bytes 3932168 | tf_op jit(solution)/shard_map/ppermute | solution.py:27
  978.1 39.5 %collective-permute-start.52 = (bf16[4,64,1024]{2,1,0:T(8,128)(2,1)}, bf16[4,64,1024]{2,1,0:T(8,128)(2,1)}, u32[]{:S(2)}, u32[]{:S(2)}) collective-permute-start(bf16[4,64,1024]{2,1,0:T(8,128)(2,1)} %fusion.42), channel_id=1, source_target_pairs={{0,2},{2,0},{1,3},{3,1},{4,6},{6,4},{5,7},{7,5},{8,10},{10,8},{9,1... | collective-permute-start | bytes 1572872 | tf_op jit(solution)/shard_map/ppermute | solution.py:27
  993.3 55.7 %collective-permute-start.34 = (bf16[512,1024]{1,0:T(8,128)(2,1)S(1)}, bf16[512,1024]{1,0:T(8,128)(2,1)S(1)}, u32[]{:S(2)}, u32[]{:S(2)}) collective-permute-start(bf16[512,1024]{1,0:T(8,128)(2,1)S(1)} %get-tuple-element.242), channel_id=1, source_target_pairs={{0,4},{4,0},{1,5},{5,1},{2,6},{6,2},{3,7},{7,3},{8,12},{12,8},{9,1... | collective-permute-start | bytes 3145736 | tf_op jit(solution)/shard_map/ppermute | solution.py:27
  1033.2 131.4 %collective-permute-start.43 = (bf16[2,4,32,2560]{3,2,1,0:T(8,128)(2,1)}, bf16[2,4,32,2560]{3,2,1,0:T(8,128)(2,1)}, u32[]{:S(2)}, u32[]{:S(2)}) collective-permute-start(bf16[2,4,32,2560]{3,2,1,0:T(8,128)(2,1)} %get-tuple-element.43), channel_id=1, source_target_pairs={{0,1},{1,0},{2,3},{3,2},{4,5},{5,4},{6,7},{7,6},{8,9},{9,8},{10,11... | collective-permute-start | bytes 3932168 | tf_op jit(solution)/shard_map/ppermute | solution.py:27
  1156.6 43.8 %collective-permute-start.37 = (bf16[2,4,32,1664]{3,2,1,0:T(8,128)(2,1)}, bf16[2,4,32,1664]{3,2,1,0:T(8,128)(2,1)S(1)}, u32[]{:S(2)}, u32[]{:S(2)}) collective-permute-start(bf16[2,4,32,1664]{3,2,1,0:T(8,128)(2,1)} %get-tuple-element.41), channel_id=1, source_target_pairs={{0,2},{2,0},{1,3},{3,1},{4,6},{6,4},{5,7},{7,5},{8,10},{10,8},{9,1... | collective-permute-start | bytes 2555912 | tf_op jit(solution)/shard_map/ppermute | solution.py:27
  1157.2 44.1 %collective-permute-start.35 = (bf16[2,4,32,1664]{3,2,1,0:T(8,128)(2,1)}, bf16[2,4,32,1664]{3,2,1,0:T(8,128)(2,1)S(1)}, u32[]{:S(2)}, u32[]{:S(2)}) collective-permute-start(bf16[2,4,32,1664]{3,2,1,0:T(8,128)(2,1)} %get-tuple-element.39), channel_id=1, source_target_pairs={{0,1},{1,0},{2,3},{3,2},{4,5},{5,4},{6,7},{7,6},{8,9},{9,8},{10,11... | collective-permute-start | bytes 2555912 | tf_op jit(solution)/shard_map/ppermute | solution.py:27
  (111 other events, 1167.0 us)

commit v2 on v1

--- a/solution.py
+++ b/solution.py
@@ -94,40 +94,29 @@
     return zz, yy * 2 + xx
 
 
-def run_copies(copies, sems):
-    started = [pltpu.make_async_copy(src, dst, sems.at[i]) for i, (src, dst) in enumerate(copies)]
-    for copy in started:
-        copy.start()
-    for copy in started:
-        copy.wait()
-
-
-def window(ref, lead, row, rows, col, cols):
+def window(row, rows, col, cols):
     rows_at = pl.ds(row if isinstance(row, int) else pl.multiple_of(row, 16), rows)
-    return ref.at[(*lead, rows_at, pl.ds(col, cols))]
+    return rows_at, pl.ds(col, cols)
+
+
+VMEM = pl.BlockSpec(memory_space=pltpu.VMEM)
+ROOM = pltpu.CompilerParams(vmem_limit_bytes=24 * 1024 * 1024)
 
 
 def place(parts, depth, outs, moves):
-    spots = gathered_places(depth)
-    count = len(spots) * len(moves(0, 0))
-
     def kernel(coords, *refs):
-        ins, out_refs, sems = refs[: len(parts)], refs[len(parts) : len(parts) + len(outs)], refs[-1]
-        copies = []
-        for array, slot, rel in spots:
+        ins, out_refs = refs[: len(parts)], refs[len(parts) :]
+        for array, slot, rel in gathered_places(depth):
             zz, plane = chip_of(coords, rel, depth, True)
             for o, sr, sc, rows, cols, tr, tc in moves(zz, plane):
-                copies.append(
-                    (window(ins[array], (slot,), sr, rows, sc, cols), window(out_refs[o], (), tr, rows, tc, cols))
-                )
-        run_copies(copies, sems)
+                out_refs[o][window(tr, rows, tc, cols)] = ins[array][(slot, *window(sr, rows, sc, cols))]
 
     return pl.pallas_call(
         kernel,
         out_shape=[jax.ShapeDtypeStruct(s, LOW) for s in outs],
-        in_specs=[pl.BlockSpec(memory_space=pltpu.SMEM)] + [pl.BlockSpec(memory_space=pl.ANY)] * len(parts),
-        out_specs=[pl.BlockSpec(memory_space=pl.ANY)] * len(outs),
-        scratch_shapes=[pltpu.SemaphoreType.DMA((count,))],
+        in_specs=[pl.BlockSpec(memory_space=pltpu.SMEM)] + [VMEM] * len(parts),
+        out_specs=[VMEM] * len(outs),
+        compiler_params=ROOM,
     )(coordinates(), *parts)
 
 
@@ -137,25 +126,20 @@
         for d in range(2):
             spots += [(0, d, dz, (dz, d, 1), 0), (1, d, dz, (dz, d, 0), 0)]
             spots += [(2, d, dz, (dz, 1, d), 1), (3, d, dz, (dz, 0, d), 1)]
-    count = len(spots) * len(moves(0, 0, 0))
 
     def kernel(coords, *refs):
-        ins, out_refs, sems = refs[: len(grads)], refs[len(grads) : len(grads) + 4], refs[-1]
-        copies = []
+        ins, out_refs = refs[: len(grads)], refs[len(grads) :]
         for array, d, dz, rel, half in spots:
             zz, plane = chip_of(coords, rel, depth, False)
             for i, sr, sc, rows, cols, tr, tc in moves(zz, plane, half):
-                copies.append(
-                    (window(ins[i], (), sr, rows, sc, cols), window(out_refs[array], (d, dz), tr, rows, tc, cols))
-                )
-        run_copies(copies, sems)
+                out_refs[array][(d, dz, *window(tr, rows, tc, cols))] = ins[i][window(sr, rows, sc, cols)]
 
     return pl.pallas_call(
         kernel,
         out_shape=[jax.ShapeDtypeStruct((2, depth) + rows_cols, LOW)] * 4,
-        in_specs=[pl.BlockSpec(memory_space=pltpu.SMEM)] + [pl.BlockSpec(memory_space=pl.ANY)] * len(grads),
-        out_specs=[pl.BlockSpec(memory_space=pl.ANY)] * 4,
-        scratch_shapes=[pltpu.SemaphoreType.DMA((count,))],
+        in_specs=[pl.BlockSpec(memory_space=pltpu.SMEM)] + [VMEM] * len(grads),
+        out_specs=[VMEM] * 4,
+        compiler_params=ROOM,
     )(coordinates(), *grads)
 
 

time: 1300 us -> 522 us (0.40)
  Pallas kernels: 792 us -> 9.68 us
    pallas_call x3, Pallas kernels: 396 us -> 4.95 us  [unplace(): pl.pallas_call(kernel, out_shape=[jax.ShapeDtypeStruct((2, depth) + rows_...]
    pallas_call x3, Pallas kernels: 396 us -> 4.73 us  [place(): pl.pallas_call(kernel, out_shape=[jax.ShapeDtypeStruct(s, LOW) for s in o...]
  transfers between devices with their start and end apart: 65 -> 65, of which waited for: 20 -> 22; matrix products, arithmetic and copies ran while one was open for 11% -> 27% of each run, Pallas kernels for 61% -> 2%
where the time goes in v2:
time: 522 us; the launch traced here: 513 us
  waiting for transfers between devices  220 us (42%)
  starting transfers between devices  91.3 us (17%)
  other arithmetic  68 us (13%)
  matrix products  64.2 us (12%)
  local copies, waits for them, and re-layouts  52.8 us (10%)
  Pallas kernels  9.68 us (2%)
  between operations  7.58 us (1%)
    ppermute x37, waiting for transfers between devices, swap(): return lax.ppermute(value, axis, SWAP)  121 us
    ppermute x27, waiting for transfers between devices, shift(): return lax.ppermute(value, 'z', pairs)  98.5 us
    ppermute x27, starting transfers between devices, shift(): return lax.ppermute(value, 'z', pairs)  61.7 us
    dot_general x13, matrix products, mul(): return jnp.einsum(spec, left, right, preferred_element_type=WIDE)  28.4 us
    ppermute x37, starting transfers between devices, swap(): return lax.ppermute(value, axis, SWAP)  28.2 us
    unnamed x192, local copies, waits for them, and re-layouts  17.1 us
    dot_general x4, matrix products, dot_rows(): lax.dot_general(left, right, (((0,), (0,)), ((), ())), preferred_element_...  13.7 us
    dot_general x4, matrix products, dot(): return jnp.dot(left, right, preferred_element_type=WIDE)  11.5 us
  transfers between devices with their start and end apart: 65, of which 22 were waited for; matrix products, arithmetic and copies ran while one was open for 27% of the time, Pallas kernels for 2%

profile of v2, /device:TPU:0, one launch (start us, length us, event | category | flops | bytes accessed | tf_op | source)
XLA Modules:
  0.0 513.3 jit_solution(2954682781193542847)
XLA Ops:
  1.8 5.1 collective-permute-start.23
  18.6 5.2 %collective-permute-done.4 = bf16[64,1664]{1,0:T(8,128)(2,1)S(1)} collective-permute-done((bf16[64,1664]{1,0:T(8,128)(2,1)S(1)}, bf16[64,1664]{1,0:T(8,128)(2,1)S(1)}, u32[]{:S(2)}, u32[]{:S(2)}) %collective-permute-start.4) | collective-permute-done | bytes 213024 | tf_op jit(solution)/shard_map/ppermute | solution.py:33
  23.9 4.3 collective-permute-start.15
  28.3 21.9 %collective-permute-done.3 = bf16[64,1664]{1,0:T(8,128)(2,1)} collective-permute-done((bf16[64,1664]{1,0:T(8,128)(2,1)S(1)}, bf16[64,1664]{1,0:T(8,128)(2,1)}, u32[]{:S(2)}, u32[]{:S(2)}) %collective-permute-start.3) | collective-permute-done | bytes 213024 | tf_op jit(solution)/shard_map/ppermute | solution.py:33
  50.2 6.2 %collective-permute-start.13 = (bf16[64,2560]{1,0:T(8,128)(2,1)S(1)}, bf16[64,2560]{1,0:T(8,128)(2,1)S(1)}, u32[]{:S(2)}, u32[]{:S(2)}) collective-permute-start(bf16[64,2560]{1,0:T(8,128)(2,1)S(1)} %get-tuple-element.212), channel_id=1, source_target_pairs={{0,8},{8,16},{16,24},{24,0},{1,9},{9,17},{17,25},{25,1},{2,10},{10... | collective-permute-start | bytes 983048 | tf_op jit(solution)/shard_map/ppermute | solution.py:33
  62.0 13.6 %collective-permute-done.14 = bf16[64,2560]{1,0:T(8,128)(2,1)S(1)} collective-permute-done((bf16[64,2560]{1,0:T(8,128)(2,1)S(1)}, bf16[64,2560]{1,0:T(8,128)(2,1)S(1)}, u32[]{:S(2)}, u32[]{:S(2)}) %collective-permute-start.14) | collective-permute-done | bytes 327712 | tf_op jit(solution)/shard_map/ppermute | solution.py:33
  83.4 32.8 %collective-permute-done.7.refs_3_ = bf16[2,64,1664]{2,1,0:T(8,128)(2,1)S(1)} collective-permute-done((bf16[2,64,1664]{2,1,0:T(8,128)(2,1)S(1)}, bf16[2,64,1664]{2,1,0:T(8,128)(2,1)S(1)}, u32[]{:S(2)}, u32[]{:S(2)}) %collective-permute-start.7) | collective-permute-done | bytes 426016 | tf_op jit(solution)/shard_map/ppermute | solution.py:27
  133.3 9.6 %collective-permute-start.10 = (bf16[260,128]{1,0:T(8,128)(2,1)S(1)}, bf16[260,128]{1,0:T(8,128)(2,1)}, u32[]{:S(2)}, u32[]{:S(2)}) collective-permute-start(bf16[260,128]{1,0:T(8,128)(2,1)S(1)} %pad_maximum_fusion.20), channel_id=1, source_target_pairs={{0,16},{8,24},{1,17},{9,25},{2,18},{10,26},{3,19},{11,27},{4,20},{... | collective-permute-start | bytes 199688 | tf_op jit(solution)/shard_map/ppermute | solution.py:33
  170.9 20.3 %collective-permute-done.18.refs_3_ = bf16[2,64,2560]{2,1,0:T(8,128)(2,1)} collective-permute-done((bf16[2,64,2560]{2,1,0:T(8,128)(2,1)}, bf16[2,64,2560]{2,1,0:T(8,128)(2,1)}, u32[]{:S(2)}, u32[]{:S(2)}) %collective-permute-start.18) | collective-permute-done | bytes 655392 | tf_op jit(solution)/shard_map/ppermute | solution.py:27
  208.9 7.1 %collective-permute-done.26.refs_3_ = bf16[2,128,1024]{2,1,0:T(8,128)(2,1)S(1)} collective-permute-done((bf16[2,128,1024]{2,1,0:T(8,128)(2,1)}, bf16[2,128,1024]{2,1,0:T(8,128)(2,1)S(1)}, u32[]{:S(2)}, u32[]{:S(2)}) %collective-permute-start.26) | collective-permute-done | bytes 524320 | tf_op jit(solution)/shard_map/ppermute | solution.py:27
  223.9 5.6 %fusion.6 = bf16[512,2048]{1,0:T(8,128)(2,1)S(1)} fusion(f32[512,2048]{1,0:T(8,128)S(1)} %fusion.90, bf16[2048,1024]{1,0:T(8,128)(2,1)S(1)} %shard_map.306, bf16[256,1024]{1,0:T(8,128)(2,1)S(1)} %get-tuple-element.201, bf16[256,1024]{1,0:T(8,128)(2,1)S(1)} %get-tuple-element.200), kind=kOutput, calls=%fused_computation.11 | convolution fusion | flops 2170552320 | bytes 11534336 | tf_op jit(solution)/shard_map/dot_general | solution.py:169
  239.7 4.7 convolution_convert_fusion.1.refs_0_
  245.4 4.6 fusion.100
  287.7 6.0 %fusion.28 = f32[8,64,512]{2,1,0:T(8,128)} fusion(bf16[512,8,64]{0,2,1:T(8,128)(2,1)S(1)} %copy-done.35, f32[8,512,512]{1,2,0:T(8,128)} %copy-done.15, f32[512,512]{0,1:T(8,128)S(1)} %copy-done.19), kind=kOutput, calls=%fused_computation.65 | convolution fusion | flops 272629760 | bytes 11010048 | tf_op jit(solution)/shard_map/hts,thf->shf/dot_general | solution.py:173
  308.9 3.9 convolution_convert_fusion.2.refs_0_
  314.5 22.1 %collective-permute-done.52 = bf16[4,64,1024]{2,1,0:T(8,128)(2,1)} collective-permute-done((bf16[4,64,1024]{2,1,0:T(8,128)(2,1)}, bf16[4,64,1024]{2,1,0:T(8,128)(2,1)}, u32[]{:S(2)}, u32[]{:S(2)}) %collective-permute-start.52) | collective-permute-done | bytes 524320 | tf_op jit(solution)/shard_map/ppermute | solution.py:27
  338.1 6.9 %collective-permute-start.57 = (bf16[128,1024]{1,0:T(8,128)(2,1)S(1)}, bf16[128,1024]{1,0:T(8,128)(2,1)S(1)}, u32[]{:S(2)}, u32[]{:S(2)}) collective-permute-start(bf16[128,1024]{1,0:T(8,128)(2,1)S(1)} %pad_maximum_fusion.14), channel_id=1, source_target_pairs={{0,24},{8,0},{16,8},{24,16},{1,25},{9,1},{17,9},{25,17},{2,26},{10... | collective-permute-start | bytes 786440 | tf_op jit(solution)/shard_map/ppermute | solution.py:33
  352.3 13.7 %collective-permute-done.56 = bf16[128,1024]{1,0:T(8,128)(2,1)S(1)} collective-permute-done((bf16[128,1024]{1,0:T(8,128)(2,1)S(1)}, bf16[128,1024]{1,0:T(8,128)(2,1)S(1)}, u32[]{:S(2)}, u32[]{:S(2)}) %collective-permute-start.56) | collective-permute-done | bytes 262176 | tf_op jit(solution)/shard_map/ppermute | solution.py:33
  376.6 7.2 %collective-permute-done.43 = bf16[2,4,32,2560]{3,2,1,0:T(8,128)(2,1)} collective-permute-done((bf16[2,4,32,2560]{3,2,1,0:T(8,128)(2,1)}, bf16[2,4,32,2560]{3,2,1,0:T(8,128)(2,1)}, u32[]{:S(2)}, u32[]{:S(2)}) %collective-permute-start.43) | collective-permute-done | bytes 1310752 | tf_op jit(solution)/shard_map/ppermute | solution.py:27
  385.6 27.0 %collective-permute-done.46 = bf16[4,32,2560]{2,1,0:T(8,128)(2,1)S(1)} collective-permute-done((bf16[4,32,2560]{2,1,0:T(8,128)(2,1)S(1)}, bf16[4,32,2560]{2,1,0:T(8,128)(2,1)S(1)}, u32[]{:S(2)}, u32[]{:S(2)}) %collective-permute-start.46) | collective-permute-done | bytes 655392 | tf_op jit(solution)/shard_map/ppermute | solution.py:27
  415.4 4.3 collective-permute-start.49
  421.9 6.0 %collective-permute-done.49 = bf16[64,2560]{1,0:T(8,128)(2,1)S(1)} collective-permute-done((bf16[64,2560]{1,0:T(8,128)(2,1)S(1)}, bf16[64,2560]{1,0:T(8,128)(2,1)S(1)}, u32[]{:S(2)}, u32[]{:S(2)}) %collective-permute-start.49) | collective-permute-done | bytes 327712 | tf_op jit(solution)/shard_map/ppermute | solution.py:33
  427.9 16.1 %collective-permute-done.48 = bf16[64,2560]{1,0:T(8,128)(2,1)S(1)} collective-permute-done((bf16[64,2560]{1,0:T(8,128)(2,1)S(1)}, bf16[64,2560]{1,0:T(8,128)(2,1)S(1)}, u32[]{:S(2)}, u32[]{:S(2)}) %collective-permute-start.48) | collective-permute-done | bytes 327712 | tf_op jit(solution)/shard_map/ppermute | solution.py:33
  454.7 15.1 %collective-permute-done.40 = bf16[64,1664]{1,0:T(8,128)(2,1)} collective-permute-done((bf16[64,1664]{1,0:T(8,128)(2,1)}, bf16[64,1664]{1,0:T(8,128)(2,1)}, u32[]{:S(2)}, u32[]{:S(2)}) %collective-permute-start.40) | collective-permute-done | bytes 213024 | tf_op jit(solution)/shard_map/ppermute | solution.py:33
  (484 shorter events, 236.4 us)
Async XLA Ops:
  6.9 50.6 %collective-permute-start.22 = (bf16[128,1024]{1,0:T(8,128)(2,1)S(1)}, bf16[128,1024]{1,0:T(8,128)(2,1)}, u32[]{:S(2)}, u32[]{:S(2)}) collective-permute-start(bf16[128,1024]{1,0:T(8,128)(2,1)S(1)} %convert_element_type.629), channel_id=1, source_target_pairs={{0,16},{8,24},{16,0},{24,8},{1,17},{9,25},{17,1},{25,9},{2,18},{10... | collective-permute-start | bytes 786440 | tf_op jit(solution)/shard_map/ppermute | solution.py:33
  10.9 39.3 %collective-permute-start.3 = (bf16[64,1664]{1,0:T(8,128)(2,1)S(1)}, bf16[64,1664]{1,0:T(8,128)(2,1)}, u32[]{:S(2)}, u32[]{:S(2)}) collective-permute-start(bf16[64,1664]{1,0:T(8,128)(2,1)S(1)} %get-tuple-element.220), channel_id=1, source_target_pairs={{0,16},{8,24},{16,0},{24,8},{1,17},{9,25},{17,1},{25,9},{2,18},{10... | collective-permute-start | bytes 638984 | tf_op jit(solution)/shard_map/ppermute | solution.py:33
  13.5 36.7 %collective-permute-start.2 = (bf16[64,1664]{1,0:T(8,128)(2,1)S(1)}, bf16[64,1664]{1,0:T(8,128)(2,1)}, u32[]{:S(2)}, u32[]{:S(2)}) collective-permute-start(bf16[64,1664]{1,0:T(8,128)(2,1)S(1)} %get-tuple-element.220), channel_id=1, source_target_pairs={{0,8},{8,16},{16,24},{24,0},{1,9},{9,17},{17,25},{25,1},{2,10},{10... | collective-permute-start | bytes 638984 | tf_op jit(solution)/shard_map/ppermute | solution.py:33
  16.3 41.4 %collective-permute-start.21 = (bf16[128,1024]{1,0:T(8,128)(2,1)S(1)}, bf16[128,1024]{1,0:T(8,128)(2,1)S(1)}, u32[]{:S(2)}, u32[]{:S(2)}) collective-permute-start(bf16[128,1024]{1,0:T(8,128)(2,1)S(1)} %convert_element_type.629), channel_id=1, source_target_pairs={{0,8},{8,16},{16,24},{24,0},{1,9},{9,17},{17,25},{25,1},{2,10},{10... | collective-permute-start | bytes 786440 | tf_op jit(solution)/shard_map/ppermute | solution.py:33
  23.9 35.4 %collective-permute-start.15 = (bf16[64,2560]{1,0:T(8,128)(2,1)S(1)}, bf16[64,2560]{1,0:T(8,128)(2,1)S(1)}, u32[]{:S(2)}, u32[]{:S(2)}) collective-permute-start(bf16[64,2560]{1,0:T(8,128)(2,1)S(1)} %get-tuple-element.212), channel_id=1, source_target_pairs={{0,24},{8,0},{16,8},{24,16},{1,25},{9,1},{17,9},{25,17},{2,26},{10... | collective-permute-start | bytes 983048 | tf_op jit(solution)/shard_map/ppermute | solution.py:33
  76.9 86.4 %collective-permute-start.16 = (bf16[4,64,2560]{2,1,0:T(8,128)(2,1)S(1)}, bf16[4,64,2560]{2,1,0:T(8,128)(2,1)}, u32[]{:S(2)}, u32[]{:S(2)}) collective-permute-start(bf16[4,64,2560]{2,1,0:T(8,128)(2,1)S(1)} %pad_maximum_fusion.2.refs_0_), channel_id=1, source_target_pairs={{0,1},{1,0},{2,3},{3,2},{4,5},{5,4},{6,7},{7,6},{8,9},{9,8},{10,11... | collective-permute-start | bytes 3932168 | tf_op jit(solution)/shard_map/ppermute | solution.py:27
  78.4 82.3 %collective-permute-start.17 = (bf16[4,64,2560]{2,1,0:T(8,128)(2,1)S(1)}, bf16[4,64,2560]{2,1,0:T(8,128)(2,1)}, u32[]{:S(2)}, u32[]{:S(2)}) collective-permute-start(bf16[4,64,2560]{2,1,0:T(8,128)(2,1)S(1)} %pad_maximum_fusion.2.refs_0_), channel_id=1, source_target_pairs={{0,2},{2,0},{1,3},{3,1},{4,6},{6,4},{5,7},{7,5},{8,10},{10,8},{9,1... | collective-permute-start | bytes 3932168 | tf_op jit(solution)/shard_map/ppermute | solution.py:27
  81.3 34.9 %collective-permute-start.7 = (bf16[2,64,1664]{2,1,0:T(8,128)(2,1)S(1)}, bf16[2,64,1664]{2,1,0:T(8,128)(2,1)S(1)}, u32[]{:S(2)}, u32[]{:S(2)}) collective-permute-start(bf16[2,64,1664]{2,1,0:T(8,128)(2,1)S(1)} %slice.538), channel_id=1, source_target_pairs={{0,1},{1,0},{2,3},{3,2},{4,5},{5,4},{6,7},{7,6},{8,9},{9,8},{10,11... | collective-permute-start | bytes 1277960 | tf_op jit(solution)/shard_map/ppermute | solution.py:27
  82.0 35.5 %collective-permute-start.8 = (bf16[2,64,1664]{2,1,0:T(8,128)(2,1)S(1)}, bf16[2,64,1664]{2,1,0:T(8,128)(2,1)S(1)}, u32[]{:S(2)}, u32[]{:S(2)}) collective-permute-start(bf16[2,64,1664]{2,1,0:T(8,128)(2,1)S(1)} %slice.539), channel_id=1, source_target_pairs={{0,2},{2,0},{1,3},{3,1},{4,6},{6,4},{5,7},{7,5},{8,10},{10,8},{9,1... | collective-permute-start | bytes 1277960 | tf_op jit(solution)/shard_map/ppermute | solution.py:27
  155.3 47.1 %collective-permute-start.24 = (bf16[4,128,1024]{2,1,0:T(8,128)(2,1)S(1)}, bf16[4,128,1024]{2,1,0:T(8,128)(2,1)S(1)}, u32[]{:S(2)}, u32[]{:S(2)}) collective-permute-start(bf16[4,128,1024]{2,1,0:T(8,128)(2,1)S(1)} %pad_maximum_fusion.4.refs_0_), channel_id=1, source_target_pairs={{0,1},{1,0},{2,3},{3,2},{4,5},{5,4},{6,7},{7,6},{8,9},{9,8},{10,11... | collective-permute-start | bytes 3145736 | tf_op jit(solution)/shard_map/ppermute | solution.py:27
  156.8 43.2 %collective-permute-start.25 = (bf16[4,128,1024]{2,1,0:T(8,128)(2,1)S(1)}, bf16[4,128,1024]{2,1,0:T(8,128)(2,1)}, u32[]{:S(2)}, u32[]{:S(2)}) collective-permute-start(bf16[4,128,1024]{2,1,0:T(8,128)(2,1)S(1)} %pad_maximum_fusion.4.refs_0_), channel_id=1, source_target_pairs={{0,2},{2,0},{1,3},{3,1},{4,6},{6,4},{5,7},{7,5},{8,10},{10,8},{9,1... | collective-permute-start | bytes 3145736 | tf_op jit(solution)/shard_map/ppermute | solution.py:27
  236.7 46.6 %collective-permute-start.53 = (bf16[2,4,64,1024]{3,2,1,0:T(8,128)(2,1)}, bf16[2,4,64,1024]{3,2,1,0:T(8,128)(2,1)}, u32[]{:S(2)}, u32[]{:S(2)}) collective-permute-start(bf16[2,4,64,1024]{3,2,1,0:T(8,128)(2,1)} %get-tuple-element.49), channel_id=1, source_target_pairs={{0,2},{2,0},{1,3},{3,1},{4,6},{6,4},{5,7},{7,5},{8,10},{10,8},{9,1... | collective-permute-start | bytes 3145736 | tf_op jit(solution)/shard_map/ppermute | solution.py:27
  238.2 55.5 %collective-permute-start.51 = (bf16[2,4,64,1024]{3,2,1,0:T(8,128)(2,1)S(1)}, bf16[2,4,64,1024]{3,2,1,0:T(8,128)(2,1)}, u32[]{:S(2)}, u32[]{:S(2)}) collective-permute-start(bf16[2,4,64,1024]{3,2,1,0:T(8,128)(2,1)S(1)} %get-tuple-element.47), channel_id=1, source_target_pairs={{0,1},{1,0},{2,3},{3,2},{4,5},{5,4},{6,7},{7,6},{8,9},{9,8},{10,11... | collective-permute-start | bytes 3145736 | tf_op jit(solution)/shard_map/ppermute | solution.py:27
  261.5 34.8 %collective-permute-start.33 = (bf16[260,128]{1,0:T(8,128)(2,1)S(1)}, bf16[260,128]{1,0:T(8,128)(2,1)S(1)}, u32[]{:S(2)}, u32[]{:S(2)}) collective-permute-start(bf16[260,128]{1,0:T(8,128)(2,1)S(1)} %pad_maximum_fusion.21), channel_id=1, source_target_pairs={{24,0},{25,1},{26,2},{27,3},{28,4},{29,5},{30,6},{31,7}} | collective-permute-start | bytes 199688 | tf_op jit(solution)/shard_map/ppermute | solution.py:33
  262.8 34.1 %collective-permute-start.32 = (bf16[260,128]{1,0:T(8,128)(2,1)S(1)}, bf16[260,128]{1,0:T(8,128)(2,1)}, u32[]{:S(2)}, u32[]{:S(2)}) collective-permute-start(bf16[260,128]{1,0:T(8,128)(2,1)S(1)} %pad_maximum_fusion.21), channel_id=1, source_target_pairs={{16,0},{24,8},{17,1},{25,9},{18,2},{26,10},{19,3},{27,11},{20,4},{... | collective-permute-start | bytes 199688 | tf_op jit(solution)/shard_map/ppermute | solution.py:33
  264.1 34.3 %collective-permute-start.31 = (bf16[260,128]{1,0:T(8,128)(2,1)S(1)}, bf16[260,128]{1,0:T(8,128)(2,1)}, u32[]{:S(2)}, u32[]{:S(2)}) collective-permute-start(bf16[260,128]{1,0:T(8,128)(2,1)S(1)} %pad_maximum_fusion.21), channel_id=1, source_target_pairs={{8,0},{16,8},{24,16},{9,1},{17,9},{25,17},{10,2},{18,10},{26,18},{... | collective-permute-start | bytes 199688 | tf_op jit(solution)/shard_map/ppermute | solution.py:33
  283.3 61.8 %collective-permute-start.28 = (bf16[256,1024]{1,0:T(8,128)(2,1)}, bf16[256,1024]{1,0:T(8,128)(2,1)}, u32[]{:S(2)}, u32[]{:S(2)}) collective-permute-start(bf16[256,1024]{1,0:T(8,128)(2,1)} %fusion.31), channel_id=1, source_target_pairs={{0,4},{4,0},{1,5},{5,1},{2,6},{6,2},{3,7},{7,3},{8,12},{12,8},{9,1... | collective-permute-start | bytes 1572872 | tf_op jit(solution)/shard_map/ppermute | solution.py:27
  293.7 80.0 %collective-permute-start.45 = (bf16[2,4,32,2560]{3,2,1,0:T(8,128)(2,1)}, bf16[2,4,32,2560]{3,2,1,0:T(8,128)(2,1)}, u32[]{:S(2)}, u32[]{:S(2)}) collective-permute-start(bf16[2,4,32,2560]{3,2,1,0:T(8,128)(2,1)} %get-tuple-element.45), channel_id=1, source_target_pairs={{0,2},{2,0},{1,3},{3,1},{4,6},{6,4},{5,7},{7,5},{8,10},{10,8},{9,1... | collective-permute-start | bytes 3932168 | tf_op jit(solution)/shard_map/ppermute | solution.py:27
  296.9 39.6 %collective-permute-start.52 = (bf16[4,64,1024]{2,1,0:T(8,128)(2,1)}, bf16[4,64,1024]{2,1,0:T(8,128)(2,1)}, u32[]{:S(2)}, u32[]{:S(2)}) collective-permute-start(bf16[4,64,1024]{2,1,0:T(8,128)(2,1)} %fusion.42), channel_id=1, source_target_pairs={{0,2},{2,0},{1,3},{3,1},{4,6},{6,4},{5,7},{7,5},{8,10},{10,8},{9,1... | collective-permute-start | bytes 1572872 | tf_op jit(solution)/shard_map/ppermute | solution.py:27
  308.7 58.8 %collective-permute-start.34 = (bf16[512,1024]{1,0:T(8,128)(2,1)S(1)}, bf16[512,1024]{1,0:T(8,128)(2,1)S(1)}, u32[]{:S(2)}, u32[]{:S(2)}) collective-permute-start(bf16[512,1024]{1,0:T(8,128)(2,1)S(1)} %get-tuple-element.242), channel_id=1, source_target_pairs={{0,4},{4,0},{1,5},{5,1},{2,6},{6,2},{3,7},{7,3},{8,12},{12,8},{9,1... | collective-permute-start | bytes 3145736 | tf_op jit(solution)/shard_map/ppermute | solution.py:27
  351.8 32.0 %collective-permute-start.43 = (bf16[2,4,32,2560]{3,2,1,0:T(8,128)(2,1)}, bf16[2,4,32,2560]{3,2,1,0:T(8,128)(2,1)}, u32[]{:S(2)}, u32[]{:S(2)}) collective-permute-start(bf16[2,4,32,2560]{3,2,1,0:T(8,128)(2,1)} %get-tuple-element.43), channel_id=1, source_target_pairs={{0,1},{1,0},{2,3},{3,2},{4,5},{5,4},{6,7},{7,6},{8,9},{9,8},{10,11... | collective-permute-start | bytes 3932168 | tf_op jit(solution)/shard_map/ppermute | solution.py:27
  369.7 50.8 %collective-permute-start.37 = (bf16[2,4,32,1664]{3,2,1,0:T(8,128)(2,1)S(1)}, bf16[2,4,32,1664]{3,2,1,0:T(8,128)(2,1)S(1)}, u32[]{:S(2)}, u32[]{:S(2)}) collective-permute-start(bf16[2,4,32,1664]{3,2,1,0:T(8,128)(2,1)S(1)} %get-tuple-element.41), channel_id=1, source_target_pairs={{0,2},{2,0},{1,3},{3,1},{4,6},{6,4},{5,7},{7,5},{8,10},{10,8},{9,1... | collective-permute-start | bytes 2555912 | tf_op jit(solution)/shard_map/ppermute | solution.py:27
  370.2 51.0 %collective-permute-start.35 = (bf16[2,4,32,1664]{3,2,1,0:T(8,128)(2,1)S(1)}, bf16[2,4,32,1664]{3,2,1,0:T(8,128)(2,1)S(1)}, u32[]{:S(2)}, u32[]{:S(2)}) collective-permute-start(bf16[2,4,32,1664]{3,2,1,0:T(8,128)(2,1)S(1)} %get-tuple-element.39), channel_id=1, source_target_pairs={{0,1},{1,0},{2,3},{3,2},{4,5},{5,4},{6,7},{7,6},{8,9},{9,8},{10,11... | collective-permute-start | bytes 2555912 | tf_op jit(solution)/shard_map/ppermute | solution.py:27
  375.0 37.5 %collective-permute-start.46 = (bf16[4,32,2560]{2,1,0:T(8,128)(2,1)S(1)}, bf16[4,32,2560]{2,1,0:T(8,128)(2,1)S(1)}, u32[]{:S(2)}, u32[]{:S(2)}) collective-permute-start(bf16[4,32,2560]{2,1,0:T(8,128)(2,1)S(1)} %fusion.37), channel_id=1, source_target_pairs={{0,1},{1,0},{2,3},{3,2},{4,5},{5,4},{6,7},{7,6},{8,9},{9,8},{10,11... | collective-permute-start | bytes 1966088 | tf_op jit(solution)/shard_map/ppermute | solution.py:27
  (132 other events, 1626.5 us)

commit v3 on v2

--- a/solution.py
+++ b/solution.py
@@ -46,26 +46,51 @@
     return jnp.concatenate([jnp.where(first, own, mate), jnp.where(first, mate, own)], axis)
 
 
-def gather_chips(shard):
-    column = jnp.stack([shard] + [shift(shard, k) for k in range(1, lax.axis_size("z"))])
+def after(value, *before):
+    return lax.optimization_barrier((value, *before))[0]
+
+
+def column_first(shard):
+    return [shard] + [shift(shard, k) for k in range(1, lax.axis_size("z"))]
+
+
+def plane_last(column):
     half = column.shape[0] // 2
     along_x, along_y = swap(column, "x"), swap(column, "y")
     far = (swap(along_y[:half], "x"), swap(along_x[half:], "y"))
     return (column, along_x, along_y) + far
 
 
-def gathered_places(depth):
+def plane_first(shard):
+    half = shard.shape[0] // 2
+    along_x, along_y = swap(shard, "x"), swap(shard, "y")
+    far_low, far_high = swap(along_y[:half], "x"), swap(along_x[half:], "y")
+    return jnp.concatenate([shard, along_x, along_y, far_low, far_high])
+
+
+def column_last(plane):
+    parts = [plane]
+    for _ in range(1, lax.axis_size("z")):
+        parts.append(shift(parts[-1], 1))
+    return parts
+
+
+def column_first_spots(depth):
     half = depth // 2
-    places = [(0, k, (k, 0, 0)) for k in range(depth)]
-    places += [(1, k, (k, 0, 1)) for k in range(depth)]
-    places += [(2, k, (k, 1, 0)) for k in range(depth)]
-    places += [(3, k, (k, 1, 1)) for k in range(half)]
-    places += [(4, k - half, (k, 1, 1)) for k in range(half, depth)]
-    return places
-
-
-def reduce_chips(send_x, keep_x, send_y, keep_y):
+    spots = [(0, (k,), 0, (k, 0, 0)) for k in range(depth)]
+    spots += [(1, (k,), 0, (k, 0, 1)) for k in range(depth)]
+    spots += [(2, (k,), 0, (k, 1, 0)) for k in range(depth)]
+    spots += [(3, (k,), 0, (k, 1, 1)) for k in range(half)]
+    return spots + [(4, (k - half,), 0, (k, 1, 1)) for k in range(half, depth)]
+
+
+def plane_first_spots(depth, rows):
+    return [(k, (), p * rows, (k, p // 2, p % 2)) for k in range(depth) for p in range(4)]
+
+
+def reduce_chips(send_x, keep_x, send_y, keep_y, gate=()):
     depth = send_x.shape[1]
+    send_x, send_y = after(send_x, *gate), after(send_y, *gate)
     got_x, got_y = swap(send_x, "x"), swap(send_y, "y")
     wide = lambda a: a.astype(WIDE)
     on_y = swap((wide(keep_x[1]) + wide(got_x[1])).astype(LOW), "y")
@@ -78,11 +103,11 @@
     total = parts[0]
     for k in range(1, depth):
         total = total + wide(shift(parts[k].astype(LOW), k))
-    return total
+    return total, (on_x, on_y)
 
 
 def coordinates():
-    return jnp.stack([lax.axis_index("z"), lax.axis_index("y"), lax.axis_index("x")]).astype(jnp.int32)
+    return jnp.stack([lax.axis_index(name) for name in ("z", "y", "x", "c")]).astype(jnp.int32)
 
 
 def chip_of(coords, rel, depth, back):
@@ -103,13 +128,13 @@
 ROOM = pltpu.CompilerParams(vmem_limit_bytes=24 * 1024 * 1024)
 
 
-def place(parts, depth, outs, moves):
+def place(parts, depth, outs, spots, moves):
     def kernel(coords, *refs):
         ins, out_refs = refs[: len(parts)], refs[len(parts) :]
-        for array, slot, rel in gathered_places(depth):
+        for array, lead, base, rel in spots:
             zz, plane = chip_of(coords, rel, depth, True)
             for o, sr, sc, rows, cols, tr, tc in moves(zz, plane):
-                out_refs[o][window(tr, rows, tc, cols)] = ins[array][(slot, *window(sr, rows, sc, cols))]
+                out_refs[o][window(tr, rows, tc, cols)] = ins[array][(*lead, *window(base + sr, rows, sc, cols))]
 
     return pl.pallas_call(
         kernel,
@@ -141,6 +166,83 @@
         out_specs=[VMEM] * 4,
         compiler_params=ROOM,
     )(coordinates(), *grads)
+
+
+def cast_qkv(qkv, norm, halves):
+    rows, cols = qkv.shape
+    wide = cols // 2 + LANES
+    block = cols // (2 * halves)
+
+    def kernel(coords, qkv_ref, norm_ref, own_ref, mate_ref, tall):
+        first = coords[3] == 0
+        for j in range(halves):
+            a = qkv_ref[:, 2 * j * block : (2 * j + 1) * block]
+            b = qkv_ref[:, (2 * j + 1) * block : (2 * j + 2) * block]
+            own_ref[:, j * block : (j + 1) * block] = jnp.where(first, a, b).astype(LOW)
+            mate_ref[:, j * block : (j + 1) * block] = jnp.where(first, b, a).astype(LOW)
+        tall[...] = jnp.zeros_like(tall)
+        tall[0:4, :] = norm_ref[...].astype(LOW).astype(WIDE)
+        i = lax.broadcasted_iota(jnp.int32, (rows, rows), 0)
+        j = lax.broadcasted_iota(jnp.int32, (rows, rows), 1)
+        columns = dot_cols((i == j).astype(LOW), tall[...].astype(LOW)).astype(LOW)
+        own_ref[:, cols // 2 :] = columns
+        mate_ref[:, cols // 2 :] = columns
+
+    return pl.pallas_call(
+        kernel,
+        out_shape=[jax.ShapeDtypeStruct((rows, wide), LOW)] * 2,
+        in_specs=[pl.BlockSpec(memory_space=pltpu.SMEM), VMEM, VMEM],
+        out_specs=[VMEM] * 2,
+        scratch_shapes=[pltpu.VMEM((LANES, rows), WIDE)],
+        compiler_params=ROOM,
+    )(coordinates(), qkv, norm)
+
+
+def cast_rest(up, out, down, halves):
+    rows, cols = up.shape
+    block, width = cols // (2 * halves), out.shape[1]
+
+    def kernel(coords, up_ref, out_ref, down_ref, own_ref, mate_ref, part_ref, low_ref):
+        first = coords[3] == 0
+        for j in range(halves):
+            a = up_ref[:, 2 * j * block : (2 * j + 1) * block]
+            b = up_ref[:, (2 * j + 1) * block : (2 * j + 2) * block]
+            own_ref[:, j * block : (j + 1) * block] = jnp.where(first, a, b).astype(LOW)
+            mate_ref[:, j * block : (j + 1) * block] = jnp.where(first, b, a).astype(LOW)
+        part_ref[:rows, :] = out_ref[:, : width // 2].astype(LOW)
+        part_ref[rows:, :] = out_ref[:, width // 2 :].astype(LOW)
+        low_ref[...] = down_ref[...].astype(LOW)
+
+    return pl.pallas_call(
+        kernel,
+        out_shape=[jax.ShapeDtypeStruct((rows, cols // 2), LOW)] * 2
+        + [jax.ShapeDtypeStruct((2 * rows, width // 2), LOW), jax.ShapeDtypeStruct(down.shape, LOW)],
+        in_specs=[pl.BlockSpec(memory_space=pltpu.SMEM), VMEM, VMEM, VMEM],
+        out_specs=[VMEM] * 4,
+        compiler_params=ROOM,
+    )(coordinates(), up, out, down)
+
+
+def join_rows(own, mate, side=None):
+    rows, cols = own.shape
+    wide = cols + (side.shape[1] if side is not None else 0)
+
+    def kernel(coords, own_ref, mate_ref, *refs):
+        out_ref = refs[-1]
+        core = coords[3]
+        out_ref[pl.ds(pl.multiple_of(core * rows, 16), rows), :cols] = own_ref[...]
+        out_ref[pl.ds(pl.multiple_of((1 - core) * rows, 16), rows), :cols] = mate_ref[...]
+        if side is not None:
+            out_ref[:, cols:] = refs[0][...]
+
+    ins = [own, mate] + ([side] if side is not None else [])
+    return pl.pallas_call(
+        kernel,
+        out_shape=jax.ShapeDtypeStruct((2 * rows, wide), LOW),
+        in_specs=[pl.BlockSpec(memory_space=pltpu.SMEM)] + [VMEM] * len(ins),
+        out_specs=VMEM,
+        compiler_params=ROOM,
+    )(coordinates(), *ins)
 
 
 def layer_norm(values, gain, bias):
@@ -238,23 +340,20 @@
     split_qkv = lambda w: jnp.moveaxis(w.reshape(-1, 3 * depth, 2, block), 2, 0).reshape(2, -1, half_qkv)
     split_up = lambda w: jnp.moveaxis(w.reshape(-1, depth, 2, ff_block), 2, 0).reshape(2, -1, half_ff)
 
-    qkv_low, out_low = qkv_weight.astype(LOW), out_weight.astype(LOW)
-    up_low, down_low = up_weight.astype(LOW), down_weight.astype(LOW)
-    norm_low = norm_params.astype(LOW)
     if ring:
-        pad = jnp.zeros((own_rows, LANES - 4), LOW)
-        norm_cols = jnp.concatenate([norm_low.T, pad], axis=1)
-        pair = split_qkv(qkv_low)
-        qkv_mine = jnp.concatenate([mine(pair), norm_cols], axis=1)
-        qkv_mate = swap(jnp.concatenate([other(pair), norm_cols], axis=1), "c")
-        pair = split_up(up_low)
-        up_mine, up_mate = mine(pair), swap(other(pair), "c")
-        out_part = jnp.concatenate([out_low[:, :half_d], out_low[:, half_d:]])
-        up_part = jnp.concatenate([in_order(up_mine, up_mate), out_part], axis=1)
-        x_mate, g_mate = swap(own_x, "c"), swap(own_g, "c")
-        qkv_parts = gather_chips(in_order(qkv_mine, qkv_mate))
-        up_parts = gather_chips(up_part)
-        down_parts = gather_chips(down_low)
+        qkv_mine, qkv_give = cast_qkv(qkv_weight, norm_params, 3 * depth)
+        up_mine, up_give, out_part, down_low = cast_rest(after(up_weight, qkv_give), out_weight, down_weight, depth)
+        qkv_mate = swap(qkv_give, "c")
+        up_mate = swap(up_give, "c")
+        x_mate = swap(own_x, "c")
+        qkv_column = column_first(join_rows(qkv_mine, qkv_mate))
+        down_plane = plane_first(down_low)
+        up_part = join_rows(up_mine, up_mate, out_part)
+        up_column = column_first(after(up_part, *qkv_column))
+        qkv_parts = plane_last(jnp.stack(qkv_column))
+        g_mate = swap(after(own_g, *qkv_column), "c")
+        up_parts = plane_last(after(jnp.stack(up_column), *qkv_parts[3:]))
+        down_parts = column_last(after(down_plane, *up_column))
 
         def qkv_moves(zz, plane):
             row = lambda h: ((zz * 2 + h) * chips + plane) * own_rows
@@ -270,11 +369,16 @@
         def down_moves(zz, plane):
             return [(0, 0, 0, own_units, width, zz * ff_block + plane * own_units, 0)]
 
-        qkv_w, norm_w = place(qkv_parts, depth, [(width, half_qkv), (width, LANES)], qkv_moves)
-        up_w, out_w = place(up_parts, depth, [(width, half_ff), (half_d, width)], up_moves)
-        (down_w,) = place(down_parts, depth, [(half_ff, width)], down_moves)
+        spots = column_first_spots(depth)
+        qkv_w, norm_w = place(qkv_parts, depth, [(width, half_qkv), (width, LANES)], spots, qkv_moves)
+        up_w, out_w = place(up_parts, depth, [(width, half_ff), (half_d, width)], spots, up_moves)
+        spots = plane_first_spots(depth, own_units)
+        (down_w,) = place(down_parts, depth, [(half_ff, width)], spots, down_moves)
         norm_vals = norm_w[:, :4].T.astype(WIDE)
     else:
+        qkv_low, out_low = qkv_weight.astype(LOW), out_weight.astype(LOW)
+        up_low, down_low = up_weight.astype(LOW), down_weight.astype(LOW)
+        norm_low = norm_params.astype(LOW)
         x_mate, g_mate = swap(own_x, "c"), swap(own_g, "c")
         whole = lambda w, axis=0: lax.all_gather(w, ALL, axis=axis, tiled=True)
         qkv_w, up_w = mine(split_qkv(whole(qkv_low))), mine(split_up(whole(up_low)))
@@ -375,9 +479,11 @@
             row = ((zz * 2 + half) * chips + plane) * own_rows
             return [(0, row, 0, own_rows, half_qkv, 0, 0), (1, row, 0, own_rows, LANES, 0, half_qkv)]
 
-        down_red = reduce_chips(*unplace([down_grad], depth, (thin, width), down_cuts))
-        up_red = reduce_chips(*unplace([up_grad, out_grad], depth, (own_rows, half_ff + half_d), up_cuts))
-        qkv_red = reduce_chips(*unplace([qkv_grad, norm_cols], depth, (own_rows, half_qkv + LANES), qkv_cuts))
+        down_red, gate = reduce_chips(*unplace([down_grad], depth, (thin, width), down_cuts))
+        cuts = unplace([up_grad, out_grad], depth, (own_rows, half_ff + half_d), up_cuts)
+        up_red, gate = reduce_chips(*cuts, gate)
+        cuts = unplace([qkv_grad, norm_cols], depth, (own_rows, half_qkv + LANES), qkv_cuts)
+        qkv_red, gate = reduce_chips(*cuts, gate)
         out_halves = up_red[:, half_ff:].reshape(2, 2, small, half_d)
         out_red = jnp.concatenate([out_halves[:, 0], out_halves[:, 1]], axis=2).reshape(own_rows, width)
         by_rows = lambda a: a.reshape(2, own_rows, -1)

time: 522 us -> 443 us (0.85)
  waiting for transfers between devices: 220 us -> 170 us
  other arithmetic: 68 us -> 56.9 us
  matrix products: 64.2 us -> 55.5 us
    ppermute x37, waiting for transfers between devices: 121 us -> 81.8 us  [swap(): return lax.ppermute(value, axis, SWAP)]
    ppermute x27, waiting for transfers between devices: 98.5 us -> 88.2 us  [shift(): return lax.ppermute(value, 'z', pairs)]
    unnamed x192 -> x184, local copies, waits for them, and re-layouts: 17.1 us -> 25.8 us
    ppermute x27, starting transfers between devices: 61.7 us -> 54.6 us  [shift(): return lax.ppermute(value, 'z', pairs)]
    dot_general x13, matrix products: 28.4 us -> 22.5 us  [mul(): return jnp.einsum(spec, left, right, preferred_element_type=WIDE)]
    slice x7 -> x6, local copies, waits for them, and re-layouts: 6.79 us -> 1.26 us  [the longest x4 1.24 us: plane_last(): far = (swap(along_y[:half], 'x'), swap(along_x[half:], 'y'))]
    another operation x12 -> x8, other arithmetic: 10.6 us -> 5.49 us
  transfers between devices with their start and end apart: 65 -> 65, of which waited for: 22 -> 31; matrix products, arithmetic and copies ran while one was open for 27% -> 24% of each run, Pallas kernels for 2% -> 2%
where the time goes in v3:
time: 443 us; the launch traced here: 439 us
  waiting for transfers between devices  170 us (38%)
  starting transfers between devices  88.5 us (20%)
  other arithmetic  56.9 us (13%)
  matrix products  55.5 us (13%)
  local copies, waits for them, and re-layouts  48.4 us (11%)
  Pallas kernels  12 us (3%)
  between operations  7.45 us (2%)
    ppermute x27, waiting for transfers between devices, shift(): return lax.ppermute(value, 'z', pairs)  88.2 us
    ppermute x37, waiting for transfers between devices, swap(): return lax.ppermute(value, axis, SWAP)  81.8 us
    ppermute x27, starting transfers between devices, shift(): return lax.ppermute(value, 'z', pairs)  54.6 us
    ppermute x37, starting transfers between devices, swap(): return lax.ppermute(value, axis, SWAP)  32.4 us
    unnamed x184, local copies, waits for them, and re-layouts  25.8 us
    dot_general x13, matrix products, mul(): return jnp.einsum(spec, left, right, preferred_element_type=WIDE)  22.5 us
    dot_general x4, matrix products, dot_rows(): lax.dot_general(left, right, (((0,), (0,)), ((), ())), preferred_element_...  12.1 us
    dot_general x4, matrix products, dot(): return jnp.dot(left, right, preferred_element_type=WIDE)  10.7 us
  transfers between devices with their start and end apart: 65, of which 31 were waited for; matrix products, arithmetic and copies ran while one was open for 24% of the time, Pallas kernels for 2%

profile of v3, /device:TPU:0, one launch (start us, length us, event | category | flops | bytes accessed | tf_op | source)
XLA Modules:
  0.0 439.2 jit_solution(17433489303627084767)
XLA Ops:
  6.8 3.0 collective-permute-start.22
  14.3 3.7 collective-permute-start.4
  24.1 12.6 %collective-permute-done.3 = bf16[64,1664]{1,0:T(8,128)(2,1)S(1)} collective-permute-done((bf16[64,1664]{1,0:T(8,128)(2,1)S(1)}, bf16[64,1664]{1,0:T(8,128)(2,1)S(1)}, u32[]{:S(2)}, u32[]{:S(2)}) %collective-permute-start.3) | collective-permute-done | bytes 213024 | tf_op jit(solution)/shard_map/ppermute | solution.py:33
  44.8 12.9 %collective-permute-done.6.refs_2_ = bf16[4,64,1664]{2,1,0:T(8,128)(2,1)S(1)} collective-permute-done((bf16[4,64,1664]{2,1,0:T(8,128)(2,1)S(1)}, bf16[4,64,1664]{2,1,0:T(8,128)(2,1)S(1)}, u32[]{:S(2)}, u32[]{:S(2)}) %collective-permute-start.6) | collective-permute-done | bytes 852000 | tf_op jit(solution)/shard_map/ppermute | solution.py:27
  59.9 8.6 %collective-permute-done.14 = bf16[64,2560]{1,0:T(8,128)(2,1)S(1)} collective-permute-done((bf16[64,2560]{1,0:T(8,128)(2,1)S(1)}, bf16[64,2560]{1,0:T(8,128)(2,1)S(1)}, u32[]{:S(2)}, u32[]{:S(2)}) %collective-permute-start.14) | collective-permute-done | bytes 327712 | tf_op jit(solution)/shard_map/ppermute | solution.py:33
  76.7 5.1 %collective-permute-start.11 = (bf16[260,128]{1,0:T(8,128)(2,1)S(1)}, bf16[260,128]{1,0:T(8,128)(2,1)S(1)}, u32[]{:S(2)}, u32[]{:S(2)}) collective-permute-start(bf16[260,128]{1,0:T(8,128)(2,1)S(1)} %pad_maximum_fusion.18), channel_id=1, source_target_pairs={{0,24},{1,25},{2,26},{3,27},{4,28},{5,29},{6,30},{7,31}} | collective-permute-start | bytes 199688 | tf_op jit(solution)/shard_map/ppermute | solution.py:33
  96.9 15.8 %collective-permute-done.17.refs_2_ = bf16[4,64,2560]{2,1,0:T(8,128)(2,1)} collective-permute-done((bf16[4,64,2560]{2,1,0:T(8,128)(2,1)S(1)}, bf16[4,64,2560]{2,1,0:T(8,128)(2,1)}, u32[]{:S(2)}, u32[]{:S(2)}) %collective-permute-start.17) | collective-permute-done | bytes 1310752 | tf_op jit(solution)/shard_map/ppermute | solution.py:27
  119.9 13.1 %collective-permute-start.27 = (bf16[512,1024]{1,0:T(8,128)(2,1)}, bf16[512,1024]{1,0:T(8,128)(2,1)}, u32[]{:S(2)}, u32[]{:S(2)}) collective-permute-start(bf16[512,1024]{1,0:T(8,128)(2,1)} %collective-permute-done.26.refs_2_), channel_id=1, source_target_pairs={{0,8},{8,16},{16,24},{24,0},{1,9},{9,17},{17,25},{25,1},{2,10},{10... | collective-permute-start | bytes 3145736 | tf_op jit(solution)/shard_map/ppermute | solution.py:33
  143.2 12.1 %collective-permute-done.27.refs_3_ = bf16[512,1024]{1,0:T(8,128)(2,1)} collective-permute-done((bf16[512,1024]{1,0:T(8,128)(2,1)}, bf16[512,1024]{1,0:T(8,128)(2,1)}, u32[]{:S(2)}, u32[]{:S(2)}) %collective-permute-start.27) | collective-permute-done | bytes 1048608 | tf_op jit(solution)/shard_map/ppermute | solution.py:33
  162.8 5.4 %fusion.6 = bf16[512,2048]{1,0:T(8,128)(2,1)S(1)} fusion(f32[512,2048]{1,0:T(8,128)S(1)} %fusion.88, bf16[2048,1024]{1,0:T(8,128)(2,1)S(1)} %shard_map.310, bf16[256,1024]{1,0:T(8,128)(2,1)S(1)} %get-tuple-element.231, bf16[256,1024]{1,0:T(8,128)(2,1)S(1)} %get-tuple-element.230), kind=kOutput, calls=%fused_computation.11 | convolution fusion | flops 2170552320 | bytes 11534336 | tf_op jit(solution)/shard_map/dot_general | solution.py:271
  170.6 3.0 convolution_convert_fusion.refs_0_
  178.4 4.7 %convolution_convert_fusion.1.refs_0_ = bf16[1024,2048]{1,0:T(8,128)(2,1)} fusion(bf16[512,2048]{1,0:T(8,128)(2,1)S(1)} %fusion.6, f32[512,1024]{1,0:T(8,128)S(1)} %get-tuple-element.204, f32[1024]{0:T(1024)S(1)} %get-tuple-element.177, f32[1024]{0:T(1024)S(1)} %get-tuple-element.176, f32[512]{0:T(512)S(1)} %fusion.81, f32[512]{0:T(512)S(1)} %broadcast_multiply_fusion.3), kind=kOutput, calls=%fused_computation.14 | convolution fusion | flops 2152202240 | bytes 8400896 | tf_op jit(solution)/shard_map/dot_general | solution.py:267
  184.1 4.5 %fusion.98 = (f32[512]{0:T(512)S(1)}, f32[512,1024]{1,0:T(8,128)S(1)}, f32[512,1024]{1,0:T(8,128)}, bf16[512,1024]{1,0:T(8,128)(2,1)}) fusion(f32[512]{0:T(512)S(1)} %multiply_multiply_fusion.8, f32[512,1024]{1,0:T(8,128)S(1)} %get-tuple-element.204, f32[512]{0:T(512)S(1)} %broadcast_multiply_fusion.3, f32[512]{0:T(512)S(1)} %fusion.81, ...), kind=kOutput, calls=%fused_computation.279 | convolution fusion | flops 2162687488 | bytes 18886656 | tf_op jit(solution)/shard_map/dot_general | solution.py:263
  222.0 4.9 %fusion.28 = f32[8,64,512]{2,1,0:T(8,128)S(1)} fusion(bf16[512,8,64]{0,2,1:T(8,128)(2,1)S(1)} %copy-done.54, f32[8,512,512]{1,2,0:T(8,128)} %copy-done.33, f32[512,512]{0,1:T(8,128)S(1)} %copy-done.37), kind=kOutput, calls=%fused_computation.65 | convolution fusion | flops 272629760 | bytes 11010048 | tf_op jit(solution)/shard_map/hts,thf->shf/dot_general | solution.py:275
  253.1 6.9 %collective-permute-start.57 = (bf16[128,1024]{1,0:T(8,128)(2,1)S(1)}, bf16[128,1024]{1,0:T(8,128)(2,1)S(1)}, u32[]{:S(2)}, u32[]{:S(2)}) collective-permute-start(bf16[128,1024]{1,0:T(8,128)(2,1)S(1)} %pad_maximum_fusion.13), channel_id=1, source_target_pairs={{0,24},{8,0},{16,8},{24,16},{1,25},{9,1},{17,9},{25,17},{2,26},{10... | collective-permute-start | bytes 786440 | tf_op jit(solution)/shard_map/ppermute | solution.py:33
  263.0 3.7 collective-permute-done.57
  268.3 12.1 %collective-permute-done.56 = bf16[128,1024]{1,0:T(8,128)(2,1)S(1)} collective-permute-done((bf16[128,1024]{1,0:T(8,128)(2,1)S(1)}, bf16[128,1024]{1,0:T(8,128)(2,1)S(1)}, u32[]{:S(2)}, u32[]{:S(2)}) %collective-permute-start.56) | collective-permute-done | bytes 262176 | tf_op jit(solution)/shard_map/ppermute | solution.py:33
  285.4 13.2 %collective-permute-done.41 = bf16[2,4,32,2560]{3,2,1,0:T(8,128)(2,1)S(1)} collective-permute-done((bf16[2,4,32,2560]{3,2,1,0:T(8,128)(2,1)S(1)}, bf16[2,4,32,2560]{3,2,1,0:T(8,128)(2,1)S(1)}, u32[]{:S(2)}, u32[]{:S(2)}) %collective-permute-start.41) | collective-permute-done | bytes 1310752 | tf_op jit(solution)/shard_map/ppermute | solution.py:27
  300.3 7.6 %collective-permute-done.40 = bf16[4,32,2560]{2,1,0:T(8,128)(2,1)S(1)} collective-permute-done((bf16[4,32,2560]{2,1,0:T(8,128)(2,1)S(1)}, bf16[4,32,2560]{2,1,0:T(8,128)(2,1)S(1)}, u32[]{:S(2)}, u32[]{:S(2)}) %collective-permute-start.40) | collective-permute-done | bytes 655392 | tf_op jit(solution)/shard_map/ppermute | solution.py:27
  311.1 4.3 collective-permute-start.53
  323.9 14.8 %collective-permute-done.52 = bf16[64,2560]{1,0:T(8,128)(2,1)} collective-permute-done((bf16[64,2560]{1,0:T(8,128)(2,1)}, bf16[64,2560]{1,0:T(8,128)(2,1)}, u32[]{:S(2)}, u32[]{:S(2)}) %collective-permute-start.52) | collective-permute-done | bytes 327712 | tf_op jit(solution)/shard_map/ppermute | solution.py:33
  346.8 17.6 %collective-permute-done.43 = bf16[2,4,32,1664]{3,2,1,0:T(8,128)(2,1)S(1)} collective-permute-done((bf16[2,4,32,1664]{3,2,1,0:T(8,128)(2,1)}, bf16[2,4,32,1664]{3,2,1,0:T(8,128)(2,1)S(1)}, u32[]{:S(2)}, u32[]{:S(2)}) %collective-permute-start.43) | collective-permute-done | bytes 852000 | tf_op jit(solution)/shard_map/ppermute | solution.py:27
  366.0 7.0 %collective-permute-done.46 = bf16[4,32,1664]{2,1,0:T(8,128)(2,1)S(1)} collective-permute-done((bf16[4,32,1664]{2,1,0:T(8,128)(2,1)S(1)}, bf16[4,32,1664]{2,1,0:T(8,128)(2,1)S(1)}, u32[]{:S(2)}, u32[]{:S(2)}) %collective-permute-start.46) | collective-permute-done | bytes 426016 | tf_op jit(solution)/shard_map/ppermute | solution.py:27
  382.4 13.5 %collective-permute-done.48 = bf16[64,1664]{1,0:T(8,128)(2,1)S(1)} collective-permute-done((bf16[64,1664]{1,0:T(8,128)(2,1)S(1)}, bf16[64,1664]{1,0:T(8,128)(2,1)S(1)}, u32[]{:S(2)}, u32[]{:S(2)}) %collective-permute-start.48) | collective-permute-done | bytes 213024 | tf_op jit(solution)/shard_map/ppermute | solution.py:33
  (460 shorter events, 221.5 us)
Async XLA Ops:
  11.3 30.8 %collective-permute-start = (bf16[256,1024]{1,0:T(8,128)(2,1)}, bf16[256,1024]{1,0:T(8,128)(2,1)S(1)}, u32[]{:S(2)}, u32[]{:S(2)}) collective-permute-start(bf16[256,1024]{1,0:T(8,128)(2,1)} %bitcast.318), channel_id=1, source_target_pairs={{0,4},{4,0},{1,5},{5,1},{2,6},{6,2},{3,7},{7,3},{8,12},{12,8},{9,1... | collective-permute-start | bytes 1572872 | tf_op jit(solution)/shard_map/ppermute | solution.py:27
  36.8 22.5 %collective-permute-start.5 = (bf16[4,64,1664]{2,1,0:T(8,128)(2,1)S(1)}, bf16[4,64,1664]{2,1,0:T(8,128)(2,1)S(1)}, u32[]{:S(2)}, u32[]{:S(2)}) collective-permute-start(bf16[4,64,1664]{2,1,0:T(8,128)(2,1)S(1)} %pad_maximum_fusion.7.refs_0_), channel_id=1, source_target_pairs={{0,1},{1,0},{2,3},{3,2},{4,5},{5,4},{6,7},{7,6},{8,9},{9,8},{10,11... | collective-permute-start | bytes 2555912 | tf_op jit(solution)/shard_map/ppermute | solution.py:27
  37.9 22.0 %collective-permute-start.15 = (bf16[64,2560]{1,0:T(8,128)(2,1)S(1)}, bf16[64,2560]{1,0:T(8,128)(2,1)S(1)}, u32[]{:S(2)}, u32[]{:S(2)}) collective-permute-start(bf16[64,2560]{1,0:T(8,128)(2,1)S(1)} %shard_map.308), channel_id=1, source_target_pairs={{0,24},{8,0},{16,8},{24,16},{1,25},{9,1},{17,9},{25,17},{2,26},{10... | collective-permute-start | bytes 983048 | tf_op jit(solution)/shard_map/ppermute | solution.py:33
  38.6 29.9 %collective-permute-start.14 = (bf16[64,2560]{1,0:T(8,128)(2,1)S(1)}, bf16[64,2560]{1,0:T(8,128)(2,1)S(1)}, u32[]{:S(2)}, u32[]{:S(2)}) collective-permute-start(bf16[64,2560]{1,0:T(8,128)(2,1)S(1)} %shard_map.308), channel_id=1, source_target_pairs={{0,16},{8,24},{16,0},{24,8},{1,17},{9,25},{17,1},{25,9},{2,18},{10... | collective-permute-start | bytes 983048 | tf_op jit(solution)/shard_map/ppermute | solution.py:33
  42.1 26.5 %collective-permute-start.13 = (bf16[64,2560]{1,0:T(8,128)(2,1)S(1)}, bf16[64,2560]{1,0:T(8,128)(2,1)S(1)}, u32[]{:S(2)}, u32[]{:S(2)}) collective-permute-start(bf16[64,2560]{1,0:T(8,128)(2,1)S(1)} %shard_map.308), channel_id=1, source_target_pairs={{0,8},{8,16},{16,24},{24,0},{1,9},{9,17},{17,25},{25,1},{2,10},{10... | collective-permute-start | bytes 983048 | tf_op jit(solution)/shard_map/ppermute | solution.py:33
  68.5 27.6 %collective-permute-start.25 = (bf16[512,1024]{1,0:T(8,128)(2,1)}, bf16[512,1024]{1,0:T(8,128)(2,1)}, u32[]{:S(2)}, u32[]{:S(2)}) collective-permute-start(bf16[512,1024]{1,0:T(8,128)(2,1)} %constant_dynamic-update-slice_fusion.refs_0_), channel_id=1, source_target_pairs={{0,8},{8,16},{16,24},{24,0},{1,9},{9,17},{17,25},{25,1},{2,10},{10... | collective-permute-start | bytes 3145736 | tf_op jit(solution)/shard_map/ppermute | solution.py:33
  83.1 31.5 %collective-permute-start.16 = (bf16[4,64,2560]{2,1,0:T(8,128)(2,1)S(1)}, bf16[4,64,2560]{2,1,0:T(8,128)(2,1)S(1)}, u32[]{:S(2)}, u32[]{:S(2)}) collective-permute-start(bf16[4,64,2560]{2,1,0:T(8,128)(2,1)S(1)} %pad_maximum_fusion.2.refs_0_), channel_id=1, source_target_pairs={{0,1},{1,0},{2,3},{3,2},{4,5},{5,4},{6,7},{7,6},{8,9},{9,8},{10,11... | collective-permute-start | bytes 3932168 | tf_op jit(solution)/shard_map/ppermute | solution.py:27
  84.6 28.2 %collective-permute-start.17 = (bf16[4,64,2560]{2,1,0:T(8,128)(2,1)S(1)}, bf16[4,64,2560]{2,1,0:T(8,128)(2,1)}, u32[]{:S(2)}, u32[]{:S(2)}) collective-permute-start(bf16[4,64,2560]{2,1,0:T(8,128)(2,1)S(1)} %pad_maximum_fusion.2.refs_0_), channel_id=1, source_target_pairs={{0,2},{2,0},{1,3},{3,1},{4,6},{6,4},{5,7},{7,5},{8,10},{10,8},{9,1... | collective-permute-start | bytes 3932168 | tf_op jit(solution)/shard_map/ppermute | solution.py:27
  96.1 23.8 %collective-permute-start.26 = (bf16[512,1024]{1,0:T(8,128)(2,1)}, bf16[512,1024]{1,0:T(8,128)(2,1)}, u32[]{:S(2)}, u32[]{:S(2)}) collective-permute-start(bf16[512,1024]{1,0:T(8,128)(2,1)} %collective-permute-done.25.refs_1_), channel_id=1, source_target_pairs={{0,8},{8,16},{16,24},{24,0},{1,9},{9,17},{17,25},{25,1},{2,10},{10... | collective-permute-start | bytes 3145736 | tf_op jit(solution)/shard_map/ppermute | solution.py:33
  119.9 35.3 %collective-permute-start.27 = (bf16[512,1024]{1,0:T(8,128)(2,1)}, bf16[512,1024]{1,0:T(8,128)(2,1)}, u32[]{:S(2)}, u32[]{:S(2)}) collective-permute-start(bf16[512,1024]{1,0:T(8,128)(2,1)} %collective-permute-done.26.refs_2_), channel_id=1, source_target_pairs={{0,8},{8,16},{16,24},{24,0},{1,9},{9,17},{17,25},{25,1},{2,10},{10... | collective-permute-start | bytes 3145736 | tf_op jit(solution)/shard_map/ppermute | solution.py:33
  175.4 42.1 %collective-permute-start.35 = (bf16[2,4,64,1024]{3,2,1,0:T(8,128)(2,1)}, bf16[2,4,64,1024]{3,2,1,0:T(8,128)(2,1)}, u32[]{:S(2)}, u32[]{:S(2)}) collective-permute-start(bf16[2,4,64,1024]{3,2,1,0:T(8,128)(2,1)} %get-tuple-element.69), channel_id=1, source_target_pairs={{0,2},{2,0},{1,3},{3,1},{4,6},{6,4},{5,7},{7,5},{8,10},{10,8},{9,1... | collective-permute-start | bytes 3145736 | tf_op jit(solution)/shard_map/ppermute | solution.py:27
  176.9 50.0 %collective-permute-start.37 = (bf16[2,4,64,1024]{3,2,1,0:T(8,128)(2,1)S(1)}, bf16[2,4,64,1024]{3,2,1,0:T(8,128)(2,1)}, u32[]{:S(2)}, u32[]{:S(2)}) collective-permute-start(bf16[2,4,64,1024]{3,2,1,0:T(8,128)(2,1)S(1)} %get-tuple-element.71), channel_id=1, source_target_pairs={{0,1},{1,0},{2,3},{3,2},{4,5},{5,4},{6,7},{7,6},{8,9},{9,8},{10,11... | collective-permute-start | bytes 3145736 | tf_op jit(solution)/shard_map/ppermute | solution.py:27
  200.1 34.8 %collective-permute-start.33 = (bf16[260,128]{1,0:T(8,128)(2,1)S(1)}, bf16[260,128]{1,0:T(8,128)(2,1)}, u32[]{:S(2)}, u32[]{:S(2)}) collective-permute-start(bf16[260,128]{1,0:T(8,128)(2,1)S(1)} %pad_maximum_fusion.19), channel_id=1, source_target_pairs={{24,0},{25,1},{26,2},{27,3},{28,4},{29,5},{30,6},{31,7}} | collective-permute-start | bytes 199688 | tf_op jit(solution)/shard_map/ppermute | solution.py:33
  201.4 34.0 %collective-permute-start.32 = (bf16[260,128]{1,0:T(8,128)(2,1)S(1)}, bf16[260,128]{1,0:T(8,128)(2,1)}, u32[]{:S(2)}, u32[]{:S(2)}) collective-permute-start(bf16[260,128]{1,0:T(8,128)(2,1)S(1)} %pad_maximum_fusion.19), channel_id=1, source_target_pairs={{16,0},{24,8},{17,1},{25,9},{18,2},{26,10},{19,3},{27,11},{20,4},{... | collective-permute-start | bytes 199688 | tf_op jit(solution)/shard_map/ppermute | solution.py:33
  202.7 32.7 %collective-permute-start.31 = (bf16[260,128]{1,0:T(8,128)(2,1)S(1)}, bf16[260,128]{1,0:T(8,128)(2,1)}, u32[]{:S(2)}, u32[]{:S(2)}) collective-permute-start(bf16[260,128]{1,0:T(8,128)(2,1)S(1)} %pad_maximum_fusion.19), channel_id=1, source_target_pairs={{8,0},{16,8},{24,16},{9,1},{17,9},{25,17},{10,2},{18,10},{26,18},{... | collective-permute-start | bytes 199688 | tf_op jit(solution)/shard_map/ppermute | solution.py:33
  217.5 42.6 %collective-permute-start.28 = (bf16[256,1024]{1,0:T(8,128)(2,1)}, bf16[256,1024]{1,0:T(8,128)(2,1)}, u32[]{:S(2)}, u32[]{:S(2)}) collective-permute-start(bf16[256,1024]{1,0:T(8,128)(2,1)} %fusion.31), channel_id=1, source_target_pairs={{0,4},{4,0},{1,5},{5,1},{2,6},{6,2},{3,7},{7,3},{8,12},{12,8},{9,1... | collective-permute-start | bytes 1572872 | tf_op jit(solution)/shard_map/ppermute | solution.py:27
  244.4 37.5 %collective-permute-start.34 = (bf16[512,1024]{1,0:T(8,128)(2,1)S(1)}, bf16[512,1024]{1,0:T(8,128)(2,1)S(1)}, u32[]{:S(2)}, u32[]{:S(2)}) collective-permute-start(bf16[512,1024]{1,0:T(8,128)(2,1)S(1)} %get-tuple-element.256), channel_id=1, source_target_pairs={{0,4},{4,0},{1,5},{5,1},{2,6},{6,2},{3,7},{7,3},{8,12},{12,8},{9,1... | collective-permute-start | bytes 3145736 | tf_op jit(solution)/shard_map/ppermute | solution.py:27
  249.3 33.7 %collective-permute-start.39 = (bf16[2,4,32,2560]{3,2,1,0:T(8,128)(2,1)S(1)}, bf16[2,4,32,2560]{3,2,1,0:T(8,128)(2,1)S(1)}, u32[]{:S(2)}, u32[]{:S(2)}) collective-permute-start(bf16[2,4,32,2560]{3,2,1,0:T(8,128)(2,1)S(1)} %copy-done.32), channel_id=1, source_target_pairs={{0,2},{2,0},{1,3},{3,1},{4,6},{6,4},{5,7},{7,5},{8,10},{10,8},{9,1... | collective-permute-start | bytes 3932168 | tf_op jit(solution)/shard_map/ppermute | solution.py:27
  266.8 31.7 %collective-permute-start.41 = (bf16[2,4,32,2560]{3,2,1,0:T(8,128)(2,1)S(1)}, bf16[2,4,32,2560]{3,2,1,0:T(8,128)(2,1)S(1)}, u32[]{:S(2)}, u32[]{:S(2)}) collective-permute-start(bf16[2,4,32,2560]{3,2,1,0:T(8,128)(2,1)S(1)} %copy-done.30), channel_id=1, source_target_pairs={{0,1},{1,0},{2,3},{3,2},{4,5},{5,4},{6,7},{7,6},{8,9},{9,8},{10,11... | collective-permute-start | bytes 3932168 | tf_op jit(solution)/shard_map/ppermute | solution.py:27
  283.8 24.1 %collective-permute-start.40 = (bf16[4,32,2560]{2,1,0:T(8,128)(2,1)S(1)}, bf16[4,32,2560]{2,1,0:T(8,128)(2,1)S(1)}, u32[]{:S(2)}, u32[]{:S(2)}) collective-permute-start(bf16[4,32,2560]{2,1,0:T(8,128)(2,1)S(1)} %fusion.36), channel_id=1, source_target_pairs={{0,1},{1,0},{2,3},{3,2},{4,5},{5,4},{6,7},{7,6},{8,9},{9,8},{10,11... | collective-permute-start | bytes 1966088 | tf_op jit(solution)/shard_map/ppermute | solution.py:27
  316.2 22.6 %collective-permute-start.52 = (bf16[64,2560]{1,0:T(8,128)(2,1)}, bf16[64,2560]{1,0:T(8,128)(2,1)}, u32[]{:S(2)}, u32[]{:S(2)}) collective-permute-start(bf16[64,2560]{1,0:T(8,128)(2,1)} %pad_maximum_fusion.9), channel_id=1, source_target_pairs={{0,16},{8,24},{16,0},{24,8},{1,17},{9,25},{17,1},{25,9},{2,18},{10... | collective-permute-start | bytes 983048 | tf_op jit(solution)/shard_map/ppermute | solution.py:33
  321.5 23.5 %collective-permute-start.45 = (bf16[2,4,32,1664]{3,2,1,0:T(8,128)(2,1)}, bf16[2,4,32,1664]{3,2,1,0:T(8,128)(2,1)}, u32[]{:S(2)}, u32[]{:S(2)}) collective-permute-start(bf16[2,4,32,1664]{3,2,1,0:T(8,128)(2,1)} %get-tuple-element.79), channel_id=1, source_target_pairs={{0,2},{2,0},{1,3},{3,1},{4,6},{6,4},{5,7},{7,5},{8,10},{10,8},{9,1... | collective-permute-start | bytes 2555912 | tf_op jit(solution)/shard_map/ppermute | solution.py:27
  342.3 22.0 %collective-permute-start.43 = (bf16[2,4,32,1664]{3,2,1,0:T(8,128)(2,1)}, bf16[2,4,32,1664]{3,2,1,0:T(8,128)(2,1)S(1)}, u32[]{:S(2)}, u32[]{:S(2)}) collective-permute-start(bf16[2,4,32,1664]{3,2,1,0:T(8,128)(2,1)} %get-tuple-element.76), channel_id=1, source_target_pairs={{0,1},{1,0},{2,3},{3,2},{4,5},{5,4},{6,7},{7,6},{8,9},{9,8},{10,11... | collective-permute-start | bytes 2555912 | tf_op jit(solution)/shard_map/ppermute | solution.py:27
  346.1 26.9 %collective-permute-start.46 = (bf16[4,32,1664]{2,1,0:T(8,128)(2,1)S(1)}, bf16[4,32,1664]{2,1,0:T(8,128)(2,1)S(1)}, u32[]{:S(2)}, u32[]{:S(2)}) collective-permute-start(bf16[4,32,1664]{2,1,0:T(8,128)(2,1)S(1)} %fusion.49), channel_id=1, source_target_pairs={{0,1},{1,0},{2,3},{3,2},{4,5},{5,4},{6,7},{7,6},{8,9},{9,8},{10,11... | collective-permute-start | bytes 1277960 | tf_op jit(solution)/shard_map/ppermute | solution.py:27
  (128 other events, 1408.5 us)

commit v4 on v3

--- a/solution.py
+++ b/solution.py
@@ -245,18 +245,18 @@
     )(coordinates(), *ins)
 
 
-def layer_norm(values, gain, bias):
-    center = values - jnp.mean(values, axis=-1, keepdims=True)
-    spread = jnp.mean(center * center, axis=-1, keepdims=True)
-    return center * lax.rsqrt(spread + NORM_EPS) * gain + bias
-
-
-def feature_map(values):
-    return jax.nn.elu(values) + 1.0
-
-
-def gelu_tanh(values):
-    return jax.nn.gelu(values, approximate=True)
+def run(kernel, outs, *ins, scalars=True, scratch=(), flops=10**9, room=40):
+    size = sum(a.size * a.dtype.itemsize for a in ins)
+    out_shape = [jax.ShapeDtypeStruct(shape, kind) for shape, kind in outs]
+    return pl.pallas_call(
+        kernel,
+        out_shape=out_shape,
+        in_specs=([pl.BlockSpec(memory_space=pltpu.SMEM)] if scalars else []) + [VMEM] * len(ins),
+        out_specs=[VMEM] * len(outs),
+        scratch_shapes=list(scratch),
+        compiler_params=pltpu.CompilerParams(vmem_limit_bytes=room * 1024 * 1024),
+        cost_estimate=pl.CostEstimate(flops=flops, bytes_accessed=2 * size, transcendentals=0),
+    )(*([coordinates()] if scalars else []), *ins)
 
 
 def dot(left, right):
@@ -271,8 +271,307 @@
     return lax.dot_general(left, right, (((1,), (1,)), ((), ())), preferred_element_type=WIDE)
 
 
-def mul(spec, left, right):
-    return jnp.einsum(spec, left, right, preferred_element_type=WIDE)
+def eye(rows, cols):
+    i = lax.broadcasted_iota(jnp.int32, (rows, cols), 0)
+    return (i == lax.broadcasted_iota(jnp.int32, (rows, cols), 1)).astype(LOW)
+
+
+def normalise(values):
+    center = values - jnp.mean(values, axis=-1, keepdims=True)
+    rate = lax.rsqrt(jnp.mean(center * center, axis=-1, keepdims=True) + NORM_EPS)
+    return center * rate, rate
+
+
+def norm_back(normed, rate, grad, gain):
+    scaled = grad * gain
+    shared = jnp.mean(scaled, axis=-1, keepdims=True)
+    along = jnp.mean(scaled * normed, axis=-1, keepdims=True)
+    return rate * (scaled - shared - normed * along)
+
+
+def low_lanes(rows):
+    return lax.broadcasted_iota(jnp.int32, (rows, LANES), 1) < HEAD_DIM
+
+
+def by_head(pair):
+    wide = pair.astype(WIDE)
+    first = low_lanes(pair.shape[0])
+    return jnp.where(first, wide, 0.0).astype(LOW), jnp.where(first, 0.0, wide).astype(LOW)
+
+
+def pack_state(square):
+    first = low_lanes(HEAD_DIM)
+    return jnp.where(first, square[:HEAD_DIM], square[HEAD_DIM:])
+
+
+def open_state(packed):
+    first = low_lanes(HEAD_DIM)
+    return jnp.concatenate([jnp.where(first, packed, 0.0), jnp.where(first, 0.0, packed)])
+
+
+def feature(values):
+    return jnp.where(values > 0.0, values + 1.0, jnp.exp(jnp.minimum(values, 0.0)))
+
+
+def project(x, norm_w, qkv_w):
+    tokens, width = x.shape
+    half = qkv_w.shape[1] // 3
+    pairs = half // LANES
+    step = tokens // 2
+
+    def kernel(x_ref, norm_ref, w_ref, rows_ref, normed_ref, qk_ref, q_ref, k_ref, v_ref, state_ref, sums):
+        rows_ref[...] = dot_cols(eye(8, LANES), norm_ref[...])
+        gain, bias = rows_ref[0:1, :], rows_ref[1:2, :]
+        for i in range(2):
+            at = slice(i * step, (i + 1) * step)
+            normed = normalise(x_ref[at, :].astype(WIDE))[0]
+            normed_ref[at, :] = (normed * gain + bias).astype(LOW)
+            low = normed_ref[at, :]
+            for j, out in enumerate((q_ref, k_ref)):
+                part = dot(low, w_ref[:, j * half : (j + 1) * half])
+                qk_ref[at, j * half : (j + 1) * half] = part
+                out[at, :] = feature(part).astype(LOW)
+            v_ref[at, :] = dot(low, w_ref[:, 2 * half :]).astype(LOW)
+        total = dot_rows(jnp.ones((tokens, 8), LOW), k_ref[...])
+        sums[...] = jnp.zeros_like(sums)
+        for p in range(pairs):
+            lanes = slice(p * LANES, (p + 1) * LANES)
+            packed = pack_state(dot_rows(k_ref[:, lanes], v_ref[:, lanes]))
+            state_ref[p * HEAD_DIM : (p + 1) * HEAD_DIM, :] = packed.astype(LOW)
+            sums[p : p + 1, :] = total[0:1, lanes]
+        state_ref[pairs * HEAD_DIM :, :] = sums[...].astype(LOW)
+
+    outs = [((8, width), WIDE), ((tokens, width), LOW), ((tokens, 2 * half), WIDE)] + [((tokens, half), LOW)] * 3
+    outs += [((pairs * HEAD_DIM + 16, LANES), LOW)]
+    scratch = [pltpu.VMEM((16, LANES), WIDE)]
+    return run(kernel, outs, x, norm_w, qkv_w, scalars=False, scratch=scratch, flops=2 * x.size * qkv_w.shape[1])
+
+
+def total_state(refs):
+    total = refs[0][...].astype(WIDE)
+    for ref in refs[1:]:
+        total = total + ref[...].astype(WIDE)
+    return total
+
+
+def causal_mask(step):
+    i = lax.broadcasted_iota(jnp.int32, (step, step), 0)
+    return i >= lax.broadcasted_iota(jnp.int32, (step, step), 1)
+
+
+def attend(query, key, value, parts):
+    tokens, half = query.shape
+    pairs, step = half // LANES, tokens // 2
+
+    def kernel(q_ref, k_ref, v_ref, *refs):
+        mixed_ref, low_ref, denom_ref, state_ref = refs[len(parts) :]
+        state_ref[...] = total_state(refs[: len(parts)])
+        lower = causal_mask(step)
+        first = low_lanes(step)
+        top = low_lanes(HEAD_DIM)
+        diagonal = eye(LANES, LANES).astype(WIDE)
+        for p in range(pairs):
+            lanes = slice(p * LANES, (p + 1) * LANES)
+            packed = state_ref[p * HEAD_DIM : (p + 1) * HEAD_DIM, :]
+            sums = state_ref[pairs * HEAD_DIM + p : pairs * HEAD_DIM + p + 1, :]
+            column = jnp.sum(diagonal * sums, axis=1, keepdims=True)
+            zero = jnp.zeros((HEAD_DIM, LANES), WIDE)
+            ext = (
+                jnp.concatenate([jnp.where(top, packed, column[:HEAD_DIM]), zero]).astype(LOW),
+                jnp.concatenate([zero, jnp.where(top, column[HEAD_DIM:], packed)]).astype(LOW),
+            )
+            wide = v_ref[:, lanes].astype(WIDE)
+            full = low_lanes(tokens)
+            value_ext = (jnp.where(full, wide, 1.0).astype(LOW), jnp.where(full, 1.0, wide).astype(LOW))
+            queries = by_head(q_ref[:, lanes])
+            for i in range(2):
+                at = slice(i * step, (i + 1) * step)
+                got = []
+                for h in range(2):
+                    rows = queries[h][at]
+                    total = dot(rows, ext[h])
+                    for j in range(i + 1):
+                        to = slice(j * step, (j + 1) * step)
+                        scores = dot_cols(rows, k_ref[to, lanes])
+                        if j == i:
+                            scores = jnp.where(lower, scores, 0.0)
+                        total = total + dot(scores.astype(LOW), value_ext[h][to])
+                    got.append(total)
+                denom = pltpu.roll(jnp.where(first, got[1], got[0]), HEAD_DIM, 1)
+                mixed = jnp.where(first, got[0], got[1]) / denom
+                mixed_ref[at, lanes] = mixed
+                low_ref[at, lanes] = mixed.astype(LOW)
+                denom_ref[at, lanes] = denom
+
+    outs = [((tokens, half), WIDE), ((tokens, half), LOW), ((tokens, half), WIDE), (parts[0].shape, WIDE)]
+    return run(kernel, outs, query, key, value, *parts, scalars=False, flops=8 * tokens * tokens * half)
+
+
+def feed(x, part, got, rows, up_w):
+    tokens, width = x.shape
+    units, step, cut = up_w.shape[1], tokens // 2, 512
+
+    def kernel(x_ref, part_ref, got_ref, rows_ref, w_ref, resid_ref, normed_ref, act_ref, slope_ref):
+        for i in range(2):
+            at = slice(i * step, (i + 1) * step)
+            resid = x_ref[at, :].astype(WIDE) + part_ref[at, :] + got_ref[at, :].astype(WIDE)
+            resid_ref[at, :] = resid
+            normed_ref[at, :] = (normalise(resid)[0] * rows_ref[2:3, :] + rows_ref[3:4, :]).astype(LOW)
+            for j in range(units // cut):
+                to = slice(j * cut, (j + 1) * cut)
+                v = dot(normed_ref[at, :], w_ref[:, to])
+                root = (2.0 / 3.141592653589793) ** 0.5
+                square = v * v
+                bend = jnp.tanh(root * v * (1.0 + 0.044715 * square))
+                cdf = 0.5 * (1.0 + bend)
+                act_ref[at, to] = (v * cdf).astype(LOW)
+                slope_ref[at, to] = cdf + 0.5 * v * (1.0 - bend * bend) * (root * (1.0 + 3.0 * 0.044715 * square))
+
+    outs = [((tokens, width), WIDE), ((tokens, width), LOW), ((tokens, units), LOW), ((tokens, units), WIDE)]
+    return run(kernel, outs, x, part, got, rows, up_w, scalars=False, flops=2 * x.size * units)
+
+
+def feed_back(grad_out, down_w, slope, up_w):
+    tokens, width = grad_out.shape
+    units, step, cut = up_w.shape[1], tokens // 2, 512
+
+    def kernel(g_ref, down_ref, slope_ref, up_ref, hidden_ref, part_ref, low_ref):
+        for i in range(2):
+            at = slice(i * step, (i + 1) * step)
+            for j in range(units // cut):
+                to = slice(j * cut, (j + 1) * cut)
+                grad = dot_cols(g_ref[at, :], down_ref[to, :]) * slope_ref[at, to]
+                hidden_ref[at, to] = grad.astype(LOW)
+            part = dot_cols(hidden_ref[at, :], up_ref[...])
+            part_ref[at, :] = part
+            low_ref[at, :] = part.astype(LOW)
+
+    outs = [((tokens, units), LOW), ((tokens, width), WIDE), ((tokens, width), LOW)]
+    return run(kernel, outs, grad_out, down_w, slope, up_w, scalars=False, flops=4 * tokens * width * units)
+
+
+def attend_turn(part, got, resid, rows, grad_out, out_w, mixed, denom, query):
+    tokens, width = resid.shape
+    half = mixed.shape[1]
+    pairs, step = half // LANES, tokens // 2
+
+    def kernel(
+        part_ref, got_ref, resid_ref, rows_ref, g_ref, w_ref, mixed_ref, denom_ref, q_ref,
+        grad_ref, low_ref, a_ref, b_ref, state_ref, norm_ref, sums,
+    ):
+        gain = rows_ref[2:3, :]
+        gain_grad, bias_grad = jnp.zeros((1, width), WIDE), jnp.zeros((1, width), WIDE)
+        first = low_lanes(step)
+        for i in range(2):
+            at = slice(i * step, (i + 1) * step)
+            normed, rate = normalise(resid_ref[at, :])
+            own = part_ref[at, :]
+            gain_grad = gain_grad + jnp.sum(own * normed, axis=0, keepdims=True)
+            bias_grad = bias_grad + jnp.sum(own, axis=0, keepdims=True)
+            grad = g_ref[at, :].astype(WIDE) + norm_back(normed, rate, own + got_ref[at, :].astype(WIDE), gain)
+            grad_ref[at, :] = grad
+            low_ref[at, :] = grad.astype(LOW)
+            turned = dot_cols(low_ref[at, :], w_ref[...]) / denom_ref[at, :]
+            a_ref[at, :] = turned.astype(LOW)
+            along = turned * mixed_ref[at, :]
+            for p in range(pairs):
+                lanes = slice(p * LANES, (p + 1) * LANES)
+                piece = along[:, lanes]
+                low = jnp.sum(jnp.where(first, piece, 0.0), axis=1, keepdims=True)
+                high = jnp.sum(jnp.where(first, 0.0, piece), axis=1, keepdims=True)
+                b_ref[at, lanes] = -jnp.where(first, low, high)
+        norm_ref[0:1, :] = gain_grad
+        norm_ref[1:2, :] = bias_grad
+        sums[...] = jnp.zeros_like(sums)
+        for p in range(pairs):
+            lanes = slice(p * LANES, (p + 1) * LANES)
+            packed = pack_state(dot_rows(q_ref[:, lanes], a_ref[:, lanes]))
+            state_ref[p * HEAD_DIM : (p + 1) * HEAD_DIM, :] = packed.astype(LOW)
+            sums[p : p + 1, :] = jnp.sum(q_ref[:, lanes].astype(WIDE) * b_ref[:, lanes], axis=0, keepdims=True)
+        state_ref[pairs * HEAD_DIM :, :] = sums[...].astype(LOW)
+
+    outs = [((tokens, width), WIDE), ((tokens, width), LOW), ((tokens, half), LOW), ((tokens, half), WIDE)]
+    outs += [((pairs * HEAD_DIM + 16, LANES), LOW), ((2, width), WIDE)]
+    ins = (part, got, resid, rows, grad_out, out_w, mixed, denom, query)
+    scratch = [pltpu.VMEM((16, LANES), WIDE)]
+    return run(kernel, outs, *ins, scalars=False, scratch=scratch, flops=2 * tokens * width * half)
+
+
+def attend_back(query, key, value, qk, a_low, b_rows, state, parts):
+    tokens, half = query.shape
+    pairs, step = half // LANES, tokens // 2
+
+    def kernel(q_ref, k_ref, v_ref, qk_ref, a_ref, b_ref, state_ref, *refs):
+        out_ref = refs[len(parts)]
+        later = total_state(refs[: len(parts)])
+        lower = causal_mask(step)
+        for p in range(pairs):
+            lanes = slice(p * LANES, (p + 1) * LANES)
+            rows = slice(p * HEAD_DIM, (p + 1) * HEAD_DIM)
+            sums = slice(pairs * HEAD_DIM + p, pairs * HEAD_DIM + p + 1)
+            before, after_it = open_state(state_ref[rows, :]).astype(LOW), open_state(later[rows]).astype(LOW)
+            queries, keys, pulls = by_head(q_ref[:, lanes]), by_head(k_ref[:, lanes]), by_head(a_ref[:, lanes])
+            cuts = [slice(i * step, (i + 1) * step) for i in range(2)]
+            grad_q = [dot_cols(a_ref[c, lanes], before) + b_ref[c, lanes] * state_ref[sums, :] for c in cuts]
+            grad_k = [dot_cols(v_ref[c, lanes], after_it) + later[sums] for c in cuts]
+            grad_v = [dot(k_ref[c, lanes], after_it) for c in cuts]
+            for i in range(2):
+                for j in range(i + 1):
+                    for h in range(2):
+                        q, a = queries[h][cuts[i]], pulls[h][cuts[i]]
+                        b = b_ref[cuts[i], p * LANES + h * HEAD_DIM : p * LANES + h * HEAD_DIM + 1]
+                        scores = dot_cols(q, k_ref[cuts[j], lanes])
+                        pull = dot_cols(a, v_ref[cuts[j], lanes]) + b
+                        if j == i:
+                            scores, pull = jnp.where(lower, scores, 0.0), jnp.where(lower, pull, 0.0)
+                        scores, pull = scores.astype(LOW), pull.astype(LOW)
+                        grad_q[i] = grad_q[i] + dot(pull, keys[h][cuts[j]])
+                        grad_k[j] = grad_k[j] + dot_rows(pull, q)
+                        grad_v[j] = grad_v[j] + dot_rows(scores, a)
+            for i, c in enumerate(cuts):
+                for n, grad in enumerate((grad_q[i], grad_k[i])):
+                    at = slice(n * half + p * LANES, n * half + (p + 1) * LANES)
+                    raw = qk_ref[c, at]
+                    out_ref[c, at] = (grad * jnp.where(raw > 0.0, 1.0, jnp.exp(jnp.minimum(raw, 0.0)))).astype(LOW)
+                out_ref[c, 2 * half + p * LANES : 2 * half + (p + 1) * LANES] = grad_v[i].astype(LOW)
+
+    ins = (query, key, value, qk, a_low, b_rows, state, *parts)
+    return run(kernel, [((tokens, 3 * half), LOW)], *ins, scalars=False, flops=20 * tokens * tokens * half)[0]
+
+
+def project_back(grad, qkv_w, x, norm_two):
+    tokens, width = x.shape
+    step = tokens // 2
+
+    def kernel(grad_ref, w_ref, x_ref, two_ref, part_ref, low_ref, cols_ref, rows):
+        gain_grad, bias_grad = jnp.zeros((1, width), WIDE), jnp.zeros((1, width), WIDE)
+        for i in range(2):
+            at = slice(i * step, (i + 1) * step)
+            part = dot_cols(grad_ref[at, :], w_ref[...])
+            part_ref[at, :] = part
+            low_ref[at, :] = part.astype(LOW)
+            gain_grad = gain_grad + jnp.sum(part * normalise(x_ref[at, :].astype(WIDE))[0], axis=0, keepdims=True)
+            bias_grad = bias_grad + jnp.sum(part, axis=0, keepdims=True)
+        rows[...] = jnp.zeros_like(rows)
+        rows[0:1, :], rows[1:2, :], rows[2:4, :] = gain_grad, bias_grad, two_ref[...]
+        cols_ref[...] = dot_rows(rows[...].astype(LOW), eye(8, LANES)).astype(LOW)
+
+    outs = [((tokens, width), WIDE), ((tokens, width), LOW), ((width, LANES), LOW)]
+    scratch = [pltpu.VMEM((8, width), WIDE)]
+    flops = 2 * x.size * grad.shape[1]
+    return run(kernel, outs, grad, qkv_w, x, norm_two, scalars=False, scratch=scratch, flops=flops)
+
+
+def input_back(part, got, grad_resid, own_x, rows):
+    group, width = own_x.shape
+
+    def kernel(coords, part_ref, got_ref, resid_ref, x_ref, rows_ref, out_ref):
+        at = pl.ds(pl.multiple_of(coords[3] * group, 16), group)
+        normed, rate = normalise(x_ref[...].astype(WIDE))
+        grad = part_ref[at, :] + got_ref[...].astype(WIDE)
+        out_ref[...] = (resid_ref[at, :] + norm_back(normed, rate, grad, rows_ref[0:1, :])).astype(LOW)
+
+    return run(kernel, [((group, width), LOW)], part, got, grad_resid, own_x, rows)[0]
 
 
 def adam_update(weight, first, second, grad, rate, decay):
@@ -284,12 +583,8 @@
     return (weight_new, first_new, second_new)
 
 
-def from_others(value, step):
-    low = value.astype(LOW)
-    total = jnp.zeros(value.shape, WIDE)
-    for k in range(1, lax.axis_size("z")):
-        total = total + shift(low, step * k, wrap=False).astype(WIDE)
-    return total
+def from_others(low, step):
+    return [shift(low, step * k, wrap=False) for k in range(1, lax.axis_size("z"))]
 
 
 def sum_everywhere(value, direct):
@@ -374,7 +669,6 @@
         up_w, out_w = place(up_parts, depth, [(width, half_ff), (half_d, width)], spots, up_moves)
         spots = plane_first_spots(depth, own_units)
         (down_w,) = place(down_parts, depth, [(half_ff, width)], spots, down_moves)
-        norm_vals = norm_w[:, :4].T.astype(WIDE)
     else:
         qkv_low, out_low = qkv_weight.astype(LOW), out_weight.astype(LOW)
         up_low, down_low = up_weight.astype(LOW), down_weight.astype(LOW)
@@ -384,87 +678,33 @@
         qkv_w, up_w = mine(split_qkv(whole(qkv_low))), mine(split_up(whole(up_low)))
         rows_half = lambda w, b: mine(jnp.moveaxis(w.reshape(depth, 2, b, width), 1, 0)).reshape(-1, width)
         out_w, down_w = rows_half(whole(out_low), block), rows_half(whole(down_low), ff_block)
-        norm_vals = whole(norm_low, 1).astype(WIDE)
-
-    inputs = in_order(own_x, x_mate).astype(WIDE)
-    grad_out = in_order(own_g, g_mate)
-    normed_one, norm_one_back = jax.vjp(layer_norm, inputs, norm_vals[0], norm_vals[1])
-    normed_one_low = normed_one.astype(LOW)
-    projected = dot(normed_one_low, qkv_w)
-    by_head = lambda a: a.reshape(tokens, heads, HEAD_DIM)
-    feats, feat_back = jax.vjp(feature_map, projected[:, : 2 * half_d])
-    feats = feats.astype(LOW)
-    query_feat, key_feat = by_head(feats[:, :half_d]), by_head(feats[:, half_d:])
-    values = by_head(projected[:, 2 * half_d :].astype(LOW))
-
-    state = mul("the,thf->hef", key_feat, values)
-    keysum = jnp.sum(key_feat.astype(WIDE), axis=0)
-    pack = lambda s, k: jnp.concatenate([s.reshape(-1, LANES), k.reshape(-1, LANES)])
-    unpack = lambda a: (
-        a[: heads * HEAD_DIM // 2].reshape(heads, HEAD_DIM, HEAD_DIM),
-        a[heads * HEAD_DIM // 2 :].reshape(heads, HEAD_DIM),
+        norm_w = jnp.pad(whole(norm_low, 1).T, ((0, 0), (0, LANES - 4)))
+
+    inputs, grad_out = join_rows(own_x, x_mate), join_rows(own_g, g_mate)
+    halves = lambda a: a.reshape(2, group, -1)
+    rows, normed_one, qk, query, key, value, state = project(inputs, norm_w, qkv_w)
+    mixed, mixed_low, denom, state_in = attend(query, key, value, from_others(state, 1))
+    out_part = dot(mixed_low, out_w)
+    out_got = swap(out_part.astype(LOW), "c")
+    resid, normed_two, activated, slope = feed(inputs, out_part, out_got, rows, up_w)
+    down_grad = dot_rows(activated, grad_out).astype(LOW)
+    grad_hidden, two_part, two_low = feed_back(grad_out, down_w, slope, up_w)
+    two_got = swap(two_low, "c")
+    grad_resid, grad_resid_low, a_low, b_rows, state_grad, norm_two = attend_turn(
+        two_part, two_got, resid, rows, grad_out, out_w, mixed, denom, query
     )
-    state_in, keysum_in = unpack(from_others(pack(state, keysum), 1))
-    state_in_low, keysum_in_low = state_in.astype(LOW), keysum_in.astype(LOW)
-    causal = jnp.tril(jnp.ones((tokens, tokens), WIDE))
-    scores = mul("the,she->hts", query_feat, key_feat) * causal
-    scores_low = scores.astype(LOW)
-    numer = mul("hts,shf->thf", scores_low, values) + mul("the,hef->thf", query_feat, state_in_low)
-    denom = jnp.sum(scores, axis=-1).T + mul("the,he->th", query_feat, keysum_in_low)
-    mixed = (numer / denom[..., None]).reshape(tokens, half_d)
-    mixed_low = mixed.astype(LOW)
-
-    out_part = dot(mixed_low, out_w)
-    resid = inputs + out_part + swap(out_part.astype(LOW), "c").astype(WIDE)
-    normed_two, norm_two_back = jax.vjp(layer_norm, resid, norm_vals[2], norm_vals[3])
-    normed_two_low = normed_two.astype(LOW)
-    hidden = dot(normed_two_low, up_w)
-    activated, gelu_back = jax.vjp(gelu_tanh, hidden)
-    activated_low = activated.astype(LOW)
-    down_grad = dot_rows(activated_low, grad_out).astype(LOW)
-
-    halves = lambda a: a.reshape(2, group, -1)
-    down_part = dot(activated_low, down_w)
-    got = swap(other(halves(down_part)).astype(LOW), "c").astype(WIDE)
-    activations = (mine(halves(resid + down_part)) + got).astype(LOW)
-
-    grad_hidden = gelu_back(dot_cols(grad_out, down_w))[0].astype(LOW)
-    up_grad = dot_rows(normed_two_low, grad_hidden).astype(LOW)
-    grad_two = dot_cols(grad_hidden, up_w)
-    grad_two = grad_two + swap(grad_two.astype(LOW), "c").astype(WIDE)
-    grad_resid_norm, gain_two_grad, bias_two_grad = norm_two_back(grad_two)
-    grad_resid = grad_out.astype(WIDE) + grad_resid_norm
-    grad_resid_low = grad_resid.astype(LOW)
+    later = from_others(state_grad, -1)
+    up_grad = dot_rows(normed_two, grad_hidden).astype(LOW)
     out_grad = dot_rows(mixed_low, grad_resid_low).astype(LOW)
-
-    grad_mixed = by_head(dot_cols(grad_resid_low, out_w))
-    a_rows = grad_mixed / denom[..., None]
-    b_rows = -jnp.sum(a_rows * by_head(mixed), axis=-1)
-    a_low = a_rows.astype(LOW)
-    state_grad = mul("the,thf->hef", query_feat, a_low)
-    keysum_grad = jnp.sum(query_feat.astype(WIDE) * b_rows[..., None], axis=0)
-    later_state, later_sum = unpack(from_others(pack(state_grad, keysum_grad), -1))
-    later_state_low = later_state.astype(LOW)
-    pulls = (mul("thf,shf->hts", a_low, values) + b_rows.T[:, :, None]) * causal
-    pulls_low = pulls.astype(LOW)
-    grad_query = mul("hts,she->the", pulls_low, key_feat)
-    grad_query = grad_query + mul("thf,hef->the", a_low, state_in_low)
-    grad_query = grad_query + b_rows[..., None] * keysum_in
-    grad_key = mul("hts,the->she", pulls_low, query_feat)
-    grad_key = grad_key + mul("shf,hef->she", values, later_state_low) + later_sum
-    grad_value = mul("hts,thf->shf", scores_low, a_low) + mul("she,hef->shf", key_feat, later_state_low)
-    flat = lambda a: a.reshape(tokens, half_d)
-    grad_feats = feat_back(jnp.concatenate([flat(grad_query), flat(grad_key)], axis=1))[0]
-    grad_projected = jnp.concatenate([grad_feats, flat(grad_value)], axis=1).astype(LOW)
-    qkv_grad = dot_rows(normed_one_low, grad_projected).astype(LOW)
-    grad_one = dot_cols(grad_projected, qkv_w)
-    grad_one = grad_one + swap(grad_one.astype(LOW), "c").astype(WIDE)
-    grad_in_norm, gain_one_grad, bias_one_grad = norm_one_back(grad_one)
-    input_grad = mine(halves(grad_resid + grad_in_norm)).astype(LOW)
-    norm_grad = jnp.stack([gain_one_grad, bias_one_grad, gain_two_grad, bias_two_grad])
+    grad_projected = attend_back(query, key, value, qk, a_low, b_rows, state_in, later)
+    qkv_grad = dot_rows(normed_one, grad_projected).astype(LOW)
+    one_part, one_low, norm_cols = project_back(grad_projected, qkv_w, inputs, norm_two)
+    input_grad = input_back(one_part, swap(other(halves(one_low)), "c"), grad_resid, own_x, rows)
+    down_part = dot(activated, down_w)
+    down_got = swap(other(halves(down_part)).astype(LOW), "c").astype(WIDE)
+    activations = (mine(halves(resid + down_part)) + down_got).astype(LOW)
 
     if ring:
-        norm_cols = jnp.concatenate([norm_grad.T.astype(LOW), jnp.zeros((width, LANES - 4), LOW)], axis=1)
         thin, small = own_units // 2, own_rows // 2
 
         def down_cuts(zz, plane, half):
@@ -487,7 +727,8 @@
         out_halves = up_red[:, half_ff:].reshape(2, 2, small, half_d)
         out_red = jnp.concatenate([out_halves[:, 0], out_halves[:, 1]], axis=2).reshape(own_rows, width)
         by_rows = lambda a: a.reshape(2, own_rows, -1)
-        norm_red = mine(by_rows(qkv_red[:, half_qkv : half_qkv + 4])).T
+        norm_parts = by_rows(qkv_red[:, half_qkv:])
+        norm_red = (mine(norm_parts) + swap(other(norm_parts), "c"))[:, :4].T
 
         def joined(part, blocks):
             part = by_rows(part)
@@ -506,7 +747,7 @@
         up_red = scatter(both(to_all(up_grad).reshape(width, depth, ff_block), 2).reshape(width, -1))
         out_red = scatter(both(to_all(out_grad).reshape(depth, block, width), 1).reshape(width, width))
         down_red = scatter(both(to_all(down_grad).reshape(depth, ff_block, width), 1).reshape(hidden_units, width))
-        norm_red = scatter(jnp.where(core == 0, norm_grad, 0.0).T).T
+        norm_red = scatter(norm_cols.astype(WIDE))[:, :4].T
 
     reduced = (qkv_red, out_red, up_red, down_red, norm_red)
     local_squares = sum(jnp.sum(grad * grad) for grad in reduced)

time: 443 us -> 439 us (level)
  waiting for transfers between devices: 170 us -> 228 us
  matrix products: 55.5 us -> 13.7 us
  Pallas kernels: 12 us -> 51.3 us
  local copies, waits for them, and re-layouts: 48.4 us -> 22.7 us
  other arithmetic: 56.9 us -> 33.1 us
  starting transfers between devices: 88.5 us -> 75.3 us
    ppermute x27, waiting for transfers between devices: 88.2 us -> 141 us  [shift(): return lax.ppermute(value, 'z', pairs)]
    pallas_call x0 -> x8, Pallas kernels: none -> 39.5 us  [run(): pl.pallas_call(kernel, out_shape=out_shape, in_specs=([pl.BlockSpec(memor...]
    dot_general x17 -> x0, matrix products: 32.8 us -> none  [the longest x13 22.5 us: mul(): return jnp.einsum(spec, left, right, preferred_element_type=WIDE)]
    unnamed x184 -> x158, local copies, waits for them, and re-layouts: 25.8 us -> 12 us
    reduce_sum x10 -> x0, other arithmetic: 10.4 us -> none  [the longest x3 4.2 us: layer_norm(): center = values - jnp.mean(values, axis=-1, keepdims=True)]
    ppermute x27, starting transfers between devices: 54.6 us -> 45.3 us  [shift(): return lax.ppermute(value, 'z', pairs)]
    ppermute x37 -> x38, waiting for transfers between devices: 81.8 us -> 87.4 us  [swap(): return lax.ppermute(value, axis, SWAP)]
    ppermute x37 -> x38, starting transfers between devices: 32.4 us -> 27.6 us  [swap(): return lax.ppermute(value, axis, SWAP)]
  transfers between devices with their start and end apart: 65 -> 66, of which waited for: 31 -> 32; matrix products, arithmetic and copies ran while one was open for 24% -> 11% of each run, Pallas kernels for 2% -> 10%
where the time goes in v4:
time: 439 us; the launch traced here: 432 us
  waiting for transfers between devices  228 us (52%)
  starting transfers between devices  75.3 us (17%)
  Pallas kernels  51.3 us (12%)
  other arithmetic  33.1 us (8%)
  local copies, waits for them, and re-layouts  22.7 us (5%)
  matrix products  13.7 us (3%)
  between operations  7.56 us (2%)
    ppermute x27, waiting for transfers between devices, shift(): return lax.ppermute(value, 'z', pairs)  141 us
    ppermute x38, waiting for transfers between devices, swap(): return lax.ppermute(value, axis, SWAP)  87.4 us
    ppermute x27, starting transfers between devices, shift(): return lax.ppermute(value, 'z', pairs)  45.3 us
    pallas_call x8, Pallas kernels, run(): pl.pallas_call(kernel, out_shape=out_shape, in_specs=([pl.BlockSpec(memor...  39.5 us
    ppermute x38, starting transfers between devices, swap(): return lax.ppermute(value, axis, SWAP)  27.6 us
    unnamed x158, local copies, waits for them, and re-layouts  12 us
  transfers between devices with their start and end apart: 66, of which 32 were waited for; matrix products, arithmetic and copies ran while one was open for 11% of the time, Pallas kernels for 10%

profile of v4, /device:TPU:0, one launch (start us, length us, event | category | flops | bytes accessed | tf_op | source)
XLA Modules:
  0.0 431.8 jit_solution(6596249427896595437)
XLA Ops:
  5.2 5.0 %collective-permute-start.4 = (bf16[64,1664]{1,0:T(8,128)(2,1)S(1)}, bf16[64,1664]{1,0:T(8,128)(2,1)S(1)}, u32[]{:S(2)}, u32[]{:S(2)}) collective-permute-start(bf16[64,1664]{1,0:T(8,128)(2,1)S(1)} %shard_map.306), channel_id=1, source_target_pairs={{0,24},{8,0},{16,8},{24,16},{1,25},{9,1},{17,9},{25,17},{2,26},{10... | collective-permute-start | bytes 638984 | tf_op jit(solution)/shard_map/ppermute | solution.py:33
  11.2 4.7 %collective-permute-done.4 = bf16[64,1664]{1,0:T(8,128)(2,1)S(1)} collective-permute-done((bf16[64,1664]{1,0:T(8,128)(2,1)S(1)}, bf16[64,1664]{1,0:T(8,128)(2,1)S(1)}, u32[]{:S(2)}, u32[]{:S(2)}) %collective-permute-start.4) | collective-permute-done | bytes 213024 | tf_op jit(solution)/shard_map/ppermute | solution.py:33
  15.9 12.7 %collective-permute-done.3 = bf16[64,1664]{1,0:T(8,128)(2,1)S(1)} collective-permute-done((bf16[64,1664]{1,0:T(8,128)(2,1)S(1)}, bf16[64,1664]{1,0:T(8,128)(2,1)S(1)}, u32[]{:S(2)}, u32[]{:S(2)}) %collective-permute-start.3) | collective-permute-done | bytes 213024 | tf_op jit(solution)/shard_map/ppermute | solution.py:33
  33.6 21.0 %collective-permute-done.22 = bf16[128,1024]{1,0:T(8,128)(2,1)S(1)} collective-permute-done((bf16[128,1024]{1,0:T(8,128)(2,1)S(1)}, bf16[128,1024]{1,0:T(8,128)(2,1)S(1)}, u32[]{:S(2)}, u32[]{:S(2)}) %collective-permute-start.22) | collective-permute-done | bytes 262176 | tf_op jit(solution)/shard_map/ppermute | solution.py:27
  66.9 21.1 %collective-permute-done.14 = bf16[64,2560]{1,0:T(8,128)(2,1)S(1)} collective-permute-done((bf16[64,2560]{1,0:T(8,128)(2,1)S(1)}, bf16[64,2560]{1,0:T(8,128)(2,1)S(1)}, u32[]{:S(2)}, u32[]{:S(2)}) %collective-permute-start.14) | collective-permute-done | bytes 327712 | tf_op jit(solution)/shard_map/ppermute | solution.py:33
  89.3 22.7 %collective-permute-done.25.refs_1_ = bf16[512,1024]{1,0:T(8,128)(2,1)S(1)} collective-permute-done((bf16[512,1024]{1,0:T(8,128)(2,1)S(1)}, bf16[512,1024]{1,0:T(8,128)(2,1)S(1)}, u32[]{:S(2)}, u32[]{:S(2)}) %collective-permute-start.25) | collective-permute-done | bytes 1048608 | tf_op jit(solution)/shard_map/ppermute | solution.py:33
  112.1 4.9 %collective-permute-done.17.refs_2_ = bf16[4,64,2560]{2,1,0:T(8,128)(2,1)S(1)} collective-permute-done((bf16[4,64,2560]{2,1,0:T(8,128)(2,1)S(1)}, bf16[4,64,2560]{2,1,0:T(8,128)(2,1)S(1)}, u32[]{:S(2)}, u32[]{:S(2)}) %collective-permute-start.17) | collective-permute-done | bytes 1310752 | tf_op jit(solution)/shard_map/ppermute | solution.py:27
  126.7 4.9 %collective-permute-start.11 = (bf16[272,128]{1,0:T(8,128)(2,1)S(1)}, bf16[272,128]{1,0:T(8,128)(2,1)S(1)}, u32[]{:S(2)}, u32[]{:S(2)}) collective-permute-start(bf16[272,128]{1,0:T(8,128)(2,1)S(1)} %get-tuple-element.83), channel_id=1, source_target_pairs={{0,24},{1,25},{2,26},{3,27},{4,28},{5,29},{6,30},{7,31}} | collective-permute-start | bytes 208904 | tf_op jit(solution)/shard_map/ppermute | solution.py:33
  154.5 14.8 %collective-permute-done.27.refs_3_ = bf16[512,1024]{1,0:T(8,128)(2,1)} collective-permute-done((bf16[512,1024]{1,0:T(8,128)(2,1)}, bf16[512,1024]{1,0:T(8,128)(2,1)}, u32[]{:S(2)}, u32[]{:S(2)}) %collective-permute-start.27) | collective-permute-done | bytes 1048608 | tf_op jit(solution)/shard_map/ppermute | solution.py:33
  171.2 7.7 %shard_map.313 = (f32[512,1024]{1,0:T(8,128)S(1)}, bf16[512,1024]{1,0:T(8,128)(2,1)S(1)}, bf16[512,2048]{1,0:T(8,128)(2,1)S(1)}, f32[512,2048]{1,0:T(8,128)S(1)}) custom-call(bf16[512,1024]{1,0:T(8,128)(2,1)S(1)} %copy-done.2, f32[512,1024]{1,0:T(8,128)S(1)} %get-tuple-element.259.part_ref, bf16[512,1024]{1,0:T(8,128)(2,1)} %collective-permute-done.20.got_ref, ...), custom_call_target="tpu_custom_call" | custom-call | flops 2147483648 | bytes 16842752 | tf_op jit(solution)/shard_map/pallas_call | solution.py:251
  185.4 8.2 %shard_map.316 = (bf16[512,2048]{1,0:T(8,128)(2,1)S(1)}, f32[512,1024]{1,0:T(8,128)S(1)}, bf16[512,1024]{1,0:T(8,128)(2,1)S(1)}) custom-call(bf16[512,1024]{1,0:T(8,128)(2,1)S(1)} %shard_map.315.g_ref, bf16[2048,1024]{1,0:T(8,128)(2,1)S(1)} %shard_map.314.down_ref, f32[512,2048]{1,0:T(8,128)} %copy-done.39, bf16[1024,2048]{1,0:T(8,128)(2,1)} %copy-done), custom_call_target="tpu_custom_call" | custom-call | flops 4294967296 | bytes 27262976 | tf_op jit(solution)/shard_map/pallas_call | solution.py:251
  193.7 4.0 fusion.50
  197.7 6.7 %collective-permute-done.37 = bf16[2,4,64,1024]{3,2,1,0:T(8,128)(2,1)} collective-permute-done((bf16[2,4,64,1024]{3,2,1,0:T(8,128)(2,1)S(1)}, bf16[2,4,64,1024]{3,2,1,0:T(8,128)(2,1)}, u32[]{:S(2)}, u32[]{:S(2)}) %collective-permute-start.37) | collective-permute-done | bytes 1048608 | tf_op jit(solution)/shard_map/ppermute | solution.py:27
  211.3 4.2 shard_map.317
  225.0 8.3 %shard_map.318.grad_ref = bf16[512,1536]{1,0:T(8,128)(2,1)S(1)} custom-call(bf16[512,512]{1,0:T(8,128)(2,1)S(1)} %copy-done.33, bf16[512,512]{1,0:T(8,128)(2,1)S(1)} %copy-done.49, bf16[512,512]{1,0:T(8,128)(2,1)S(1)} %copy-done.51, f32[512,1024]{1,0:T(8,128)S(1)} %copy-done.43, bf16[512,512]{1,0:T(8,128)(2,1)S(1)} %get-tuple-element.105.a_ref, ...), custom_call_target="tpu_custom_call" | custom-call | flops 2684354560 | bytes 11182080 | tf_op jit(solution)/shard_map/pallas_call | solution.py:251
  249.1 17.9 %collective-permute-done.39 = bf16[2,4,32,2560]{3,2,1,0:T(8,128)(2,1)S(1)} collective-permute-done((bf16[2,4,32,2560]{3,2,1,0:T(8,128)(2,1)S(1)}, bf16[2,4,32,2560]{3,2,1,0:T(8,128)(2,1)S(1)}, u32[]{:S(2)}, u32[]{:S(2)}) %collective-permute-start.39) | collective-permute-done | bytes 1310752 | tf_op jit(solution)/shard_map/ppermute | solution.py:27
  268.7 10.6 %collective-permute-done.42 = bf16[4,32,2560]{2,1,0:T(8,128)(2,1)S(1)} collective-permute-done((bf16[4,32,2560]{2,1,0:T(8,128)(2,1)S(1)}, bf16[4,32,2560]{2,1,0:T(8,128)(2,1)S(1)}, u32[]{:S(2)}, u32[]{:S(2)}) %collective-permute-start.42) | collective-permute-done | bytes 655392 | tf_op jit(solution)/shard_map/ppermute | solution.py:27
  281.0 5.4 %collective-permute-start.52 = (bf16[64,2560]{1,0:T(8,128)(2,1)S(1)}, bf16[64,2560]{1,0:T(8,128)(2,1)S(1)}, u32[]{:S(2)}, u32[]{:S(2)}) collective-permute-start(bf16[64,2560]{1,0:T(8,128)(2,1)S(1)} %pad_maximum_fusion.3), channel_id=1, source_target_pairs={{0,16},{8,24},{16,0},{24,8},{1,17},{9,25},{17,1},{25,9},{2,18},{10... | collective-permute-start | bytes 983048 | tf_op jit(solution)/shard_map/ppermute | solution.py:33
  290.7 29.1 %collective-permute-done.52 = bf16[64,2560]{1,0:T(8,128)(2,1)S(1)} collective-permute-done((bf16[64,2560]{1,0:T(8,128)(2,1)S(1)}, bf16[64,2560]{1,0:T(8,128)(2,1)S(1)}, u32[]{:S(2)}, u32[]{:S(2)}) %collective-permute-start.52) | collective-permute-done | bytes 327712 | tf_op jit(solution)/shard_map/ppermute | solution.py:33
  320.6 11.8 %collective-permute-done.56 = bf16[128,1024]{1,0:T(8,128)(2,1)S(1)} collective-permute-done((bf16[128,1024]{1,0:T(8,128)(2,1)S(1)}, bf16[128,1024]{1,0:T(8,128)(2,1)S(1)}, u32[]{:S(2)}, u32[]{:S(2)}) %collective-permute-start.56) | collective-permute-done | bytes 262176 | tf_op jit(solution)/shard_map/ppermute | solution.py:33
  347.4 12.0 %collective-permute-done.45 = bf16[2,4,32,1664]{3,2,1,0:T(8,128)(2,1)} collective-permute-done((bf16[2,4,32,1664]{3,2,1,0:T(8,128)(2,1)}, bf16[2,4,32,1664]{3,2,1,0:T(8,128)(2,1)}, u32[]{:S(2)}, u32[]{:S(2)}) %collective-permute-start.45) | collective-permute-done | bytes 852000 | tf_op jit(solution)/shard_map/ppermute | solution.py:27
  360.5 5.9 %collective-permute-done.44 = bf16[4,32,1664]{2,1,0:T(8,128)(2,1)S(1)} collective-permute-done((bf16[4,32,1664]{2,1,0:T(8,128)(2,1)S(1)}, bf16[4,32,1664]{2,1,0:T(8,128)(2,1)S(1)}, u32[]{:S(2)}, u32[]{:S(2)}) %collective-permute-start.44) | collective-permute-done | bytes 426016 | tf_op jit(solution)/shard_map/ppermute | solution.py:27
  370.4 5.8 %collective-permute-start.49 = (bf16[64,1664]{1,0:T(8,128)(2,1)S(1)}, bf16[64,1664]{1,0:T(8,128)(2,1)S(1)}, u32[]{:S(2)}, u32[]{:S(2)}) collective-permute-start(bf16[64,1664]{1,0:T(8,128)(2,1)S(1)} %pad_maximum_fusion.10), channel_id=1, source_target_pairs={{0,24},{8,0},{16,8},{24,16},{1,25},{9,1},{17,9},{25,17},{2,26},{10... | collective-permute-start | bytes 638984 | tf_op jit(solution)/shard_map/ppermute | solution.py:33
  377.7 7.9 %collective-permute-done.48 = bf16[64,1664]{1,0:T(8,128)(2,1)S(1)} collective-permute-done((bf16[64,1664]{1,0:T(8,128)(2,1)S(1)}, bf16[64,1664]{1,0:T(8,128)(2,1)S(1)}, u32[]{:S(2)}, u32[]{:S(2)}) %collective-permute-start.48) | collective-permute-done | bytes 213024 | tf_op jit(solution)/shard_map/ppermute | solution.py:33
  (368 shorter events, 166.9 us)
Async XLA Ops:
  28.8 33.7 %collective-permute-start.6 = (bf16[4,64,1664]{2,1,0:T(8,128)(2,1)S(1)}, bf16[4,64,1664]{2,1,0:T(8,128)(2,1)S(1)}, u32[]{:S(2)}, u32[]{:S(2)}) collective-permute-start(bf16[4,64,1664]{2,1,0:T(8,128)(2,1)S(1)} %pad_maximum_fusion.1.refs_0_), channel_id=1, source_target_pairs={{0,2},{2,0},{1,3},{3,1},{4,6},{6,4},{5,7},{7,5},{8,10},{10,8},{9,1... | collective-permute-start | bytes 2555912 | tf_op jit(solution)/shard_map/ppermute | solution.py:27
  30.4 33.0 %collective-permute-start.5 = (bf16[4,64,1664]{2,1,0:T(8,128)(2,1)S(1)}, bf16[4,64,1664]{2,1,0:T(8,128)(2,1)S(1)}, u32[]{:S(2)}, u32[]{:S(2)}) collective-permute-start(bf16[4,64,1664]{2,1,0:T(8,128)(2,1)S(1)} %pad_maximum_fusion.1.refs_0_), channel_id=1, source_target_pairs={{0,1},{1,0},{2,3},{3,2},{4,5},{5,4},{6,7},{7,6},{8,9},{9,8},{10,11... | collective-permute-start | bytes 2555912 | tf_op jit(solution)/shard_map/ppermute | solution.py:27
  33.1 23.8 %collective-permute-start.21 = (bf16[128,1024]{1,0:T(8,128)(2,1)S(1)}, bf16[128,1024]{1,0:T(8,128)(2,1)S(1)}, u32[]{:S(2)}, u32[]{:S(2)}) collective-permute-start(bf16[128,1024]{1,0:T(8,128)(2,1)S(1)} %get-tuple-element.96), channel_id=1, source_target_pairs={{0,1},{1,0},{2,3},{3,2},{4,5},{5,4},{6,7},{7,6},{8,9},{9,8},{10,11... | collective-permute-start | bytes 786440 | tf_op jit(solution)/shard_map/ppermute | solution.py:27
  33.6 22.6 %collective-permute-start.12 = (bf16[32,2048]{1,0:T(8,128)(2,1)S(1)}, bf16[32,2048]{1,0:T(8,128)(2,1)S(1)}, u32[]{:S(2)}, u32[]{:S(2)}) collective-permute-start(bf16[32,2048]{1,0:T(8,128)(2,1)S(1)} %get-tuple-element.87), channel_id=1, source_target_pairs={{0,4},{4,0},{1,5},{5,1},{2,6},{6,2},{3,7},{7,3},{8,12},{12,8},{9,1... | collective-permute-start | bytes 393224 | tf_op jit(solution)/shard_map/ppermute | solution.py:27
  59.7 28.3 %collective-permute-start.14 = (bf16[64,2560]{1,0:T(8,128)(2,1)S(1)}, bf16[64,2560]{1,0:T(8,128)(2,1)S(1)}, u32[]{:S(2)}, u32[]{:S(2)}) collective-permute-start(bf16[64,2560]{1,0:T(8,128)(2,1)S(1)} %shard_map.311), channel_id=1, source_target_pairs={{0,16},{8,24},{16,0},{24,8},{1,17},{9,25},{17,1},{25,9},{2,18},{10... | collective-permute-start | bytes 983048 | tf_op jit(solution)/shard_map/ppermute | solution.py:33
  62.4 25.6 %collective-permute-start.13 = (bf16[64,2560]{1,0:T(8,128)(2,1)S(1)}, bf16[64,2560]{1,0:T(8,128)(2,1)S(1)}, u32[]{:S(2)}, u32[]{:S(2)}) collective-permute-start(bf16[64,2560]{1,0:T(8,128)(2,1)S(1)} %shard_map.311), channel_id=1, source_target_pairs={{0,8},{8,16},{16,24},{24,0},{1,9},{9,17},{17,25},{25,1},{2,10},{10... | collective-permute-start | bytes 983048 | tf_op jit(solution)/shard_map/ppermute | solution.py:33
  63.4 24.8 %collective-permute-start.7 = (bf16[2,64,1664]{2,1,0:T(8,128)(2,1)S(1)}, bf16[2,64,1664]{2,1,0:T(8,128)(2,1)S(1)}, u32[]{:S(2)}, u32[]{:S(2)}) collective-permute-start(bf16[2,64,1664]{2,1,0:T(8,128)(2,1)S(1)} %slice.455), channel_id=1, source_target_pairs={{0,1},{1,0},{2,3},{3,2},{4,5},{5,4},{6,7},{7,6},{8,9},{9,8},{10,11... | collective-permute-start | bytes 1277960 | tf_op jit(solution)/shard_map/ppermute | solution.py:27
  64.2 24.0 %collective-permute-start.8 = (bf16[2,64,1664]{2,1,0:T(8,128)(2,1)S(1)}, bf16[2,64,1664]{2,1,0:T(8,128)(2,1)S(1)}, u32[]{:S(2)}, u32[]{:S(2)}) collective-permute-start(bf16[2,64,1664]{2,1,0:T(8,128)(2,1)S(1)} %slice.456), channel_id=1, source_target_pairs={{0,2},{2,0},{1,3},{3,1},{4,6},{6,4},{5,7},{7,5},{8,10},{10,8},{9,1... | collective-permute-start | bytes 1277960 | tf_op jit(solution)/shard_map/ppermute | solution.py:27
  88.0 24.0 %collective-permute-start.25 = (bf16[512,1024]{1,0:T(8,128)(2,1)S(1)}, bf16[512,1024]{1,0:T(8,128)(2,1)S(1)}, u32[]{:S(2)}, u32[]{:S(2)}) collective-permute-start(bf16[512,1024]{1,0:T(8,128)(2,1)S(1)} %constant_dynamic-update-slice_fusion.refs_0_), channel_id=1, source_target_pairs={{0,8},{8,16},{16,24},{24,0},{1,9},{9,17},{17,25},{25,1},{2,10},{10... | collective-permute-start | bytes 3145736 | tf_op jit(solution)/shard_map/ppermute | solution.py:33
  88.2 28.8 %collective-permute-start.17 = (bf16[4,64,2560]{2,1,0:T(8,128)(2,1)S(1)}, bf16[4,64,2560]{2,1,0:T(8,128)(2,1)S(1)}, u32[]{:S(2)}, u32[]{:S(2)}) collective-permute-start(bf16[4,64,2560]{2,1,0:T(8,128)(2,1)S(1)} %pad_maximum_fusion.refs_0_), channel_id=1, source_target_pairs={{0,2},{2,0},{1,3},{3,1},{4,6},{6,4},{5,7},{7,5},{8,10},{10,8},{9,1... | collective-permute-start | bytes 3932168 | tf_op jit(solution)/shard_map/ppermute | solution.py:27
  88.8 28.9 %collective-permute-start.16 = (bf16[4,64,2560]{2,1,0:T(8,128)(2,1)S(1)}, bf16[4,64,2560]{2,1,0:T(8,128)(2,1)S(1)}, u32[]{:S(2)}, u32[]{:S(2)}) collective-permute-start(bf16[4,64,2560]{2,1,0:T(8,128)(2,1)S(1)} %pad_maximum_fusion.refs_0_), channel_id=1, source_target_pairs={{0,1},{1,0},{2,3},{3,2},{4,5},{5,4},{6,7},{7,6},{8,9},{9,8},{10,11... | collective-permute-start | bytes 3932168 | tf_op jit(solution)/shard_map/ppermute | solution.py:27
  112.0 31.2 %collective-permute-start.26 = (bf16[512,1024]{1,0:T(8,128)(2,1)S(1)}, bf16[512,1024]{1,0:T(8,128)(2,1)}, u32[]{:S(2)}, u32[]{:S(2)}) collective-permute-start(bf16[512,1024]{1,0:T(8,128)(2,1)S(1)} %collective-permute-done.25.refs_1_), channel_id=1, source_target_pairs={{0,8},{8,16},{16,24},{24,0},{1,9},{9,17},{17,25},{25,1},{2,10},{10... | collective-permute-start | bytes 3145736 | tf_op jit(solution)/shard_map/ppermute | solution.py:33
  117.1 29.0 %collective-permute-start.18 = (bf16[2,64,2560]{2,1,0:T(8,128)(2,1)S(1)}, bf16[2,64,2560]{2,1,0:T(8,128)(2,1)S(1)}, u32[]{:S(2)}, u32[]{:S(2)}) collective-permute-start(bf16[2,64,2560]{2,1,0:T(8,128)(2,1)S(1)} %slice.457), channel_id=1, source_target_pairs={{0,1},{1,0},{2,3},{3,2},{4,5},{5,4},{6,7},{7,6},{8,9},{9,8},{10,11... | collective-permute-start | bytes 1966088 | tf_op jit(solution)/shard_map/ppermute | solution.py:27
  117.7 28.4 %collective-permute-start.19 = (bf16[2,64,2560]{2,1,0:T(8,128)(2,1)S(1)}, bf16[2,64,2560]{2,1,0:T(8,128)(2,1)S(1)}, u32[]{:S(2)}, u32[]{:S(2)}) collective-permute-start(bf16[2,64,2560]{2,1,0:T(8,128)(2,1)S(1)} %slice.458), channel_id=1, source_target_pairs={{0,2},{2,0},{1,3},{3,1},{4,6},{6,4},{5,7},{7,5},{8,10},{10,8},{9,1... | collective-permute-start | bytes 1966088 | tf_op jit(solution)/shard_map/ppermute | solution.py:27
  143.2 26.1 %collective-permute-start.27 = (bf16[512,1024]{1,0:T(8,128)(2,1)}, bf16[512,1024]{1,0:T(8,128)(2,1)}, u32[]{:S(2)}, u32[]{:S(2)}) collective-permute-start(bf16[512,1024]{1,0:T(8,128)(2,1)} %collective-permute-done.26.refs_2_), channel_id=1, source_target_pairs={{0,8},{8,16},{16,24},{24,0},{1,9},{9,17},{17,25},{25,1},{2,10},{10... | collective-permute-start | bytes 3145736 | tf_op jit(solution)/shard_map/ppermute | solution.py:33
  221.3 26.0 %collective-permute-start.41 = (bf16[2,4,32,2560]{3,2,1,0:T(8,128)(2,1)S(1)}, bf16[2,4,32,2560]{3,2,1,0:T(8,128)(2,1)}, u32[]{:S(2)}, u32[]{:S(2)}) collective-permute-start(bf16[2,4,32,2560]{3,2,1,0:T(8,128)(2,1)S(1)} %get-tuple-element.129), channel_id=1, source_target_pairs={{0,1},{1,0},{2,3},{3,2},{4,5},{5,4},{6,7},{7,6},{8,9},{9,8},{10,11... | collective-permute-start | bytes 3932168 | tf_op jit(solution)/shard_map/ppermute | solution.py:27
  223.7 181.6 %collective-permute-start.28 = (bf16[256,1024]{1,0:T(8,128)(2,1)}, bf16[256,1024]{1,0:T(8,128)(2,1)}, u32[]{:S(2)}, u32[]{:S(2)}) collective-permute-start(bf16[256,1024]{1,0:T(8,128)(2,1)} %fusion), channel_id=1, source_target_pairs={{0,4},{4,0},{1,5},{5,1},{2,6},{6,2},{3,7},{7,3},{8,12},{12,8},{9,1... | collective-permute-start | bytes 1572872 | tf_op jit(solution)/shard_map/ppermute | solution.py:27
  235.2 31.8 %collective-permute-start.39 = (bf16[2,4,32,2560]{3,2,1,0:T(8,128)(2,1)S(1)}, bf16[2,4,32,2560]{3,2,1,0:T(8,128)(2,1)S(1)}, u32[]{:S(2)}, u32[]{:S(2)}) collective-permute-start(bf16[2,4,32,2560]{3,2,1,0:T(8,128)(2,1)S(1)} %get-tuple-element.126), channel_id=1, source_target_pairs={{0,2},{2,0},{1,3},{3,1},{4,6},{6,4},{5,7},{7,5},{8,10},{10,8},{9,1... | collective-permute-start | bytes 3932168 | tf_op jit(solution)/shard_map/ppermute | solution.py:27
  248.5 30.8 %collective-permute-start.42 = (bf16[4,32,2560]{2,1,0:T(8,128)(2,1)S(1)}, bf16[4,32,2560]{2,1,0:T(8,128)(2,1)S(1)}, u32[]{:S(2)}, u32[]{:S(2)}) collective-permute-start(bf16[4,32,2560]{2,1,0:T(8,128)(2,1)S(1)} %fusion.4), channel_id=1, source_target_pairs={{0,2},{2,0},{1,3},{3,1},{4,6},{6,4},{5,7},{7,5},{8,10},{10,8},{9,1... | collective-permute-start | bytes 1966088 | tf_op jit(solution)/shard_map/ppermute | solution.py:27
  281.0 38.8 %collective-permute-start.52 = (bf16[64,2560]{1,0:T(8,128)(2,1)S(1)}, bf16[64,2560]{1,0:T(8,128)(2,1)S(1)}, u32[]{:S(2)}, u32[]{:S(2)}) collective-permute-start(bf16[64,2560]{1,0:T(8,128)(2,1)S(1)} %pad_maximum_fusion.3), channel_id=1, source_target_pairs={{0,16},{8,24},{16,0},{24,8},{1,17},{9,25},{17,1},{25,9},{2,18},{10... | collective-permute-start | bytes 983048 | tf_op jit(solution)/shard_map/ppermute | solution.py:33
  286.4 33.4 %collective-permute-start.53 = (bf16[64,2560]{1,0:T(8,128)(2,1)S(1)}, bf16[64,2560]{1,0:T(8,128)(2,1)S(1)}, u32[]{:S(2)}, u32[]{:S(2)}) collective-permute-start(bf16[64,2560]{1,0:T(8,128)(2,1)S(1)} %pad_maximum_fusion.4), channel_id=1, source_target_pairs={{0,24},{8,0},{16,8},{24,16},{1,25},{9,1},{17,9},{25,17},{2,26},{10... | collective-permute-start | bytes 983048 | tf_op jit(solution)/shard_map/ppermute | solution.py:33
  287.9 31.8 %collective-permute-start.51 = (bf16[64,2560]{1,0:T(8,128)(2,1)S(1)}, bf16[64,2560]{1,0:T(8,128)(2,1)S(1)}, u32[]{:S(2)}, u32[]{:S(2)}) collective-permute-start(bf16[64,2560]{1,0:T(8,128)(2,1)S(1)} %pad_maximum_fusion.2), channel_id=1, source_target_pairs={{0,8},{8,16},{16,24},{24,0},{1,9},{9,17},{17,25},{25,1},{2,10},{10... | collective-permute-start | bytes 983048 | tf_op jit(solution)/shard_map/ppermute | solution.py:33
  288.6 32.0 %collective-permute-start.55 = (bf16[128,1024]{1,0:T(8,128)(2,1)S(1)}, bf16[128,1024]{1,0:T(8,128)(2,1)S(1)}, u32[]{:S(2)}, u32[]{:S(2)}) collective-permute-start(bf16[128,1024]{1,0:T(8,128)(2,1)S(1)} %pad_maximum_fusion.5), channel_id=1, source_target_pairs={{0,8},{8,16},{16,24},{24,0},{1,9},{9,17},{17,25},{25,1},{2,10},{10... | collective-permute-start | bytes 786440 | tf_op jit(solution)/shard_map/ppermute | solution.py:33
  319.8 25.7 %collective-permute-start.43 = (bf16[2,4,32,1664]{3,2,1,0:T(8,128)(2,1)}, bf16[2,4,32,1664]{3,2,1,0:T(8,128)(2,1)}, u32[]{:S(2)}, u32[]{:S(2)}) collective-permute-start(bf16[2,4,32,1664]{3,2,1,0:T(8,128)(2,1)} %get-tuple-element.130), channel_id=1, source_target_pairs={{0,1},{1,0},{2,3},{3,2},{4,5},{5,4},{6,7},{7,6},{8,9},{9,8},{10,11... | collective-permute-start | bytes 2555912 | tf_op jit(solution)/shard_map/ppermute | solution.py:27
  (116 other events, 1105.6 us)
